TPU v7x, 32 devices: a whole 2x2x4 slice. The times are simulated.
32 devices in a mesh: rows: 8 (over z, y), seq: 4 (over x, core).
Axes of the slice: x: 2, y: 2, z: 4, core: 2. Of those that a mesh axis runs over, the one named last changes fastest.
Arguments:
- molecules: bfloat16 [64, 512, 768], P('rows', 'seq'), may hold values from -6 to 6
- ln1_gain: float32 [768], replicated, may hold values from 0.5 to 1.5
- ln1_bias: float32 [768], replicated, may hold values from -3 to 3
- w_qkv: bfloat16 [768, 2304], replicated, may hold values from -0.21875 to 0.21875
- qkv_bias: float32 [2, 768], replicated, may hold values from -3 to 3
- w_out: bfloat16 [768, 768], replicated, may hold values from -3 to 3
- out_bias: float32 [768], replicated, may hold values from -3 to 3
- ln2_gain: float32 [768], replicated, may hold values from 0.5 to 1.5
- ln2_bias: float32 [768], replicated, may hold values from -3 to 3
- w_up: bfloat16 [768, 3072], replicated, may hold values from -0.21875 to 0.21875
- up_bias: float32 [3072], replicated, may hold values from -3 to 3
- w_down: bfloat16 [3072, 768], replicated, may hold values from -0.109375 to 0.109375
- down_bias: float32 [768], replicated, may hold values from -3 to 3
- out_cotangent: bfloat16 [64, 512, 768], P('rows', 'seq'), may hold values from -6 to 6
- bucket_ids: int32 [8, 64, 2048], P(None, 'rows', 'seq'), may hold values from 0 to 16383
Outputs:
- layer_out: bfloat16 [64, 512, 768], P('rows', 'seq')
- grad_molecules: float32 [64, 512, 768], P('rows', 'seq')
- grad_ln1_gain: float32 [768], replicated
- grad_ln1_bias: float32 [768], replicated
- grad_w_qkv: float32 [768, 2304], replicated
- grad_qkv_bias: float32 [2, 768], replicated
- grad_w_out: float32 [768, 768], replicated
- grad_out_bias: float32 [768], replicated
- grad_ln2_gain: float32 [768], replicated
- grad_ln2_bias: float32 [768], replicated
- grad_w_up: float32 [768, 3072], replicated
- grad_up_bias: float32 [3072], replicated
- grad_w_down: float32 [3072, 768], replicated
- grad_down_bias: float32 [768], replicated
- bucket_counts: int32 [8, 16384], replicated
All inputs are finite; a program needn't handle non-finite values.
Results may differ from a plain program's by a relative error of at most 0.0085.
The roundings to bfloat16 on the way count: a program that leaves them out, or rounds other values in their place, can miss the bound.
Values may be sent and summed in bfloat16 or wider, within the bound.
A program may use at most 256 MiB of HBM per device.

v0:
```python
import jax
import jax.numpy as jnp
from jax import lax
from jax.sharding import PartitionSpec as P

HEAD_DIM = 64
BUCKETS = 16384


norm_eps = 1e-05


def layer_norm(value, gain, shift):
    center = value - jnp.mean(value, -1, keepdims=True)
    spread = jnp.mean(center * center, -1, keepdims=True)
    return center * lax.rsqrt(spread + norm_eps) * gain + shift


def gelu_exact(value):
    return jax.nn.gelu(value, approximate=False)


def attend(block):
    count, length, three, cols = block.shape
    local_heads = cols // HEAD_DIM
    parts = block.reshape(count, length, three, local_heads, HEAD_DIM)
    query, keys, values = (parts[:, :, 0], parts[:, :, 1], parts[:, :, 2])
    scores = jnp.einsum(
        "nqhd,nkhd->nhqk", query, keys, preferred_element_type=jnp.float32
    ) * HEAD_DIM ** (-0.5)
    peak = jnp.max(scores, -1, keepdims=True)
    expo = jnp.exp(scores - peak)
    total = jnp.sum(expo, -1, keepdims=True)
    probs = (expo / total).astype(jnp.bfloat16)
    context = jnp.einsum("nhqk,nkhd->nqhd", probs, values, preferred_element_type=jnp.float32)
    context = context.astype(jnp.bfloat16).reshape(count, length, cols)
    logsum = (peak + jnp.log(total))[..., 0]
    return (context, logsum, block)


def attend_back(triple):
    block, logsum, dcontext = triple
    length, three, cols = block.shape
    local_heads = cols // HEAD_DIM
    parts = block.reshape(length, three, local_heads, HEAD_DIM)
    query, keys, values = (parts[:, 0], parts[:, 1], parts[:, 2])
    dctx = dcontext.reshape(length, local_heads, HEAD_DIM)
    scale = HEAD_DIM ** (-0.5)
    scores = jnp.einsum("qhd,khd->hqk", query, keys, preferred_element_type=jnp.float32) * scale
    probs = jnp.exp(scores - logsum[..., None])
    dprobs = jnp.einsum("qhd,khd->hqk", dctx, values, preferred_element_type=jnp.float32)
    dvalues = jnp.einsum(
        "hqk,qhd->khd", probs.astype(jnp.bfloat16), dctx, preferred_element_type=jnp.float32
    )
    inner = jnp.sum(probs * dprobs, -1, keepdims=True)
    dscores = (probs * (dprobs - inner)).astype(jnp.bfloat16)
    dquery = jnp.einsum("hqk,khd->qhd", dscores, keys, preferred_element_type=jnp.float32) * scale
    dkeys = jnp.einsum("hqk,qhd->khd", dscores, query, preferred_element_type=jnp.float32) * scale
    stacked = jnp.stack([dquery, dkeys, dvalues], 1).astype(jnp.bfloat16)
    return stacked.reshape(length, three, cols)


def on_device(
    molecules,
    ln1_gain,
    ln1_bias,
    w_qkv,
    qkv_bias,
    w_out,
    out_bias,
    ln2_gain,
    ln2_bias,
    w_up,
    up_bias,
    w_down,
    down_bias,
    out_cotangent,
    bucket_ids,
):
    source, cot_low = (molecules, out_cotangent)
    rows_here, local_len, width = source.shape
    inputs = source.astype(jnp.float32)
    a_one = layer_norm(inputs, ln1_gain, ln1_bias).astype(jnp.bfloat16)
    joined = jnp.dot(a_one, w_qkv, preferred_element_type=jnp.float32)
    bias_row = jnp.concatenate([qkv_bias[0], jnp.zeros((width,), jnp.float32), qkv_bias[1]])
    qkv_low = (joined + bias_row).astype(jnp.bfloat16).reshape(rows_here, local_len, 3, width)
    ctx_heads, logsum, kept = attend(
        lax.all_to_all(qkv_low, "seq", split_axis=3, concat_axis=1, tiled=True)
    )
    context = lax.all_to_all(ctx_heads, "seq", split_axis=1, concat_axis=2, tiled=True)
    mid = inputs + jnp.dot(context, w_out, preferred_element_type=jnp.float32) + out_bias
    a_two = layer_norm(mid, ln2_gain, ln2_bias).astype(jnp.bfloat16)
    upper = jnp.dot(a_two, w_up, preferred_element_type=jnp.float32) + up_bias
    hidden = gelu_exact(upper).astype(jnp.bfloat16)
    result = mid + jnp.dot(hidden, w_down, preferred_element_type=jnp.float32) + down_bias
    layer_out = result.astype(jnp.bfloat16)
    dout = cot_low.astype(jnp.float32)
    grad_w_down = jnp.einsum("rlf,rld->fd", hidden, cot_low, preferred_element_type=jnp.float32)
    grad_down_bias = jnp.sum(dout, (0, 1))
    dhidden = jnp.dot(cot_low, w_down.T, preferred_element_type=jnp.float32)
    gelu_pull = jax.vjp(gelu_exact, upper)[1]
    dupper = gelu_pull(dhidden)[0].astype(jnp.bfloat16)
    grad_w_up = jnp.einsum("rld,rlf->df", a_two, dupper, preferred_element_type=jnp.float32)
    grad_up_bias = jnp.sum(dupper.astype(jnp.float32), (0, 1))
    da_two = jnp.dot(dupper, w_up.T, preferred_element_type=jnp.float32)
    norm_two_pull = jax.vjp(layer_norm, mid, ln2_gain, ln2_bias)[1]
    dmid_part, grad_ln2_gain, grad_ln2_bias = norm_two_pull(da_two)
    dmid = dout + dmid_part
    dbranch = dmid.astype(jnp.bfloat16)
    grad_w_out = jnp.einsum("rlc,rld->cd", context, dbranch, preferred_element_type=jnp.float32)
    grad_out_bias = jnp.sum(dbranch.astype(jnp.float32), (0, 1))
    dcontext = jnp.dot(dbranch, w_out.T, preferred_element_type=jnp.float32).astype(jnp.bfloat16)
    dctx_heads = lax.all_to_all(dcontext, "seq", split_axis=2, concat_axis=1, tiled=True)
    dqkv_heads = lax.map(attend_back, (kept, logsum, dctx_heads))
    dqkv = lax.all_to_all(dqkv_heads, "seq", split_axis=1, concat_axis=3, tiled=True).reshape(
        rows_here, local_len, 3 * width
    )
    grad_w_qkv = jnp.einsum("rld,rle->de", a_one, dqkv, preferred_element_type=jnp.float32)
    dqkv_sum = jnp.sum(dqkv.astype(jnp.float32), (0, 1))
    grad_qkv_bias = jnp.stack([dqkv_sum[:width], dqkv_sum[2 * width :]])
    da_one = jnp.dot(dqkv, w_qkv.T, preferred_element_type=jnp.float32)
    norm_one_pull = jax.vjp(layer_norm, inputs, ln1_gain, ln1_bias)[1]
    din_part, grad_ln1_gain, grad_ln1_bias = norm_one_pull(da_one)
    grad_molecules = dmid + din_part
    hashes_here = bucket_ids.shape[0]
    offsets = (jnp.arange(hashes_here, dtype=jnp.int32) * BUCKETS)[:, None, None]
    flat_ids = (bucket_ids + offsets).reshape(-1)
    tally = (
        jnp.zeros((hashes_here * BUCKETS,), jnp.int32)
        .at[flat_ids]
        .add(1)
        .reshape(hashes_here, BUCKETS)
    )
    summed = lax.psum(
        (
            grad_ln1_gain,
            grad_ln1_bias,
            grad_w_qkv,
            grad_qkv_bias,
            grad_w_out,
            grad_out_bias,
            grad_ln2_gain,
            grad_ln2_bias,
            grad_w_up,
            grad_up_bias,
            grad_w_down,
            grad_down_bias,
        ),
        ("rows", "seq"),
    )
    counts = lax.psum(tally, ("rows", "seq"))
    return (
        layer_out,
        grad_molecules,
        summed[0],
        summed[1],
        summed[2],
        summed[3],
        summed[4],
        summed[5],
        summed[6],
        summed[7],
        summed[8],
        summed[9],
        summed[10],
        summed[11],
        counts,
    )


def solution(mesh):
    placed = (
        P("rows", "seq", None),
        P(),
        P(),
        P(),
        P(),
        P(),
        P(),
        P(),
        P(),
        P(),
        P(),
        P(),
        P(),
        P("rows", "seq", None),
        P(None, "rows", "seq"),
    )
    return jax.shard_map(
        on_device,
        mesh=mesh,
        in_specs=placed,
        out_specs=(
            P("rows", "seq", None),
            P("rows", "seq", None),
            P(),
            P(),
            P(),
            P(),
            P(),
            P(),
            P(),
            P(),
            P(),
            P(),
            P(),
            P(),
            P(),
        ),
        check_vma=False,
    )
```

profile of v0, /device:TPU:0, one launch (start us, length us, event | category | flops | bytes accessed | tf_op | source)
XLA Modules:
  0.0 1104.1 jit_solution(9991028642667410425)
XLA Ops:
  8.1 2.2 convert_reduce_fusion.2
  13.5 5.8 add_convert_fusion.1
  19.3 6.6 copy.126
  25.9 5.4 copy.127
  31.3 58.0 %all_to_all.69 = bf16[8,128,3,768]{1,0,2,3:T(8,128)(2,1)S(1)} all-to-all(bf16[8,128,3,768]{1,0,2,3:T(8,128)(2,1)S(1)} %copy.127), channel_id=1, replica_groups=mesh['rows'=8,'seq'=4] {'seq'}, dimensions={3} | all-to-all | bytes 9437184 | tf_op jit(solution)/shard_map/all_to_all | solution.py:88
  89.2 2.2 copy-done.2
  91.4 5.8 copy.129
  97.3 8.0 reshape.223
  105.3 13.7 %multiply_reduce_fusion.1 = (f32[8,3,512]{2,1,0:T(4,128)S(1)}, f32[8,3,512,512]{2,3,1,0:T(8,128)}) fusion(bf16[8,512,3,3,64]{1,4,3,0,2:T(8,128)(2,1)} %reshape.223), kind=kOutput, calls=%fused_computation.25 | convolution fusion | flops 817876992 | bytes 28360704 | tf_op jit(solution)/shard_map/nqhd,nkhd->nhqk/dot_general | solution.py:28
  119.0 10.7 fusion.13
  129.7 12.3 %fusion.48 = bf16[8,3,64,512]{3,2,1,0:T(8,128)(2,1)} fusion(f32[8,3,512,512]{2,3,1,0:T(8,128)} %get-tuple-element.89, f32[8,3,512]{2,1,0:T(4,128)S(1)} %fusion.13, f32[8,3,512]{2,1,0:T(4,128)S(1)} %get-tuple-element.88, bf16[8,512,3,3,64]{1,4,3,0,2:T(8,128)(2,1)S(1)} %copy-done.9), kind=kOutput, calls=%fused_computation.94 | convolution fusion | flops 831258624 | bytes 28442624 | tf_op jit(solution)/shard_map/nhqk,nkhd->nqhd/dot_general | solution.py:35
  142.0 4.4 copy.131
  146.4 4.6 all-to-all-start.1
  154.4 22.4 %all-to-all-done.1 = bf16[8,512,192]{2,0,1:T(8,128)(2,1)} async-done(((bf16[8,512,192]{2,0,1:T(8,128)(2,1)}), bf16[8,512,192]{2,0,1:T(8,128)(2,1)}, u32[]{:S(2)}, u32[]{:S(2)}) %all-to-all-start.1) | async-done | bytes 1572896 | tf_op jit(solution)/shard_map/all_to_all | solution.py:90
  176.8 3.7 copy.160
  185.5 8.3 fusion.44
  193.8 30.5 %multiply_convert_fusion.1 = (bf16[8,128,3072]{2,1,0:T(8,128)(2,1)}, f32[8,128,3072]{2,1,0:T(8,128)}) fusion(f32[8,128,3072]{2,1,0:T(8,128)S(1)} %get-tuple-element.92, f32[3072]{0:T(1024)S(1)} %copy-done.36, u8[128,3072]{1,0:T(8,128)(4,1)S(1)} %get-tuple-element.44, u8[128,3072]{1,0:T(8,128)(4,1)S(1)} %get-tuple-element.43), kind=kLoop, calls=%fused_computation.36 | loop fusion | flops 223346688 | bytes 32256000 | tf_op jit(solution)/shard_map/convert_element_type | solution.py:94
  224.3 18.7 %convert_reduce_fusion = (f32[3072]{0:T(1024)}, bf16[8,128,3072]{2,1,0:T(8,128)(2,1)}) fusion(f32[8,128,3072]{2,1,0:T(8,128)} %get-tuple-element.81, bf16[8,128,768]{2,1,0:T(8,128)(2,1)} %param.30, bf16[3072,768]{1,0:T(8,128)(2,1)} %param.28, f32[8,128,3072]{2,1,0:T(8,128)} %copy-done.10, f32[3072]{0:T(1024)S(1)} %copy-done.36), kind=kOutput, calls=%fused_computation.34 | convolution fusion | flops 4885312512 | bytes 37773312 | tf_op jit(solution)/shard_map/dot_general | solution.py:100
  243.0 9.9 multiply_reduce_fusion.2
  257.1 2.6 convolution_convert_fusion
  259.7 2.9 copy.136
  262.6 4.3 all-to-all-start.2
  269.4 172.1 %scatter_custom_fusion = s32[131072]{0:T(1024)} fusion(s32[32768]{0:T(1024)} %bitcast.172, s32[32768]{0:T(1024)} %broadcast.238, s32[]{:T(128)} %copy.176), kind=kCustom, calls=%fused_computation.105 | custom fusion | flops 32768 | bytes 524800 | tf_op jit(solution)/shard_map/scatter-add | solution.py:131
  443.4 8.1 copy.135
  451.5 8.1 all_to_all.57
  461.1 4.7 convolution_bitcast_fusion.3
  465.8 3.8 copy.138
  469.5 3.7 all_to_all.61
  473.2 60.8 %while.10 = (s32[]{:T(128)}, bf16[8,512,3,192]{1,3,2,0:T(8,128)(2,1)}, bf16[8,512,3,192]{1,3,2,0:T(8,128)(2,1)}, f32[8,3,512]{2,1,0:T(4,128)}, bf16[8,512,192]{1,2,0:T(8,128)(2,1)}, /*index=5*/s32[]{:T(128)}) while((s32[]{:T(128)}, bf16[8,512,3,192]{1,3,2,0:T(8,128)(2,1)}, bf16[8,512,3,192]{1,3,2,0:T(8,128)(2,1)}, f32[8,3,512]{2,1,0:T(4,128)}, ...), condition=%wide.region_10.0_spmd, body=%wide.region_8.10_spmd.sunk | while | flops 515013120 | bytes 28356700 | solution.py:114
  534.0 9.2 copy.139
  543.2 5.2 all-to-all-start.3
  548.5 11.4 %convolution_bitcast_fusion.1 = f32[768,3072]{1,0:T(8,128)} fusion(bf16[8,128,3072]{2,1,0:T(8,128)(2,1)} %get-tuple-element.96, f32[8,128,768]{2,1,0:T(8,128)} %copy-done.1, f32[768]{0:T(1024)S(1)} %copy-done.23, f32[768]{0:T(1024)S(1)} %copy-done.22, f32[8,128]{1,0:T(8,128)S(1)} %fusion.58, f32[8,128]{1,0:T(8,128)S(1)} %broadcast_multiply_fusion), kind=kOutput, calls=%fused_computation.53 | convolution fusion | flops 4835770368 | bytes 18888704 | tf_op jit(solution)/shard_map/rld,rlf->df/dot_general | solution.py:103
  559.9 10.1 convolution_bitcast_fusion
  570.0 50.1 %all-to-all-done.3 = bf16[8,512,3,192]{3,0,2,1:T(8,128)(2,1)} async-done(((bf16[8,512,3,192]{3,0,2,1:T(8,128)(2,1)}), bf16[8,512,3,192]{3,0,2,1:T(8,128)(2,1)}, u32[]{:S(2)}, u32[]{:S(2)}) %all-to-all-start.3) | async-done | bytes 4718624 | tf_op jit(solution)/shard_map/all_to_all | solution.py:115
  620.1 8.6 copy.163
  628.8 3.7 copy.141
  632.5 2.1 copy-done.15
  634.6 6.6 convolution_bitcast_fusion.2
  641.9 10.1 add_convert_fusion.2
  652.0 4.5 convert_reduce_fusion.1
  661.2 8.2 fusion.60
  669.5 2.3 fusion.39
  671.8 3.3 convert_reduce_fusion.3
  675.2 42.9 %all-reduce = (f32[768]{0:T(1024)}, f32[768]{0:T(1024)}, f32[2,768]{1,0:T(2,128)}, f32[768]{0:T(1024)}, f32[768]{0:T(1024)}, /*index=5*/f32[768]{0:T(1024)}, f32[3072]{0:T(1024)}, f32[768]{0:T(1024)}) all-reduce(f32[768]{0:T(1024)} %get-tuple-element.47, ...), channel_id=1, replica_groups=mesh['rows'=8,'seq'=4] {'rows','seq'}, use_global_device_ids=true, to_apply=%region_14.0 | all-reduce | flops 9216 | bytes 73728 | tf_op jit(solution)/shard_map/psum | solution.py:134
  718.1 356.8 %all-reduce.7.cloned.1.call-done = (f32[768,2304]{1,0:T(8,128)}, f32[768,768]{1,0:T(8,128)}, f32[768,3072]{1,0:T(8,128)}, f32[3072,768]{1,0:T(8,128)}) async-done(((f32[768,2304]{1,0:T(8,128)}, f32[768,768]{1,0:T(8,128)}, f32[768,3072]{1,0:T(8,128)}, f32[3072,768]{1,0:T(8,128)}), (f32[768,2304]{1,0:T(8,128)}, f32[768,768]{1,0:T(8,128)}, f32[768,3072]{1,0:T(8,128)}, ...) | async-done | bytes 28311568 | tf_op jit(solution)/shard_map/psum | solution.py:134
  1075.0 6.6 copy.177
  1083.0 9.3 copy.179
  1092.3 3.7 copy.180
  (211 shorter events, 90.8 us)
Async XLA Ops:
  7.2 6.3 copy-start
  7.2 6.3 copy-start.3
  7.2 6.3 copy-start.38
  7.2 6.3 copy-start.33
  10.3 2.6 copy-start.25
  89.2 2.2 copy-start.2
  119.0 10.7 copy-start.20
  119.0 10.7 copy-start.9
  129.7 12.3 %copy-start.24 = (f32[8,3,512]{2,1,0:T(4,128)}, f32[8,3,512]{2,1,0:T(4,128)S(1)}, u32[]{:S(2)}) copy-start(f32[8,3,512]{2,1,0:T(4,128)S(1)} %fusion.13) | copy-start | bytes 147460
  146.4 30.4 %all-to-all-start.1 = ((bf16[8,512,192]{2,0,1:T(8,128)(2,1)}), bf16[8,512,192]{2,0,1:T(8,128)(2,1)}, u32[]{:S(2)}, u32[]{:S(2)}) async-start(bf16[8,512,192]{2,0,1:T(8,128)(2,1)} %copy.131), calls=%async_computation.1 | async-start | bytes 4194304 | tf_op jit(solution)/shard_map/all_to_all | solution.py:90
  176.8 5.7 copy-start.37
  180.5 2.0 copy-start.4
  180.5 2.2 copy-start.18
  182.4 2.0 copy-start.14
  182.4 2.8 slice-start.3
  182.7 2.6 slice-start.4
  184.4 68.5 %copy-start.1 = (f32[8,128,768]{2,1,0:T(8,128)}, f32[8,128,768]{2,1,0:T(8,128)S(1)}, u32[]{:S(2)}) copy-start(f32[8,128,768]{2,1,0:T(8,128)S(1)} %get-tuple-element.91) | copy-start | bytes 9437188
  184.5 0.9 copy-start.22
  184.5 0.9 copy-start.23
  184.5 1.0 copy-start.36
  193.8 30.5 %copy-start.10 = (f32[8,128,3072]{2,1,0:T(8,128)}, f32[8,128,3072]{2,1,0:T(8,128)S(1)}, u32[]{:S(2)}) copy-start(f32[8,128,3072]{2,1,0:T(8,128)S(1)} %get-tuple-element.92) | copy-start | bytes 37748740
  252.9 1.4 copy-start.11
  254.3 1.7 copy-start.7
  254.3 1.7 copy-start.29
  254.3 2.8 copy-start.19
  255.9 1.2 copy-start.17
  262.6 203.2 %all-to-all-start.2 = ((bf16[8,128,768]{1,0,2:T(8,128)(2,1)}), bf16[8,128,768]{1,0,2:T(8,128)(2,1)}, u32[]{:S(2)}, u32[]{:S(2)}) async-start(bf16[8,128,768]{1,0,2:T(8,128)(2,1)} %copy.136), calls=%async_computation.2 | async-start | bytes 3145728 | tf_op jit(solution)/shard_map/all_to_all | solution.py:113
  266.9 451.2 %all-reduce.5.cloned.1.call-start = ((), (), s32[]{:S(2)}) async-start(), calls=%async_computation.4 | async-start | bytes 1048576 | tf_op jit(solution)/shard_map/psum | solution.py:151
  543.2 77.0 %all-to-all-start.3 = ((bf16[8,512,3,192]{3,0,2,1:T(8,128)(2,1)}), bf16[8,512,3,192]{3,0,2,1:T(8,128)(2,1)}, u32[]{:S(2)}, u32[]{:S(2)}) async-start(bf16[8,512,3,192]{3,0,2,1:T(8,128)(2,1)} %copy.139), calls=%async_computation.3 | async-start | bytes 12582912 | tf_op jit(solution)/shard_map/all_to_all | solution.py:115
  548.4 526.6 %all-reduce.7.cloned.1.call-start = ((), (), s32[]{:S(2)}) async-start(), calls=%async_computation.5 | async-start | bytes 56623104 | tf_op jit(solution)/shard_map/psum | solution.py:134
  548.5 11.4 %copy-start.12 = (bf16[8,128,768]{2,1,0:T(8,128)(2,1)S(1)}, bf16[8,128,768]{2,1,0:T(8,128)(2,1)}, u32[]{:S(2)}) copy-start(bf16[8,128,768]{2,1,0:T(8,128)(2,1)} %param.30) | copy-start | bytes 4718596
  628.7 5.8 copy-start.5
  628.7 5.8 copy-start.26
  628.7 5.8 copy-start.28
  628.8 5.8 copy-start.34
  628.8 5.8 copy-start.39
  632.5 2.1 copy-start.15
  661.2 8.3 copy-start.32
  661.2 8.3 copy-start.6
  661.2 8.3 copy-start.35
  669.4 2.3 copy-start.8
  669.4 2.4 copy-start.13
  669.4 2.4 copy-start.30
  1075.0 6.6 copy-start.16
  1081.5 10.7 slice-start
  1082.9 9.3 slice-start.1
  1083.0 9.3 slice-start.2
  1092.3 3.8 copy-start.21
  (3 other events, 1.9 us)
Sparse Core Ops, SparseCore 0:
  443.5 129.7 all-reduce.4
  641.4 433.5 all-reduce.6
where the time goes:
time: 1110 us; the launch traced here: 1100 us
  waiting for transfers between devices  429 us (39%)
  other arithmetic  250 us (23%)
  matrix products  149 us (13%)
  local copies, waits for them, and re-layouts  146 us (13%)
  blocking collectives  101 us (9%)
  between operations  15 us (1%)
  starting transfers between devices  14.3 us (1%)
    psum x1, waiting for transfers between devices, on_device(): lax.psum((grad_ln1_gain, grad_ln1_bias, grad_w_qkv, grad_qkv_bias, grad_w...  357 us
    scatter-add x1, other arithmetic, on_device(): tally = jnp.zeros((hashes_here * BUCKETS,), jnp.int32).at[flat_ids].add(1...  172 us
    all_to_all x1, blocking collectives, on_device(): lax.all_to_all(qkv_low, 'seq', split_axis=3, concat_axis=1, tiled=True)  58 us
    all_to_all x1, waiting for transfers between devices, on_device(): lax.all_to_all(dqkv_heads, 'seq', split_axis=1, concat_axis=3, tiled=True)  50.1 us
    psum x1, blocking collectives, on_device(): lax.psum((grad_ln1_gain, grad_ln1_bias, grad_w_qkv, grad_qkv_bias, grad_w...  42.9 us
    unnamed x97, local copies, waits for them, and re-layouts  30.6 us
    convert_element_type x1, other arithmetic, on_device(): hidden = gelu_exact(upper).astype(jnp.bfloat16)  30.5 us
    all_to_all x1, waiting for transfers between devices, on_device(): lax.all_to_all(ctx_heads, 'seq', split_axis=1, concat_axis=2, tiled=True)  22.4 us
  transfers between devices with their start and end apart: 5, of which 3 were waited for; matrix products, arithmetic and copies ran while one was open for 31% of the time, Pallas kernels for 0%

commit v1 on v0

v1 whole, which is shorter than its diff:
```python
import functools
import jax
import jax.numpy as jnp
from jax import lax
from jax.experimental import pallas as pl
from jax.experimental.pallas import tpu as pltpu
from jax.sharding import PartitionSpec as P

MESH = pl.DeviceIdType.MESH
BF = jnp.bfloat16
F32 = jnp.float32
EPS = 1e-5
D = 768
HD = 64
NH = 12
FF = 3072
BUCKETS = 16384
LANE = 128
MIB = 1 << 20


def dot_nn(a, b):
    return lax.dot_general(a, b, (((1,), (0,)), ((), ())), preferred_element_type=F32)


def dot_nt(a, b):
    return lax.dot_general(a, b, (((1,), (1,)), ((), ())), preferred_element_type=F32)


def dot_tn(a, b):
    return lax.dot_general(a, b, (((0,), (0,)), ((), ())), preferred_element_type=F32)


def norm_parts(x):
    mean = jnp.mean(x, -1, keepdims=True)
    cen = x - mean
    var = jnp.mean(cen * cen, -1, keepdims=True)
    rstd = lax.rsqrt(var + EPS)
    return cen * rstd, rstd


def norm_back(xhat, rstd, gain, dy):
    dxh = dy * gain
    m1 = jnp.mean(dxh, -1, keepdims=True)
    m2 = jnp.mean(dxh * xhat, -1, keepdims=True)
    return rstd * (dxh - m1 - xhat * m2)


def lane_half(shape, half):
    lane = lax.broadcasted_iota(jnp.int32, shape, 1)
    return (lane < HD) if half == 0 else (lane >= HD)


def fwd_kernel(x_ref, g1_ref, b1_ref, wqkv_ref, qb_ref, wout_ref, ob_ref, qkv_ref, lse_ref, ctx_ref, mid_ref, lacc):
    length = x_ref.shape[0]
    x = x_ref[...].astype(F32)
    xhat, _ = norm_parts(x)
    a1 = (xhat * g1_ref[...] + b1_ref[...]).astype(BF)
    for j in range(3):
        c = slice(j * D, (j + 1) * D)
        qkv_ref[:, c] = (dot_nn(a1, wqkv_ref[:, c]) + qb_ref[:, c]).astype(BF)

    def pair(p, carry):
        at = pl.multiple_of(p * LANE, LANE)
        q = qkv_ref[:, pl.ds(at, LANE)] * BF(0.125)
        k = qkv_ref[:, pl.ds(pl.multiple_of(D + at, LANE), LANE)]
        v = qkv_ref[:, pl.ds(pl.multiple_of(2 * D + at, LANE), LANE)]
        outs = []
        lse = lacc[...]
        lane = lax.broadcasted_iota(jnp.int32, lse.shape, 1)
        for half in range(2):
            qm = jnp.where(lane_half(q.shape, half), q, BF(0))
            s = dot_nt(qm, k)
            m = jnp.max(s, -1, keepdims=True)
            e = jnp.exp(s - m)
            t = jnp.sum(e, -1, keepdims=True)
            pr = (e * (1.0 / t)).astype(BF)
            outs.append(dot_nn(pr, v))
            lse = jnp.where(lane == 2 * p + half, m + jnp.log(t), lse)
        lacc[...] = lse
        ctx_ref[:, pl.ds(at, LANE)] = jnp.where(lane_half(outs[0].shape, 0), outs[0], outs[1]).astype(BF)
        return carry

    lacc[...] = jnp.zeros_like(lacc)
    lax.fori_loop(0, NH // 2, pair, 0)
    lt = lacc[...].T
    for h in range(NH):
        lse_ref[h] = lt[h : h + 1, :]
    mid_ref[...] = x + (dot_nn(ctx_ref[...], wout_ref[...]) + ob_ref[...])


def forward(x, g1, b1, wqkv, qb, wout, ob, length):
    tokens = x.shape[0]
    rows = tokens // length
    whole = lambda a: pl.BlockSpec(a.shape, lambda i: (0,) * a.ndim)
    return pl.pallas_call(
        fwd_kernel,
        grid=(rows,),
        in_specs=[pl.BlockSpec((length, D), lambda i: (i, 0))] + [whole(a) for a in (g1, b1, wqkv, qb, wout, ob)],
        out_specs=[
            pl.BlockSpec((length, 3 * D), lambda i: (i, 0)),
            pl.BlockSpec((NH, 1, length), lambda i: (i, 0, 0)),
            pl.BlockSpec((length, D), lambda i: (i, 0)),
            pl.BlockSpec((length, D), lambda i: (i, 0)),
        ],
        out_shape=[
            jax.ShapeDtypeStruct((tokens, 3 * D), BF),
            jax.ShapeDtypeStruct((rows * NH, 1, length), F32),
            jax.ShapeDtypeStruct((tokens, D), BF),
            jax.ShapeDtypeStruct((tokens, D), F32),
        ],
        scratch_shapes=[pltpu.VMEM((length, LANE), F32)],
        compiler_params=pltpu.CompilerParams(vmem_limit_bytes=58 * MIB),
        name="attn_forward",
    )(x, g1, b1, wqkv, qb, wout, ob)


def mlp_kernel(nb, mid_ref, dy_ref, g2_ref, b2_ref, wup_ref, ub_ref, wdn_ref, db_ref,
               lo_ref, dx2_ref, gd_ref, gu_ref, vec_ref, gub_ref, a2_s, a2t_s, dyt_s, acc_s, da2_s):
    i = pl.program_id(0)

    @pl.when(i == 0)
    def _():
        xhat, _ = norm_parts(mid_ref[...])
        a2 = (xhat * g2_ref[...] + b2_ref[...]).astype(BF)
        a2_s[...] = a2
        a2t_s[...] = a2.T
        dyt_s[...] = dy_ref[...].T
        acc_s[...] = mid_ref[...] + db_ref[...]
        da2_s[...] = jnp.zeros_like(da2_s)

    u = dot_nn(a2_s[...], wup_ref[...]) + ub_ref[...]
    dh = dot_nt(dy_ref[...], wdn_ref[...])
    cdf = 0.5 + 0.5 * lax.erf(u * (2.0 ** -0.5))
    pdf = jnp.exp(u * u * -0.5) * 0.3989422804014327
    hid = (u * cdf).astype(BF)
    du32 = dh * (cdf + u * pdf)
    du = du32.astype(BF)
    gub_ref[...] = jnp.sum(du.astype(F32), 0, keepdims=True)
    acc_s[...] += dot_nn(hid, wdn_ref[...])
    da2_s[...] += dot_nt(du, wup_ref[...])
    gd = dot_nn(dyt_s[...], hid).astype(BF)
    gu = dot_nn(a2t_s[...], du).astype(BF)
    for j in range(nb):
        gd_ref[j] = gd[:, j * LANE : (j + 1) * LANE]
        gu_ref[j] = gu[:, j * LANE : (j + 1) * LANE]

    @pl.when(i == pl.num_programs(0) - 1)
    def _():
        lo_ref[...] = acc_s[...].astype(BF)
        dy = dy_ref[...].astype(F32)
        xhat, rstd = norm_parts(mid_ref[...])
        da2 = da2_s[...]
        dx2 = dy + norm_back(xhat, rstd, g2_ref[...], da2)
        dx2_ref[...] = dx2
        vec_ref[0:1, :] = jnp.sum(dy, 0, keepdims=True)
        vec_ref[1:2, :] = jnp.sum(da2 * xhat, 0, keepdims=True)
        vec_ref[2:3, :] = jnp.sum(da2, 0, keepdims=True)
        vec_ref[3:4, :] = jnp.sum(dx2.astype(BF).astype(F32), 0, keepdims=True)
        vec_ref[4:8, :] = jnp.zeros((4, D), F32)


def mlp(mid, dy, g2, b2, wup, ub, wdn, db, nb):
    tokens = mid.shape[0]
    fc = nb * LANE
    whole = lambda a: pl.BlockSpec(a.shape, lambda i: (0,) * a.ndim)
    tok = pl.BlockSpec((tokens, D), lambda i: (0, 0))
    return pl.pallas_call(
        functools.partial(mlp_kernel, nb),
        grid=(FF // fc,),
        in_specs=[tok, tok, whole(g2), whole(b2), pl.BlockSpec((D, fc), lambda i: (0, i)), pl.BlockSpec((1, fc), lambda i: (0, i)),
                  pl.BlockSpec((fc, D), lambda i: (i, 0)), whole(db)],
        out_specs=[tok, tok, pl.BlockSpec((nb, D, LANE), lambda i: (i, 0, 0)), pl.BlockSpec((nb, D, LANE), lambda i: (i, 0, 0)),
                   pl.BlockSpec((8, D), lambda i: (0, 0)), pl.BlockSpec((1, fc), lambda i: (0, i))],
        out_shape=[jax.ShapeDtypeStruct((tokens, D), BF), jax.ShapeDtypeStruct((tokens, D), F32),
                   jax.ShapeDtypeStruct((FF // LANE, D, LANE), BF), jax.ShapeDtypeStruct((FF // LANE, D, LANE), BF),
                   jax.ShapeDtypeStruct((8, D), F32), jax.ShapeDtypeStruct((1, FF), F32)],
        scratch_shapes=[pltpu.VMEM((tokens, D), BF), pltpu.VMEM((D, tokens), BF), pltpu.VMEM((D, tokens), BF),
                        pltpu.VMEM((tokens, D), F32), pltpu.VMEM((tokens, D), F32)],
        compiler_params=pltpu.CompilerParams(vmem_limit_bytes=60 * MIB),
        name="feed_forward",
    )(mid, dy, g2, b2, wup, ub, wdn, db)


def bwd_kernel(length, x_ref, qkv_ref, lse_ref, ctx_ref, dx2_ref, g1_ref, b1_ref, wqkv_ref, wout_ref,
               gm_ref, gr_ref, vec_ref, dctx_s, dqkv_s, do_s):
    tokens = x_ref.shape[0]
    rows = tokens // length
    do_s[...] = dx2_ref[...].astype(BF)
    dctx_s[...] = dot_nt(do_s[...], wout_ref[...]).astype(BF)
    gout = dot_tn(ctx_ref[...], do_s[...]).astype(BF)
    nq = 3 * D // LANE
    for j in range(D // LANE):
        gr_ref[nq + j] = gout[:, j * LANE : (j + 1) * LANE]

    def pair(i, carry):
        r = i // (NH // 2)
        p = i % (NH // 2)
        tok = pl.ds(pl.multiple_of(r * length, length), length)
        cq = pl.ds(pl.multiple_of(p * LANE, LANE), LANE)
        ck = pl.ds(pl.multiple_of(p * LANE + D, LANE), LANE)
        cv = pl.ds(pl.multiple_of(p * LANE + 2 * D, LANE), LANE)
        q = qkv_ref[tok, cq] * BF(0.125)
        k = qkv_ref[tok, ck]
        v = qkv_ref[tok, cv]
        dc = dctx_s[tok, cq]
        dqs, dks, dvs = [], [], []
        for half in range(2):
            keep = lane_half(k.shape, half)
            km = jnp.where(keep, k, BF(0))
            vm = jnp.where(keep, v, BF(0))
            lse = lse_ref[r * NH + 2 * p + half]
            st = dot_nt(km, q)
            pt = jnp.exp(st - lse)
            dpt = dot_nt(vm, dc)
            inner = jnp.sum(pt * dpt, 0, keepdims=True)
            dst = (pt * (dpt - inner)).astype(BF)
            dvs.append(dot_nn(pt.astype(BF), dc))
            dks.append(dot_nn(dst, q))
            dqs.append(dot_tn(dst, k))
        sel = lane_half(dqs[0].shape, 0)
        dqkv_s[tok, cq] = (jnp.where(sel, dqs[0], dqs[1]) * 0.125).astype(BF)
        dqkv_s[tok, ck] = jnp.where(sel, dks[0], dks[1]).astype(BF)
        dqkv_s[tok, cv] = jnp.where(sel, dvs[0], dvs[1]).astype(BF)
        return carry

    lax.fori_loop(0, rows * (NH // 2), pair, 0)
    xhat, rstd = norm_parts(x_ref[...].astype(F32))
    a1 = (xhat * g1_ref[...] + b1_ref[...]).astype(BF)
    a1t = a1.T
    for j in range(3):
        c = slice(j * D, (j + 1) * D)
        gq = dot_nn(a1t, dqkv_s[:, c]).astype(BF)
        for t in range(D // LANE):
            gr_ref[j * (D // LANE) + t] = gq[:, t * LANE : (t + 1) * LANE]
    da1 = dot_nt(dqkv_s[...], wqkv_ref[...])
    gm_ref[...] = (dx2_ref[...] + norm_back(xhat, rstd, g1_ref[...], da1)).astype(BF)
    vec_ref[0:1, :] = jnp.sum(da1 * xhat, 0, keepdims=True)
    vec_ref[1:2, :] = jnp.sum(da1, 0, keepdims=True)
    vec_ref[2:3, :] = jnp.sum(dqkv_s[:, 0:D].astype(F32), 0, keepdims=True)
    vec_ref[3:4, :] = jnp.sum(dqkv_s[:, 2 * D : 3 * D].astype(F32), 0, keepdims=True)
    vec_ref[4:8, :] = jnp.zeros((4, D), F32)


def backward(x, qkv, lse, ctx, dx2, g1, b1, wqkv, wout, length):
    tokens = x.shape[0]
    vm = pl.BlockSpec(memory_space=pltpu.VMEM)
    return pl.pallas_call(
        functools.partial(bwd_kernel, length),
        in_specs=[vm] * 9,
        out_specs=[vm] * 3,
        out_shape=[jax.ShapeDtypeStruct((tokens, D), BF), jax.ShapeDtypeStruct((4 * D // LANE, D, LANE), BF),
                   jax.ShapeDtypeStruct((8, D), F32)],
        scratch_shapes=[pltpu.VMEM((tokens, D), BF), pltpu.VMEM((tokens, 3 * D), BF), pltpu.VMEM((tokens, D), BF)],
        compiler_params=pltpu.CompilerParams(vmem_limit_bytes=60 * MIB),
        name="attn_backward",
    )(x, qkv, lse, ctx, dx2, g1, b1, wqkv, wout)


def count_kernel(ids_ref, out_ref):
    hashes, rows, chars = ids_ref.shape
    high = BUCKETS // LANE

    def one(h, carry):
        total = jnp.zeros((high, LANE), F32)
        for r in range(rows):
            ids = ids_ref[h, r : r + 1, :]
            row = lax.broadcasted_iota(jnp.int32, (high, chars), 0)
            hi = jnp.where(row == (ids >> 7), 1.0, 0.0).astype(BF)
            lo = jnp.where(row == (ids & (LANE - 1)), 1.0, 0.0).astype(BF)
            total = total + dot_nt(hi, lo)
        out_ref[h] = total.astype(jnp.int32)
        return carry

    lax.fori_loop(0, hashes, one, 0)


def count(ids):
    return pl.pallas_call(
        count_kernel,
        in_specs=[pl.BlockSpec(memory_space=pltpu.VMEM)],
        out_specs=pl.BlockSpec(memory_space=pltpu.VMEM),
        out_shape=jax.ShapeDtypeStruct((ids.shape[0], BUCKETS // LANE, LANE), jnp.int32),
        compiler_params=pltpu.CompilerParams(vmem_limit_bytes=32 * MIB),
        name="bucket_tally",
    )(ids)


def widen_kernel(src_ref, out_ref):
    for j in range(src_ref.shape[0]):
        out_ref[:, j * LANE : (j + 1) * LANE] = src_ref[j].astype(F32)


def widen(blocks, at, number, step):
    assert at % step == 0
    return pl.pallas_call(
        widen_kernel,
        grid=(number // step,),
        in_specs=[pl.BlockSpec((step, D, LANE), lambda i: (at // step + i, 0, 0))],
        out_specs=pl.BlockSpec((D, step * LANE), lambda i: (0, i)),
        out_shape=jax.ShapeDtypeStruct((D, number * LANE), F32),
        compiler_params=pltpu.CompilerParams(vmem_limit_bytes=32 * MIB),
        name="widen",
    )(blocks)


def widen_t_kernel(src_ref, out_ref):
    for j in range(src_ref.shape[0]):
        out_ref[j * LANE : (j + 1) * LANE, :] = src_ref[j].astype(F32).T


def widen_t(blocks, at, number, step):
    assert at % step == 0
    return pl.pallas_call(
        widen_t_kernel,
        grid=(number // step,),
        in_specs=[pl.BlockSpec((step, D, LANE), lambda i: (at // step + i, 0, 0))],
        out_specs=pl.BlockSpec((step * LANE, D), lambda i: (i, 0)),
        out_shape=jax.ShapeDtypeStruct((number * LANE, D), F32),
        compiler_params=pltpu.CompilerParams(vmem_limit_bytes=32 * MIB),
        name="widen_turned",
    )(blocks)


def on_device(shape, molecules, ln1_gain, ln1_bias, w_qkv, qkv_bias, w_out, out_bias, ln2_gain, ln2_bias, w_up, up_bias,
              w_down, down_bias, out_cotangent, bucket_ids):
    rows_here, local_len, width = molecules.shape
    seq = shape["seq"]
    length = local_len * seq
    row = lambda a: a.reshape(1, -1)
    tally = count(bucket_ids)
    counts = lax.psum(tally, ("rows", "seq")).reshape(bucket_ids.shape[0], BUCKETS)
    x = lax.all_to_all(molecules, "seq", split_axis=0, concat_axis=1, tiled=True).reshape(-1, width)
    dy = lax.all_to_all(out_cotangent, "seq", split_axis=0, concat_axis=1, tiled=True).reshape(-1, width)
    qb = jnp.concatenate([qkv_bias[0], jnp.zeros((width,), F32), qkv_bias[1]]).reshape(1, -1)
    qkv, lse, ctx, mid = forward(x, row(ln1_gain), row(ln1_bias), w_qkv, qb, w_out, row(out_bias), length)
    lo, dx2, gd, gu, vec2, gub = mlp(mid, dy, row(ln2_gain), row(ln2_bias), w_up, row(up_bias), w_down, row(down_bias), 4)
    gm, gr, vec1 = backward(x, qkv, lse, ctx, dx2, row(ln1_gain), row(ln1_bias), w_qkv, w_out, length)
    back = lambda a: lax.all_to_all(a.reshape(-1, length, width), "seq", split_axis=1, concat_axis=0, tiled=True)
    layer_out = back(lo)
    gmol = back(gm).astype(F32)
    gd, gu, gr = lax.psum((gd, gu, gr), ("rows", "seq"))
    small = lax.psum(jnp.concatenate([vec2.reshape(-1), vec1.reshape(-1), gub.reshape(-1)]), ("rows", "seq"))
    v2 = small[: 8 * D].reshape(8, D)
    v1 = small[8 * D : 16 * D].reshape(8, D)
    return (layer_out, gmol, v1[0], v1[1], widen(gr, 0, 18, 6), v1[2:4], widen(gr, 18, 6, 6), v2[3], v2[1], v2[2],
            widen(gu, 0, 24, 6), small[16 * D :], widen_t(gd, 0, 24, 6), v2[0], counts)


def solution(mesh):
    tok = P("rows", "seq", None)
    return jax.shard_map(
        functools.partial(on_device, dict(mesh.shape)),
        mesh=mesh,
        in_specs=(tok,) + (P(),) * 12 + (tok, P(None, "rows", "seq")),
        out_specs=(tok, tok) + (P(),) * 13,
        check_vma=False,
    )
```

time: 1110 us -> 561 us (0.51)
  other arithmetic: 250 us -> 1.1 us
  matrix products: 149 us -> 0 us
  waiting for transfers between devices: 429 us -> 299 us
  Pallas kernels: 0 us -> 127 us
  local copies, waits for them, and re-layouts: 146 us -> 24.1 us
  blocking collectives: 101 us -> 83.2 us
    scatter-add x1 -> x0, other arithmetic: 172 us -> none  [on_device(): tally = jnp.zeros((hashes_here * BUCKETS,), jnp.int32).at[flat_ids].add(1...]
    dot_general x54 -> x0, matrix products: 149 us -> none  [the longest x1 18.7 us: on_device(): dhidden = jnp.dot(cot_low, w_down.T, preferred_element_type=jnp.float32)]
    pallas_call x0 -> x8, Pallas kernels: none -> 127 us  [the longest x1 42.3 us: mlp(): pl.pallas_call(functools.partial(mlp_kernel, nb), grid=(FF // fc,), in_sp...]
    psum x2, waiting for transfers between devices: 357 us -> 255 us  [the longest x1 138 us: on_device(): gd, gu, gr = lax.psum((gd, gu, gr), ('rows', 'seq'))]
    all_to_all x9 -> x3, local copies, waits for them, and re-layouts: 47.4 us -> 3.87 us  [the longest x1 1.34 us: on_device(): lax.all_to_all(a.reshape(-1, length, width), 'seq', split_axis=1, concat_...]
    convert_element_type x9 -> x1, other arithmetic: 37.3 us -> 1.08 us  [on_device(): gmol = back(gm).astype(F32)]
    all_to_all x1, blocking collectives: 58 us -> 24.4 us  [on_device(): lax.all_to_all(molecules, 'seq', split_axis=0, concat_axis=1, tiled=True)]
    all_to_all x3, waiting for transfers between devices: 72.5 us -> 43.5 us  [the longest x2 29 us: on_device(): lax.all_to_all(a.reshape(-1, length, width), 'seq', split_axis=1, concat_...]
  transfers between devices with their start and end apart: 5 -> 5, of which waited for: 3 -> 4; matrix products, arithmetic and copies ran while one was open for 31% -> 3% of each run, Pallas kernels for 0% -> 3%
where the time goes in v1:
time: 561 us; the launch traced here: 560 us
  waiting for transfers between devices  299 us (53%)
  Pallas kernels  127 us (23%)
  blocking collectives  83.2 us (15%)
  local copies, waits for them, and re-layouts  24.1 us (4%)
  between operations  14.3 us (3%)
  starting transfers between devices  11.2 us (2%)
    psum x1, waiting for transfers between devices, on_device(): gd, gu, gr = lax.psum((gd, gu, gr), ('rows', 'seq'))  138 us
    psum x1, waiting for transfers between devices, on_device(): lax.psum(tally, ('rows', 'seq')).reshape(bucket_ids.shape[0], BUCKETS)  118 us
    psum x1, blocking collectives, on_device(): lax.psum(jnp.concatenate([vec2.reshape(-1), vec1.reshape(-1), gub.reshape...  58.8 us
    pallas_call x1, Pallas kernels, mlp(): pl.pallas_call(functools.partial(mlp_kernel, nb), grid=(FF // fc,), in_sp...  42.3 us
    pallas_call x1, Pallas kernels, backward(): pl.pallas_call(functools.partial(bwd_kernel, length), in_specs=[vm] * 9,...  41.4 us
    all_to_all x2, waiting for transfers between devices, on_device(): lax.all_to_all(a.reshape(-1, length, width), 'seq', split_axis=1, concat_...  29 us
    pallas_call x1, Pallas kernels, forward(): pl.pallas_call(fwd_kernel, grid=(rows,), in_specs=[pl.BlockSpec((length,...  26 us
    all_to_all x1, blocking collectives, on_device(): lax.all_to_all(molecules, 'seq', split_axis=0, concat_axis=1, tiled=True)  24.4 us
  transfers between devices with their start and end apart: 5, of which 4 were waited for; matrix products, arithmetic and copies ran while one was open for 3% of the time, Pallas kernels for 3%

profile of v1, /device:TPU:0, one launch (start us, length us, event | category | flops | bytes accessed | tf_op | source)
XLA Modules:
  0.0 560.0 jit_solution(13974824240267108202)
XLA Ops:
  7.2 0.0 copy-start.8
  7.2 0.0 copy-start.9
  7.2 0.0 copy-start.10
  7.2 0.0 copy-start.11
  7.3 24.4 %all_to_all.57 = bf16[8,128,768]{2,1,0:T(8,128)(2,1)S(1)} all-to-all(bf16[8,128,768]{2,1,0:T(8,128)(2,1)} %param.15), channel_id=1, replica_groups=mesh['rows'=8,'seq'=4] {'seq'}, dimensions={0} | all-to-all | bytes 3145728 | tf_op jit(solution)/shard_map/all_to_all | solution.py:333
  31.7 3.6 all-to-all-start.1
  35.3 0.0 all-reduce.6.cloned.1.call-start
  35.4 0.6 reshape.114.qb_ref
  36.0 0.6 reshape.112.g1_ref
  36.6 0.6 reshape.113.b1_ref
  37.1 0.6 reshape.115.ob_ref
  37.7 0.6 reshape.117.g2_ref
  38.3 0.6 reshape.118.b2_ref
  38.9 0.6 reshape.120.db_ref
  39.5 1.3 copy.34
  40.7 14.6 %all-to-all-done.1 = bf16[8,128,768]{2,1,0:T(8,128)(2,1)S(1)} async-done(((bf16[8,128,768]{2,1,0:T(8,128)(2,1)}), bf16[8,128,768]{2,1,0:T(8,128)(2,1)S(1)}, u32[]{:S(2)}, u32[]{:S(2)}) %all-to-all-start.1) | async-done | bytes 1572896 | tf_op jit(solution)/shard_map/all_to_all | solution.py:334
  55.3 1.3 copy.35
  56.6 26.0 %attn_forward.1 = (bf16[1024,2304]{1,0:T(8,128)(2,1)}, f32[24,1,512]{2,1,0:T(1,128)}, bf16[1024,768]{1,0:T(8,128)(2,1)}, f32[1024,768]{1,0:T(8,128)}) custom-call(bf16[1024,768]{1,0:T(8,128)(2,1)} %bitcast.28, f32[1,768]{1,0:T(1,128)} %reshape.112.g1_ref, f32[1,768]{1,0:T(1,128)} %reshape.113.b1_ref, bf16[768,2304]{1,0:T(8,128)(2,1)} %wqkv_ref.3, ...), custom_call_target="tpu_custom_call" | custom-call | tf_op jit(solution)/shard_map/attn_forward/pallas_call | solution.py:96
  82.6 42.3 %feed_forward.1 = (bf16[1024,768]{1,0:T(8,128)(2,1)}, f32[1024,768]{1,0:T(8,128)}, bf16[24,768,128]{2,1,0:T(8,128)(2,1)}, bf16[24,768,128]{2,1,0:T(8,128)(2,1)}, f32[8,768]{1,0:T(8,128)}, /*index=5*/f32[1,3072]{1,0:T(1,128)}) custom-call(f32[1024,768]{1,0:T(8,128)} %get-tuple-element.28.mid_ref, bf16[1024,768]{1,0:T(8,128)(2,1)} %bitcast.33, ...), custom_call_target="tpu_custom_call" | custom-call | tf_op jit(solution)/shard_map/feed_forward/pallas_call | solution.py:168
  124.9 41.4 %attn_backward.1 = (bf16[1024,768]{1,0:T(8,128)(2,1)}, bf16[24,768,128]{2,1,0:T(8,128)(2,1)}, f32[8,768]{1,0:T(8,128)}) custom-call(bf16[1024,768]{1,0:T(8,128)(2,1)} %bitcast.29, bf16[1024,2304]{1,0:T(8,128)(2,1)} %get-tuple-element.30.qkv_ref, f32[24,1,512]{2,1,0:T(1,128)} %get-tuple-element.31.lse_ref, bf16[1024,768]{1,0:T(8,128)(2,1)} %get-tuple-element.32.ctx_ref, ...), custom_call_target="tpu_custom_call" | custom-call | tf_op jit(solution)/shard_map/attn_backward/pallas_call | solution.py:248
  166.3 0.0 all-reduce.6.cloned.1.call-update
  166.4 1.4 copy-done.4
  167.8 2.8 copy.38
  170.5 3.9 all-to-all-start.3
  174.5 0.0 copy-start.2
  174.5 2.8 copy.36
  177.3 29.0 %all-to-all-done.3 = bf16[2,512,768]{2,0,1:T(2,128)(2,1)S(1)} async-done(((bf16[2,512,768]{2,0,1:T(2,128)(2,1)}), bf16[2,512,768]{2,0,1:T(2,128)(2,1)S(1)}, u32[]{:S(2)}, u32[]{:S(2)}) %all-to-all-start.3) | async-done | bytes 1572896 | tf_op jit(solution)/shard_map/all_to_all | solution.py:339
  206.2 3.6 all-to-all-start.2
  209.9 0.0 all-reduce.4.cloned.1.call-start
  209.9 3.7 bucket_tally.1
  213.6 1.1 copy.42
  214.7 0.0 all-reduce.4.cloned.1.call-update
  214.8 58.8 %psum.35 = f32[15360]{0:T(1024)S(1)} all-reduce(f32[15360]{0:T(1024)S(1)} %pad_maximum_fusion), channel_id=1, replica_groups=mesh['rows'=8,'seq'=4] {'rows','seq'}, use_global_device_ids=true, to_apply=%region_0.0 | all-reduce | flops 15360 | bytes 122880 | tf_op jit(solution)/shard_map/psum | solution.py:343
  273.6 0.6 slice.75
  274.2 0.6 slice.63
  274.8 0.6 fusion
  275.4 1.1 convert_bitcast_fusion
  276.5 2.0 copy.39
  278.5 0.0 all-to-all-done.2
  278.5 1.3 copy.37
  279.8 137.9 %all-reduce.6.cloned.1.call-done = (bf16[24,768,128]{2,1,0:T(8,128)(2,1)}, bf16[24,768,128]{2,1,0:T(8,128)(2,1)}, bf16[24,768,128]{2,1,0:T(8,128)(2,1)}) async-done(((bf16[24,768,128]{2,1,0:T(8,128)(2,1)}, bf16[24,768,128]{2,1,0:T(8,128)(2,1)}, bf16[24,768,128]{2,1,0:T(8,128)(2,1)}), (bf16[24,768,128]{2,1,0:T(8,128)(2,1)}, bf16[24,768,128]{2,1,0:T(8,128)(2,1)}, ...) | async-done | bytes 14155792 | tf_op jit(solution)/shard_map/psum | solution.py:342
  417.7 2.3 copy-done
  420.1 3.7 widen.3
  423.8 1.6 widen.4
  425.3 4.1 widen.5
  429.5 4.4 widen_turned.1
  433.8 117.5 %all-reduce.4.cloned.1.call-done = s32[8,16384]{1,0:T(8,128)} async-done(((s32[8,16384]{1,0:T(8,128)}), s32[8,16384]{1,0:T(8,128)}) %all-reduce.4.cloned.1.call-update) | async-done | bytes 524304 | tf_op jit(solution)/shard_map/psum | solution.py:332
  551.3 1.9 copy.47
  (35 shorter events, 0.1 us)
Async XLA Ops:
  7.2 28.1 %copy-start.8 = (f32[2,768]{1,0:T(2,128)S(1)}, f32[2,768]{1,0:T(2,128)}, u32[]{:S(2)}) copy-start(f32[2,768]{1,0:T(2,128)} %param.19) | copy-start | bytes 18436
  7.2 28.8 %copy-start.9 = (f32[768]{0:T(1024)S(1)}, f32[768]{0:T(1024)}, u32[]{:S(2)}) copy-start(f32[768]{0:T(1024)} %param.16) | copy-start | bytes 9220
  7.2 29.4 %copy-start.10 = (f32[768]{0:T(1024)S(1)}, f32[768]{0:T(1024)}, u32[]{:S(2)}) copy-start(f32[768]{0:T(1024)} %param.17) | copy-start | bytes 9220
  7.2 29.9 %copy-start.11 = (f32[768]{0:T(1024)S(1)}, f32[768]{0:T(1024)}, u32[]{:S(2)}) copy-start(f32[768]{0:T(1024)} %param.21) | copy-start | bytes 9220
  7.2 30.5 %copy-start.12 = (f32[768]{0:T(1024)S(1)}, f32[768]{0:T(1024)}, u32[]{:S(2)}) copy-start(f32[768]{0:T(1024)} %param.22) | copy-start | bytes 9220
  7.2 31.1 %copy-start.13 = (f32[768]{0:T(1024)S(1)}, f32[768]{0:T(1024)}, u32[]{:S(2)}) copy-start(f32[768]{0:T(1024)} %param.23) | copy-start | bytes 9220
  7.2 31.7 %copy-start.14 = (f32[768]{0:T(1024)S(1)}, f32[768]{0:T(1024)}, u32[]{:S(2)}) copy-start(f32[768]{0:T(1024)} %param.27) | copy-start | bytes 9220
  31.7 23.6 %all-to-all-start.1 = ((bf16[8,128,768]{2,1,0:T(8,128)(2,1)}), bf16[8,128,768]{2,1,0:T(8,128)(2,1)S(1)}, u32[]{:S(2)}, u32[]{:S(2)}) async-start(bf16[8,128,768]{2,1,0:T(8,128)(2,1)} %param.28), calls=%async_computation.1 | async-start | bytes 3145728 | tf_op jit(solution)/shard_map/all_to_all | solution.py:334
  35.3 382.5 %all-reduce.6.cloned.1.call-start = ((), (), s32[]{:S(2)}) async-start(), calls=%async_computation.5 | async-start | bytes 28311552 | tf_op jit(solution)/shard_map/psum | solution.py:342
  166.3 1.4 copy-start.4
  167.8 6.7 %copy-start.3 = (bf16[1024,768]{1,0:T(8,128)(2,1)S(1)}, bf16[1024,768]{1,0:T(8,128)(2,1)}, u32[]{:S(2)}) copy-start(bf16[1024,768]{1,0:T(8,128)(2,1)} %get-tuple-element.29) | copy-start | bytes 4718596
  170.5 35.7 %all-to-all-start.3 = ((bf16[2,512,768]{2,0,1:T(2,128)(2,1)}), bf16[2,512,768]{2,0,1:T(2,128)(2,1)S(1)}, u32[]{:S(2)}, u32[]{:S(2)}) async-start(bf16[2,512,768]{2,0,1:T(2,128)(2,1)} %copy.38), calls=%async_computation.3 | async-start | bytes 3145728 | tf_op jit(solution)/shard_map/all_to_all | solution.py:339
  174.5 35.4 %copy-start.2 = (s32[8,8,512]{2,1,0:T(8,128)S(1)}, s32[8,8,512]{2,1,0:T(8,128)}, u32[]{:S(2)}) copy-start(s32[8,8,512]{2,1,0:T(8,128)} %ids_ref.1) | copy-start | bytes 393220
  177.2 37.5 %copy-start.6 = (f32[8,768]{1,0:T(8,128)S(1)}, f32[8,768]{1,0:T(8,128)}, u32[]{:S(2)}) copy-start(f32[8,768]{1,0:T(8,128)} %get-tuple-element.36) | copy-start | bytes 73732
  177.3 37.5 %copy-start.5 = (f32[8,768]{1,0:T(8,128)S(1)}, f32[8,768]{1,0:T(8,128)}, u32[]{:S(2)}) copy-start(f32[8,768]{1,0:T(8,128)} %get-tuple-element.35) | copy-start | bytes 73732
  177.3 37.6 %copy-start.7 = (f32[1,3072]{1,0:T(1,128)S(1)}, f32[1,3072]{1,0:T(1,128)}, u32[]{:S(2)}) copy-start(f32[1,3072]{1,0:T(1,128)} %get-tuple-element.37) | copy-start | bytes 36868
  206.2 72.2 %all-to-all-start.2 = ((bf16[2,512,768]{2,0,1:T(2,128)(2,1)}), bf16[2,512,768]{2,0,1:T(2,128)(2,1)S(1)}, u32[]{:S(2)}, u32[]{:S(2)}) async-start(bf16[2,512,768]{2,0,1:T(2,128)(2,1)} %copy.36), calls=%async_computation.2 | async-start | bytes 3145728 | tf_op jit(solution)/shard_map/all_to_all | solution.py:339
  209.9 341.5 %all-reduce.4.cloned.1.call-start = ((), (), s32[]{:S(2)}) async-start(), calls=%async_computation.4 | async-start | bytes 1048576 | tf_op jit(solution)/shard_map/psum | solution.py:332
  417.7 2.3 copy-start
  420.1 5.3 copy-start.1
  423.8 5.7 %slice-start = ((s8[4718592]{0:T(1024)(128)(4,1)}), s8[4194304]{0:T(1024)(128)(4,1)S(1)}, s32[]{:S(2)}) async-start(s8[4718592]{0:T(1024)(128)(4,1)} %bitcast.25), calls=%async_computation.6 | async-start | bytes 8388608
  425.3 4.1 slice-start.1
Sparse Core Ops, SparseCore 0:
  166.5 251.2 all-reduce.5
  423.6 127.6 all-reduce.3

commit v2 on v1

v2 whole, which is shorter than its diff:
```python
import functools
import jax
import jax.numpy as jnp
from jax import lax
from jax.experimental import pallas as pl
from jax.experimental.pallas import tpu as pltpu
from jax.sharding import PartitionSpec as P

MESH = pl.DeviceIdType.MESH
BF = jnp.bfloat16
F32 = jnp.float32
EPS = 1e-5
D = 768
HD = 64
NH = 12
FF = 3072
BUCKETS = 16384
LANE = 128
MIB = 1 << 20


def dot_nn(a, b):
    return lax.dot_general(a, b, (((1,), (0,)), ((), ())), preferred_element_type=F32)


def dot_nt(a, b):
    return lax.dot_general(a, b, (((1,), (1,)), ((), ())), preferred_element_type=F32)


def dot_tn(a, b):
    return lax.dot_general(a, b, (((0,), (0,)), ((), ())), preferred_element_type=F32)


def norm_parts(x):
    mean = jnp.mean(x, -1, keepdims=True)
    cen = x - mean
    var = jnp.mean(cen * cen, -1, keepdims=True)
    rstd = lax.rsqrt(var + EPS)
    return cen * rstd, rstd


def norm_back(xhat, rstd, gain, dy):
    dxh = dy * gain
    m1 = jnp.mean(dxh, -1, keepdims=True)
    m2 = jnp.mean(dxh * xhat, -1, keepdims=True)
    return rstd * (dxh - m1 - xhat * m2)


def lane_half(shape, half):
    lane = lax.broadcasted_iota(jnp.int32, shape, 1)
    return (lane < HD) if half == 0 else (lane >= HD)


def fwd_kernel(x_ref, g1_ref, b1_ref, wqkv_ref, qb_ref, wout_ref, ob_ref, qkv_ref, lse_ref, ctx_ref, mid_ref, lacc):
    length = x_ref.shape[0]
    x = x_ref[...].astype(F32)
    xhat, _ = norm_parts(x)
    a1 = (xhat * g1_ref[...] + b1_ref[...]).astype(BF)
    for j in range(3):
        c = slice(j * D, (j + 1) * D)
        qkv_ref[:, c] = (dot_nn(a1, wqkv_ref[:, c]) + qb_ref[:, c]).astype(BF)

    def pair(p, carry):
        at = pl.multiple_of(p * LANE, LANE)
        q = qkv_ref[:, pl.ds(at, LANE)] * BF(0.125)
        k = qkv_ref[:, pl.ds(pl.multiple_of(D + at, LANE), LANE)]
        v = qkv_ref[:, pl.ds(pl.multiple_of(2 * D + at, LANE), LANE)]
        outs = []
        lse = lacc[...]
        lane = lax.broadcasted_iota(jnp.int32, lse.shape, 1)
        for half in range(2):
            qm = jnp.where(lane_half(q.shape, half), q, BF(0))
            s = dot_nt(qm, k)
            m = jnp.max(s, -1, keepdims=True)
            e = jnp.exp(s - m)
            t = jnp.sum(e, -1, keepdims=True)
            pr = (e * (1.0 / t)).astype(BF)
            outs.append(dot_nn(pr, v))
            lse = jnp.where(lane == 2 * p + half, m + jnp.log(t), lse)
        lacc[...] = lse
        ctx_ref[:, pl.ds(at, LANE)] = jnp.where(lane_half(outs[0].shape, 0), outs[0], outs[1]).astype(BF)
        return carry

    lacc[...] = jnp.zeros_like(lacc)
    lax.fori_loop(0, NH // 2, pair, 0)
    lt = lacc[...].T
    for h in range(NH):
        lse_ref[h] = lt[h : h + 1, :]
    mid_ref[...] = x + (dot_nn(ctx_ref[...], wout_ref[...]) + ob_ref[...])


def forward(x, g1, b1, wqkv, qb, wout, ob, length):
    tokens = x.shape[0]
    rows = tokens // length
    whole = lambda a: pl.BlockSpec(a.shape, lambda i: (0,) * a.ndim)
    return pl.pallas_call(
        fwd_kernel,
        grid=(rows,),
        in_specs=[pl.BlockSpec((length, D), lambda i: (i, 0))] + [whole(a) for a in (g1, b1, wqkv, qb, wout, ob)],
        out_specs=[
            pl.BlockSpec((length, 3 * D), lambda i: (i, 0)),
            pl.BlockSpec((NH, 1, length), lambda i: (i, 0, 0)),
            pl.BlockSpec((length, D), lambda i: (i, 0)),
            pl.BlockSpec((length, D), lambda i: (i, 0)),
        ],
        out_shape=[
            jax.ShapeDtypeStruct((tokens, 3 * D), BF),
            jax.ShapeDtypeStruct((rows * NH, 1, length), F32),
            jax.ShapeDtypeStruct((tokens, D), BF),
            jax.ShapeDtypeStruct((tokens, D), F32),
        ],
        scratch_shapes=[pltpu.VMEM((length, LANE), F32)],
        compiler_params=pltpu.CompilerParams(vmem_limit_bytes=58 * MIB),
        name="attn_forward",
    )(x, g1, b1, wqkv, qb, wout, ob)


def count_kernel(ids_ref, out_ref):
    hashes, rows, chars = ids_ref.shape
    high = BUCKETS // LANE

    def one(h, carry):
        total = jnp.zeros((high, LANE), F32)
        for r in range(rows):
            ids = ids_ref[h, r : r + 1, :]
            row = lax.broadcasted_iota(jnp.int32, (high, chars), 0)
            hi = jnp.where(row == (ids >> 7), 1.0, 0.0).astype(BF)
            lo = jnp.where(row == (ids & (LANE - 1)), 1.0, 0.0).astype(BF)
            total = total + dot_nt(hi, lo)
        out_ref[h] = total.astype(jnp.int32)
        return carry

    lax.fori_loop(0, hashes, one, 0)


def count(ids):
    return pl.pallas_call(
        count_kernel,
        in_specs=[pl.BlockSpec(memory_space=pltpu.VMEM)],
        out_specs=pl.BlockSpec(memory_space=pltpu.VMEM),
        out_shape=jax.ShapeDtypeStruct((ids.shape[0], BUCKETS // LANE, LANE), jnp.int32),
        compiler_params=pltpu.CompilerParams(vmem_limit_bytes=32 * MIB),
        name="bucket_tally",
    )(ids)


NB = 4
NFF = FF // (NB * LANE)
NPAIR = NFF + 3


def spots():
    return lax.axis_index("rows"), lax.axis_index("seq")


def bit_of(step):
    axis, mask = step
    return (lax.axis_index(axis) // mask) % 2


def across(step):
    axis, mask = step
    rows, seq = spots()
    move = mask - 2 * mask * bit_of(step)
    return (rows + move, seq) if axis == "rows" else (rows, seq + move)


def orders(shape):
    seq = [("seq", 1 << b) for b in range(shape["seq"].bit_length() - 1)]
    row = [("rows", 1 << b) for b in range(shape["rows"].bit_length() - 1)]
    return [seq + row, seq[:1] + row[:1] + seq[1:] + row[1:]]


class Halving:
    def __init__(self, order, lead, rows, tile):
        self.order, self.tile = order, tile
        self.size, self.split, self.lead_at, self.row_at, self.own = [], [], [], [], []
        lead_at, row_at = 0, 0
        for i, step in enumerate(order):
            bit = bit_of(step)
            if lead > 1:
                lead //= 2
                how = 0
                if i == 0:
                    self.first = bit * lead
                else:
                    lead_at = lead_at + bit * lead
            elif rows % (2 * tile) == 0:
                rows //= 2
                how = 1
                row_at = row_at + bit * rows
            else:
                how = None
            self.own.append(bit)
            self.split.append(how)
            self.size.append((lead, rows))
            self.lead_at.append(lead_at)
            self.row_at.append(row_at)
        self.gathers = [i for i in reversed(range(len(order))) if self.split[i] is not None]

    def rows_of(self, at, size):
        return pl.ds(pl.multiple_of(at, self.tile), size)

    def send(self, i, mine, land, sems):
        step, (lead, rows) = self.order[i], self.size[i]
        if i == 0:
            src = mine.at[pl.ds(lead - self.first, lead)]
        else:
            la, ra = self.lead_at[i - 1], self.row_at[i - 1]
            if self.split[i] == 0:
                la = la + (1 - self.own[i]) * lead
            elif self.split[i] == 1:
                ra = ra + (1 - self.own[i]) * rows
            src = land[0].at[pl.ds(la, lead), self.rows_of(ra, rows)]
        return pltpu.make_async_remote_copy(src_ref=src, dst_ref=land[i], send_sem=sems[0].at[i], recv_sem=sems[1].at[i],
                                            device_id=across(step), device_id_type=MESH)

    def add(self, i, mine, land):
        lead, rows = self.size[i]
        part = rows if rows <= LANE else 96
        wide = F32 if land[0].dtype == BF else land[0].dtype

        def some(t, carry):
            at = t * part
            if i == 0:
                here = (slice(None), self.rows_of(at, part))
                left, right = land[0][here], mine[pl.ds(self.first, lead), self.rows_of(at, part)]
            else:
                here = (pl.ds(self.lead_at[i], lead), self.rows_of(self.row_at[i] + at, part))
                left, right = land[0][here], land[i][:, self.rows_of(at, part)]
            land[0][here] = (left.astype(wide) + right.astype(wide)).astype(land[0].dtype)
            return carry

        lax.fori_loop(0, rows // part, some, 0)

    def at_level(self, i):
        lead, rows = self.size[i]
        return pl.ds(self.lead_at[i], lead), self.rows_of(self.row_at[i], rows)

    def out_level(self, i):
        lead, rows = self.size[i]
        return pl.ds(self.first + self.lead_at[i], lead), self.rows_of(self.row_at[i], rows)

    def keep(self, land, out, sem):
        last = len(self.order) - 1
        return pltpu.make_async_copy(land[0].at[self.at_level(last)], out.at[self.out_level(last)], sem)

    def gather(self, m, land, out, sems):
        i = self.gathers[m]
        here = out.at[self.out_level(i)]
        src = land[0].at[self.at_level(len(self.order) - 1)] if m == 0 else here
        return pltpu.make_async_remote_copy(src_ref=src, dst_ref=here, send_sem=sems[0].at[m], recv_sem=sems[1].at[m],
                                            device_id=across(self.order[i]), device_id_type=MESH)

    def reduce_step(self, k, mine, land, sems):
        n = len(self.order)
        if k > 0:
            self.send(k - 1, mine, land, sems).wait()
            self.add(k - 1, mine, land)
        if k < n:
            self.send(k, mine, land, sems).start()

    def gather_step(self, m, land, out, sems, sem):
        if m == 0:
            self.keep(land, out, sem).start()
        else:
            if m == 1:
                self.keep(land, out, sem).wait()
            self.gather(m - 1, land, out, sems).wait()
        if m < len(self.gathers):
            self.gather(m, land, out, sems).start()


def land_shapes(count, lead, rows, tile, steps, dtype):
    shapes = []
    for _ in range(steps):
        if lead > 1:
            lead //= 2
        elif rows % (2 * tile) == 0:
            rows //= 2
        shapes.append(pltpu.VMEM(count + (lead, rows, LANE), dtype))
    return shapes


AG_AT = (8, 13, 18, 22, 23, 24, 25, 27, 28)


def rear_kernel(shape, length, mid_h, dy_h, x_h, qkv_h, ctx_h, wup_h, wdn_h, wqkv_h, wout_h, lse_ref, cnt_ref,
                g1_ref, b1_ref, g2_ref, b2_ref, ub_ref, db_ref,
                lo_out, gm_out, sum_out, cnt_out, vec_out,
                mid_s, dy_s, a2_s, a2t_s, dyt_s, acc_s, da2_s, wup_s, wdn_s, qkv_s, ctx_s, x_s, wqkv_s, wout_s,
                dqkv_s, gout_s, lo_s, vec_s, gub_s, part_s, fetch_sem, stage_s, vland_s, vacc_s,
                rs_send, rs_recv, ag_send, ag_recv, keep_sem, crs_send, crs_recv, cag_send, cag_recv, ckeep_sem,
                v_send, v_recv, t_send, t_recv, t_own, *lands):
    both = orders(shape)
    nd = len(both[0])
    nseq = shape["seq"]
    land = lands[:nd]
    cland = lands[nd:]
    rows_idx, me = spots()
    tokens = mid_s.shape[0]
    rows = tokens // length
    local = length // nseq
    fc = NB * LANE

    barrier = pltpu.get_barrier_semaphore()
    others = [across(step) for step in both[0]]
    for m in range(3, nseq):
        if m & (m - 1):
            others.append((rows_idx, sum(((me // (1 << b)) % 2 + ((m >> b) & 1) * (1 - 2 * ((me // (1 << b)) % 2))) * (1 << b)
                                         for b in range(nseq.bit_length() - 1))))
    for other in others:
        pl.semaphore_signal(barrier, inc=1, device_id=other, device_id_type=MESH)

    def fetch(t):
        return pltpu.make_async_copy((mid_h, dy_h, x_h, qkv_h, ctx_h, wqkv_h, wout_h)[t],
                                     (mid_s, dy_s, x_s, qkv_s, ctx_s, wqkv_s, wout_s)[t], fetch_sem.at[t])

    def weights(i, slot):
        return (pltpu.make_async_copy(wup_h.at[:, pl.ds(pl.multiple_of(i * fc, fc), fc)], wup_s.at[slot], fetch_sem.at[8 + slot]),
                pltpu.make_async_copy(wdn_h.at[pl.ds(pl.multiple_of(i * fc, fc), fc)], wdn_s.at[slot], fetch_sem.at[10 + slot]))

    fetch(0).start()
    fetch(1).start()
    for copy in weights(0, 0):
        copy.start()
    pl.semaphore_wait(barrier, len(others))

    plans = [Halving(order, NB, D, 16) for order in both]
    tally = Halving(both[1], cnt_ref.shape[0], cnt_ref.shape[1], 8)
    in_at = list(range(NFF)) + [NFF + 5, NFF + 10, NFF + 15]
    out_at = [max(a, b + nd) for a, b in zip(AG_AT, in_at)]
    last_tick = NFF + 16

    def tick(t):
        for k in reversed(range(nd + 1)):
            hit = sum(jnp.where(t == in_at[j] + k, 1, 0) for j in range(NPAIR))
            j = sum(jnp.where(t == in_at[j] + k, j, 0) for j in range(NPAIR))

            @pl.when(hit == 1)
            def _():
                for o, plan in enumerate(plans):
                    plan.reduce_step(k, stage_s.at[j % 2, o], [r.at[j, o] for r in land], (rs_send.at[j, o], rs_recv.at[j, o]))

        most = max(len(plan.gathers) for plan in plans)
        for m in reversed(range(most + 1)):
            hit = sum(jnp.where(t == out_at[j] + m, 1, 0) for j in range(NPAIR))
            j = sum(jnp.where(t == out_at[j] + m, j, 0) for j in range(NPAIR))

            @pl.when(hit == 1)
            def _():
                for o, plan in enumerate(plans):
                    plan.gather_step(m, [r.at[j, o] for r in land], sum_out.at[j, o], (ag_send.at[j, o], ag_recv.at[j, o]),
                                     keep_sem.at[j, o])

    def tick_counts(t):
        for k in range(nd + 1):

            @pl.when(t == k)
            def _():
                tally.reduce_step(k, cnt_ref, cland, (crs_send, crs_recv))

        for m in range(len(tally.gathers) + 1):

            @pl.when(t == nd + 1 + m)
            def _():
                tally.gather_step(m, cland, cnt_out, (cag_send, cag_recv), ckeep_sem)

    def give_back(which, out):
        copies = []
        for m in range(1, nseq):
            bits = [(me // (1 << b)) % 2 for b in range(nseq.bit_length() - 1)]
            to = sum((bit + ((m >> b) & 1) * (1 - 2 * bit)) * (1 << b) for b, bit in enumerate(bits))
            copies.append(pltpu.make_async_remote_copy(
                src_ref=lo_s.at[:, pl.ds(pl.multiple_of(to * local, local), local)], dst_ref=out.at[pl.ds(me * rows, rows)],
                send_sem=t_send.at[which, m], recv_sem=t_recv.at[which, m], device_id=(rows_idx, to), device_id_type=MESH))
        copies.append(pltpu.make_async_copy(lo_s.at[:, pl.ds(pl.multiple_of(me * local, local), local)],
                                            out.at[pl.ds(me * rows, rows)], t_own.at[which]))
        return copies

    step = 256
    pieces = tokens // step
    fetch(0).wait()
    fetch(1).wait()
    for t in (6, 4, 2, 3, 5):
        fetch(t).start()

    def open_piece(n, carry):
        at = pl.ds(pl.multiple_of(n * step, step), step)
        mid = mid_s[at]
        xhat, _ = norm_parts(mid)
        a2 = (xhat * g2_ref[...] + b2_ref[...]).astype(BF)
        a2_s[at] = a2
        a2t_s[:, at] = a2.T
        dyt_s[:, at] = dy_s[at].T
        acc_s[at] = mid + db_ref[...]
        da2_s[at] = jnp.zeros((step, D), F32)
        return carry

    lax.fori_loop(0, pieces, open_piece, 0)

    def ff(i, carry):
        slot = i % 2

        @pl.when(i + 1 < NFF)
        def _():
            for copy in weights(i + 1, 1 - slot):
                copy.start()

        for copy in weights(i, slot):
            copy.wait()
        cols = pl.ds(pl.multiple_of(i * fc, fc), fc)
        u = dot_nn(a2_s[...], wup_s[slot]) + ub_ref[:, cols]
        dh = dot_nt(dy_s[...], wdn_s[slot])
        cdf = 0.5 + 0.5 * lax.erf(u * (2.0 ** -0.5))
        pdf = jnp.exp(u * u * -0.5) * 0.3989422804014327
        hid = (u * cdf).astype(BF)
        du = (dh * (cdf + u * pdf)).astype(BF)
        gub_s[:, cols] = jnp.sum(du.astype(F32), 0, keepdims=True)
        acc_s[...] += dot_nn(hid, wdn_s[slot])
        da2_s[...] += dot_nt(du, wup_s[slot])
        gd = dot_nn(dyt_s[...], hid).astype(BF)
        gu = dot_nn(a2t_s[...], du).astype(BF)
        for b in range(NB):
            stage_s[slot, 0, b] = gd[:, b * LANE : (b + 1) * LANE]
            stage_s[slot, 1, b] = gu[:, b * LANE : (b + 1) * LANE]
        tick(i)
        tick_counts(i)
        return carry

    lax.fori_loop(0, NFF, ff, 0)

    part_s[...] = jnp.zeros_like(part_s)
    fetch(6).wait()

    def turn_piece(n, carry):
        at = pl.ds(pl.multiple_of(n * step, step), step)
        lo_s[n * step // length, pl.ds(pl.multiple_of((n * step) % length, step), step)] = acc_s[at].astype(BF)
        dy = dy_s[at].astype(F32)
        xhat, rstd = norm_parts(mid_s[at])
        da2 = da2_s[at]
        dx2 = dy + norm_back(xhat, rstd, g2_ref[...], da2)
        da2_s[at] = dx2
        do = dx2.astype(BF)
        a2_s[at] = do
        part_s[0:1] += jnp.sum(dy, 0, keepdims=True)
        part_s[1:2] += jnp.sum(da2 * xhat, 0, keepdims=True)
        part_s[2:3] += jnp.sum(da2, 0, keepdims=True)
        part_s[3:4] += jnp.sum(do.astype(F32), 0, keepdims=True)
        dy_s[at] = dot_nt(do, wout_s[...]).astype(BF)
        return carry

    lax.fori_loop(0, pieces, turn_piece, 0)
    dctx_s, do_s, dx2_s, da1_s, a1t_s = dy_s, a2_s, da2_s, acc_s, a2t_s
    for copy in give_back(0, lo_out):
        copy.start()
    fetch(4).wait()
    fetch(2).wait()
    gout = dot_tn(ctx_s[...], do_s[...]).astype(BF)
    for b in range(D // LANE):
        gout_s[b] = gout[:, b * LANE : (b + 1) * LANE]

    def first_norm(n, carry):
        at = pl.ds(pl.multiple_of(n * step, step), step)
        xhat, _ = norm_parts(x_s[at].astype(F32))
        a1t_s[:, at] = (xhat * g1_ref[...] + b1_ref[...]).astype(BF).T
        da1_s[at] = jnp.zeros((step, D), F32)
        return carry

    lax.fori_loop(0, pieces, first_norm, 0)
    fetch(3).wait()
    fetch(5).wait()
    tick(NFF)
    tick_counts(NFF)

    def group(g, carry):
        def unit(n, inner_carry):
            r = n // 2
            h = n % 2
            p = 2 * g + h
            tok = pl.ds(pl.multiple_of(r * length, length), length)
            cq = pl.ds(pl.multiple_of(p * LANE, LANE), LANE)
            q = qkv_s[tok, cq] * BF(0.125)
            k = qkv_s[tok, pl.ds(pl.multiple_of(p * LANE + D, LANE), LANE)]
            v = qkv_s[tok, pl.ds(pl.multiple_of(p * LANE + 2 * D, LANE), LANE)]
            dc = dctx_s[tok, cq]
            dqs, dks, dvs = [], [], []
            for half in range(2):
                keep = lane_half(k.shape, half)
                km = jnp.where(keep, k, BF(0))
                vm = jnp.where(keep, v, BF(0))
                lse = lse_ref[r * NH + 2 * p + half]
                st = dot_nt(km, q)
                pt = jnp.exp(st - lse)
                dpt = dot_nt(vm, dc)
                inner = jnp.sum(pt * dpt, 0, keepdims=True)
                dst = (pt * (dpt - inner)).astype(BF)
                dvs.append(dot_nn(pt.astype(BF), dc))
                dks.append(dot_nn(dst, q))
                dqs.append(dot_tn(dst, k))
            sel = lane_half(dqs[0].shape, 0)
            dqkv_s[tok, pl.ds(pl.multiple_of(h * LANE, LANE), LANE)] = (jnp.where(sel, dqs[0], dqs[1]) * 0.125).astype(BF)
            dqkv_s[tok, pl.ds(pl.multiple_of(h * LANE + 2 * LANE, LANE), LANE)] = jnp.where(sel, dks[0], dks[1]).astype(BF)
            dqkv_s[tok, pl.ds(pl.multiple_of(h * LANE + 4 * LANE, LANE), LANE)] = jnp.where(sel, dvs[0], dvs[1]).astype(BF)
            tick(NFF + 1 + 5 * g + n)
            tick_counts(NFF + 1 + 5 * g + n)
            return inner_carry

        lax.fori_loop(0, 4, unit, 0)
        slot = (NFF + g) % 2
        grads = dot_nn(a1t_s[...], dqkv_s[...]).astype(BF)
        for b in range(6):
            stage_s[slot, b // NB, b % NB] = grads[:, b * LANE : (b + 1) * LANE]
        for b in range(2):
            stage_s[slot, 1, 2 + b] = gout_s[2 * g + b]
        two = 2 * LANE
        for c in range(3):
            at = pl.ds(pl.multiple_of(c * D + g * two, two), two)
            da1_s[...] += dot_nt(dqkv_s[:, c * two : (c + 1) * two], wqkv_s[:, at])
        here = pl.ds(pl.multiple_of(g * two, two), two)
        part_s[6:7, here] = jnp.sum(dqkv_s[:, 0:two].astype(F32), 0, keepdims=True)
        part_s[7:8, here] = jnp.sum(dqkv_s[:, 2 * two : 3 * two].astype(F32), 0, keepdims=True)
        tick(NFF + 5 + 5 * g)
        tick_counts(NFF + 5 + 5 * g)
        return carry

    lax.fori_loop(0, 3, group, 0)

    for copy in give_back(0, lo_out):
        copy.wait()

    def last_piece(n, carry):
        at = pl.ds(pl.multiple_of(n * step, step), step)
        xhat, rstd = norm_parts(x_s[at].astype(F32))
        da1 = da1_s[at]
        part_s[4:5] += jnp.sum(da1 * xhat, 0, keepdims=True)
        part_s[5:6] += jnp.sum(da1, 0, keepdims=True)
        gm = dx2_s[at] + norm_back(xhat, rstd, g1_ref[...], da1)
        lo_s[n * step // length, pl.ds(pl.multiple_of((n * step) % length, step), step)] = gm.astype(BF)
        return carry

    lax.fori_loop(0, pieces, last_piece, 0)
    for copy in give_back(1, gm_out):
        copy.start()
    vacc_s[0, 0:8] = part_s[...]
    for b in range(FF // (2 * LANE)):
        vacc_s[0, 8 + b // 3 : 9 + b // 3, (b % 3) * 2 * LANE : (b % 3 + 1) * 2 * LANE] = gub_s[:, b * 2 * LANE : (b + 1) * 2 * LANE]
    vacc_s[0, 12:16] = jnp.zeros((4, D), F32)

    def swap(i):
        return pltpu.make_async_remote_copy(src_ref=vacc_s.at[i], dst_ref=vland_s.at[i], send_sem=v_send.at[i], recv_sem=v_recv.at[i],
                                            device_id=across(both[0][i]), device_id_type=MESH)

    def drain(t, carry):
        for i in range(nd + 1):

            @pl.when(t == last_tick + i)
            def _():
                if i > 0:
                    swap(i - 1).wait()
                    vacc_s[i] = vacc_s[i - 1] + vland_s[i - 1]
                if i < nd:
                    swap(i).start()

        tick(t)
        return carry

    end = max(max(out_at) + max(len(plan.gathers) for plan in plans), last_tick + nd) + 1
    lax.fori_loop(last_tick, end, drain, 0)
    vec_out[...] = vacc_s[nd]
    for copy in give_back(1, gm_out):
        copy.wait()


def rear(shape, length, mid, dy, x, qkv, ctx, wup, wdn, wqkv, wout, lse, cnt, g1, b1, g2, b2, ub, db):
    tokens = mid.shape[0]
    nseq = shape["seq"]
    rows = tokens // length
    nd = len(orders(shape)[0])
    vm, hb = pl.BlockSpec(memory_space=pltpu.VMEM), pl.BlockSpec(memory_space=pl.ANY)
    dma = pltpu.SemaphoreType.DMA
    V = pltpu.VMEM
    fc = NB * LANE
    scratch = [
        V((tokens, D), F32), V((tokens, D), BF), V((tokens, D), BF), V((D, tokens), BF), V((D, tokens), BF), V((tokens, D), F32),
        V((tokens, D), F32), V((2, D, fc), BF), V((2, fc, D), BF), V((tokens, 3 * D), BF), V((tokens, D), BF), V((tokens, D), BF),
        V((D, 3 * D), BF), V((D, D), BF), V((tokens, D), BF), V((D // LANE, D, LANE), BF), V((rows, length, D), BF), V((8, D), F32),
        V((1, FF), F32), V((8, D), F32), dma((12,)), V((2, 2, NB, D, LANE), BF), V((nd, 16, D), F32), V((nd + 1, 16, D), F32),
        dma((NPAIR, 2, nd)), dma((NPAIR, 2, nd)), dma((NPAIR, 2, nd)), dma((NPAIR, 2, nd)), dma((NPAIR, 2)),
        dma((nd,)), dma((nd,)), dma((nd,)), dma((nd,)), dma, dma((nd,)), dma((nd,)), dma((2, nseq)), dma((2, nseq)), dma((2,)),
    ]
    scratch += land_shapes((NPAIR, 2), NB, D, 16, nd, BF)
    scratch += land_shapes((), cnt.shape[0], cnt.shape[1], 8, nd, jnp.int32)
    local = length // nseq
    return pl.pallas_call(
        functools.partial(rear_kernel, shape, length),
        in_specs=[hb] * 9 + [vm] * 8,
        out_specs=[hb, hb, hb, hb, vm],
        out_shape=[jax.ShapeDtypeStruct((rows * nseq, local, D), BF), jax.ShapeDtypeStruct((rows * nseq, local, D), BF),
                   jax.ShapeDtypeStruct((NPAIR, 2, NB, D, LANE), BF), jax.ShapeDtypeStruct(cnt.shape, jnp.int32),
                   jax.ShapeDtypeStruct((16, D), F32)],
        scratch_shapes=scratch,
        compiler_params=pltpu.CompilerParams(vmem_limit_bytes=63 * MIB, collective_id=0, has_side_effects=True),
        name="rear",
    )(mid, dy, x, qkv, ctx, wup, wdn, wqkv, wout, lse, cnt, g1, b1, g2, b2, ub, db)


def widen_kernel(turned, src_ref, out_ref):
    for j in range(src_ref.shape[0]):
        at = slice(j * LANE, (j + 1) * LANE)
        if turned:
            out_ref[at, :] = src_ref[j].astype(F32).T
        else:
            out_ref[:, at] = src_ref[j].astype(F32)


def widen(blocks, number, group, where, turned=False):
    wide = group * LANE
    return pl.pallas_call(
        functools.partial(widen_kernel, turned),
        grid=(number,),
        in_specs=[pl.BlockSpec((group, D, LANE), lambda i: (where(i), 0, 0))],
        out_specs=pl.BlockSpec((wide, D), lambda i: (i, 0)) if turned else pl.BlockSpec((D, wide), lambda i: (0, i)),
        out_shape=jax.ShapeDtypeStruct((number * wide, D) if turned else (D, number * wide), F32),
        compiler_params=pltpu.CompilerParams(vmem_limit_bytes=32 * MIB),
        name="widen",
    )(blocks)


def on_device(shape, molecules, ln1_gain, ln1_bias, w_qkv, qkv_bias, w_out, out_bias, ln2_gain, ln2_bias, w_up, up_bias,
              w_down, down_bias, out_cotangent, bucket_ids):
    rows_here, local_len, width = molecules.shape
    length = local_len * shape["seq"]
    row = lambda a: a.reshape(1, -1)
    tally = count(bucket_ids)
    x = lax.all_to_all(molecules, "seq", split_axis=0, concat_axis=1, tiled=True).reshape(-1, width)
    dy = lax.all_to_all(out_cotangent, "seq", split_axis=0, concat_axis=1, tiled=True).reshape(-1, width)
    qb = jnp.concatenate([qkv_bias[0], jnp.zeros((width,), F32), qkv_bias[1]]).reshape(1, -1)
    qkv, lse, ctx, mid = forward(x, row(ln1_gain), row(ln1_bias), w_qkv, qb, w_out, row(out_bias), length)
    layer_out, gm, sums, counts, vec = rear(
        shape, length, mid, dy, x, qkv, ctx, w_up, w_down, w_qkv, w_out, lse, tally, row(ln1_gain), row(ln1_bias),
        row(ln2_gain), row(ln2_bias), row(up_bias), row(down_bias))
    blocks = sums.reshape(-1, D, LANE)
    g_qkv = widen(blocks, 9, 2, lambda i: (NFF + i % 3) * NB + i // 3)
    g_out = widen(blocks, 3, 2, lambda i: (NFF + i) * NB + 3)
    g_up = widen(blocks, NFF, NB, lambda i: 2 * i + 1)
    g_down = widen(blocks, NFF, NB, lambda i: 2 * i, True)
    return (layer_out, gm.astype(F32), vec[4], vec[5], g_qkv, vec[6:8], g_out, vec[3], vec[1], vec[2],
            g_up, vec[8:12].reshape(-1), g_down, vec[0], counts.reshape(bucket_ids.shape[0], BUCKETS))


def solution(mesh):
    tok = P("rows", "seq", None)
    return jax.shard_map(
        functools.partial(on_device, dict(mesh.shape)),
        mesh=mesh,
        in_specs=(tok,) + (P(),) * 12 + (tok, P(None, "rows", "seq")),
        out_specs=(tok, tok) + (P(),) * 13,
        check_vma=False,
    )
```

time: 561 us -> 335 us (0.60)
  waiting for transfers between devices: 299 us -> 10.1 us
  Pallas kernels: 127 us -> 277 us
  blocking collectives: 83.2 us -> 24.3 us
  between operations: 14.3 us -> 0.77 us
  local copies, waits for them, and re-layouts: 24.1 us -> 16.6 us
  starting transfers between devices: 11.2 us -> 3.71 us
    psum x2 -> x0, waiting for transfers between devices: 255 us -> none  [the longest x1 138 us: on_device(): gd, gu, gr = lax.psum((gd, gu, gr), ('rows', 'seq'))]
    pallas_call x6 -> x5, Pallas kernels: 97.5 us -> 247 us  [the longest x1 231 us: rear(): pl.pallas_call(functools.partial(rear_kernel, shape, length), in_specs=[h...]
    psum x1 -> x0, blocking collectives: 58.8 us -> none  [on_device(): lax.psum(jnp.concatenate([vec2.reshape(-1), vec1.reshape(-1), gub.reshape...]
    all_to_all x2 -> x0, waiting for transfers between devices: 29 us -> none  [on_device(): lax.all_to_all(a.reshape(-1, length, width), 'seq', split_axis=1, concat_...]
    all_to_all x2 -> x0, starting transfers between devices: 7.55 us -> none  [on_device(): lax.all_to_all(a.reshape(-1, length, width), 'seq', split_axis=1, concat_...]
  transfers between devices with their start and end apart: 5 -> 1, of which waited for: 4 -> 1; matrix products, arithmetic and copies ran while one was open for 3% -> 2% of each run, Pallas kernels for 3% -> 1%
where the time goes in v2:
time: 335 us; the launch traced here: 334 us
  Pallas kernels  277 us (83%)
  blocking collectives  24.3 us (7%)
  local copies, waits for them, and re-layouts  16.6 us (5%)
  waiting for transfers between devices  10.1 us (3%)
  starting transfers between devices  3.71 us (1%)
    pallas_call x1, Pallas kernels, rear(): pl.pallas_call(functools.partial(rear_kernel, shape, length), in_specs=[h...  231 us
    pallas_call x1, Pallas kernels, forward(): pl.pallas_call(fwd_kernel, grid=(rows,), in_specs=[pl.BlockSpec((length,...  26 us
    all_to_all x1, blocking collectives, on_device(): lax.all_to_all(molecules, 'seq', split_axis=0, concat_axis=1, tiled=True)  24.3 us
    pallas_call x4, Pallas kernels, widen(): pl.pallas_call(functools.partial(widen_kernel, turned), grid=(number,), i...  15.9 us
    all_to_all x1, waiting for transfers between devices, on_device(): lax.all_to_all(out_cotangent, 'seq', split_axis=0, concat_axis=1, tiled=T...  10.1 us
    unnamed x30, local copies, waits for them, and re-layouts  8.1 us
  transfers between devices with their start and end apart: 1, of which 1 were waited for; matrix products, arithmetic and copies ran while one was open for 2% of the time, Pallas kernels for 1%

profile of v2, /device:TPU:0, one launch (start us, length us, event | category | flops | bytes accessed | tf_op | source)
XLA Modules:
  0.0 334.4 jit_solution(3760749819540062289)
XLA Ops:
  0.6 24.3 %all_to_all.30 = bf16[8,128,768]{2,1,0:T(8,128)(2,1)S(1)} all-to-all(bf16[8,128,768]{2,1,0:T(8,128)(2,1)} %param.15), channel_id=1, replica_groups=mesh['rows'=8,'seq'=4] {'seq'}, dimensions={0} | all-to-all | bytes 3145728 | tf_op jit(solution)/shard_map/all_to_all | solution.py:636
  24.9 0.0 copy-start.7
  24.9 0.0 copy-start.8
  24.9 0.0 copy-start.9
  25.0 0.0 copy-start.2
  25.0 0.0 copy-start.11
  25.0 0.0 copy-start.12
  25.0 0.0 copy-start.13
  25.0 3.7 %all-to-all-start.1 = ((bf16[8,128,768]{2,1,0:T(8,128)(2,1)}), bf16[8,128,768]{2,1,0:T(8,128)(2,1)S(1)}, u32[]{:S(2)}, u32[]{:S(2)}) async-start(bf16[8,128,768]{2,1,0:T(8,128)(2,1)} %param.28), calls=%async_computation.1 | async-start | bytes 3145728 | tf_op jit(solution)/shard_map/all_to_all | solution.py:637
  28.7 0.0 copy-done.7
  28.8 0.6 reshape.76.qb_ref
  29.4 0.0 copy-done.8
  29.4 0.6 reshape.74.g1_ref
  30.0 0.0 copy-done.9
  30.0 0.6 reshape.75.b1_ref
  30.6 0.0 copy-done.10
  30.6 0.6 reshape.77.ob_ref
  31.1 0.0 copy-done.2
  31.1 3.7 %bucket_tally.1.cnt_ref = s32[8,128,128]{2,1,0:T(8,128)S(1)} custom-call(s32[8,8,512]{2,1,0:T(8,128)S(1)} %copy-done.2), custom_call_target="tpu_custom_call" | custom-call | tf_op jit(solution)/shard_map/bucket_tally/pallas_call | solution.py:137
  34.9 0.0 copy-start.1
  34.9 0.8 copy-done.1
  35.7 0.0 copy-done.11
  35.7 0.6 reshape.79.g2_ref
  36.2 0.0 copy-done.12
  36.2 0.6 reshape.80.b2_ref
  36.8 0.0 copy-done.13
  36.8 0.6 reshape.82.db_ref
  37.4 1.3 copy.30
  38.7 10.1 %all-to-all-done.1 = bf16[8,128,768]{2,1,0:T(8,128)(2,1)S(1)} async-done(((bf16[8,128,768]{2,1,0:T(8,128)(2,1)}), bf16[8,128,768]{2,1,0:T(8,128)(2,1)S(1)}, u32[]{:S(2)}, u32[]{:S(2)}) %all-to-all-start.1) | async-done | bytes 1572896 | tf_op jit(solution)/shard_map/all_to_all | solution.py:637
  48.8 1.3 copy.31
  50.0 26.0 %attn_forward.1 = (bf16[1024,2304]{1,0:T(8,128)(2,1)}, f32[24,1,512]{2,1,0:T(1,128)}, bf16[1024,768]{1,0:T(8,128)(2,1)}, f32[1024,768]{1,0:T(8,128)}) custom-call(bf16[1024,768]{1,0:T(8,128)(2,1)} %bitcast.18, f32[1,768]{1,0:T(1,128)} %reshape.74.g1_ref, f32[1,768]{1,0:T(1,128)} %reshape.75.b1_ref, bf16[768,2304]{1,0:T(8,128)(2,1)} %wqkv_h.1, ...), custom_call_target="tpu_custom_call" | custom-call | tf_op jit(solution)/shard_map/attn_forward/pallas_call | solution.py:96
  76.0 231.4 %rear.1 = (bf16[8,128,768]{2,1,0:T(8,128)(2,1)}, bf16[8,128,768]{2,1,0:T(8,128)(2,1)}, bf16[9,2,4,768,128]{4,3,2,1,0:T(8,128)(2,1)}, s32[8,128,128]{2,1,0:T(8,128)}, f32[16,768]{1,0:T(8,128)}) custom-call(f32[1024,768]{1,0:T(8,128)} %get-tuple-element.24.mid_h, bf16[1024,768]{1,0:T(8,128)(2,1)} %bitcast.22, bf16[1024,768]{1,0:T(8,128)(2,1)} %bitcast.19, ...), custom_call_target="tpu_custom_call" | custom-call | tf_op jit(solution)/shard_map/rear/pallas_call | solution.py:595
  307.4 0.0 copy-start
  307.4 5.0 %copy-done = bf16[9,2,4,768,128]{4,3,2,1,0:T(8,128)(2,1)S(1)} copy-done((bf16[9,2,4,768,128]{4,3,2,1,0:T(8,128)(2,1)S(1)}, bf16[9,2,4,768,128]{4,3,2,1,0:T(8,128)(2,1)}, u32[]{:S(2)}) %copy-start) | copy-done | bytes 14155800
  312.5 4.6 %widen.6 = f32[768,3072]{1,0:T(8,128)} custom-call(bf16[72,768,128]{2,1,0:T(8,128)(2,1)S(1)} %bitcast.14), custom_call_target="tpu_custom_call" | custom-call | tf_op jit(solution)/shard_map/widen/pallas_call | solution.py:619
  317.0 4.8 %widen.7 = f32[3072,768]{1,0:T(8,128)} custom-call(bf16[72,768,128]{2,1,0:T(8,128)(2,1)S(1)} %bitcast.15), custom_call_target="tpu_custom_call" | custom-call | tf_op jit(solution)/shard_map/widen/pallas_call | solution.py:619
  321.8 4.7 %widen.4 = f32[768,2304]{1,0:T(8,128)} custom-call(bf16[72,768,128]{2,1,0:T(8,128)(2,1)S(1)} %bitcast.16), custom_call_target="tpu_custom_call" | custom-call | tf_op jit(solution)/shard_map/widen/pallas_call | solution.py:619
  326.4 1.9 widen.5
  328.3 0.0 copy-done.6
  328.3 0.6 slice_reduce_fusion
  329.0 0.6 slice.34
  329.6 0.6 reshape.84
  330.2 0.0 copy-done.4
  330.2 1.9 convert_element_type.3
  332.1 0.0 copy-done.5
  332.1 1.1 copy.34
  333.2 0.0 copy-done.3
  333.2 1.1 copy.36
  (9 shorter events, 0.0 us)
Async XLA Ops:
  24.9 3.8 %copy-start.7 = (f32[2,768]{1,0:T(2,128)S(1)}, f32[2,768]{1,0:T(2,128)}, u32[]{:S(2)}) copy-start(f32[2,768]{1,0:T(2,128)} %param.19) | copy-start | bytes 18436
  24.9 4.4 %copy-start.8 = (f32[768]{0:T(1024)S(1)}, f32[768]{0:T(1024)}, u32[]{:S(2)}) copy-start(f32[768]{0:T(1024)} %param.16) | copy-start | bytes 9220
  24.9 5.0 %copy-start.9 = (f32[768]{0:T(1024)S(1)}, f32[768]{0:T(1024)}, u32[]{:S(2)}) copy-start(f32[768]{0:T(1024)} %param.17) | copy-start | bytes 9220
  25.0 5.6 %copy-start.10 = (f32[768]{0:T(1024)S(1)}, f32[768]{0:T(1024)}, u32[]{:S(2)}) copy-start(f32[768]{0:T(1024)} %param.21) | copy-start | bytes 9220
  25.0 6.2 %copy-start.2 = (s32[8,8,512]{2,1,0:T(8,128)S(1)}, s32[8,8,512]{2,1,0:T(8,128)}, u32[]{:S(2)}) copy-start(s32[8,8,512]{2,1,0:T(8,128)} %ids_ref.1) | copy-start | bytes 393220
  25.0 10.7 %copy-start.11 = (f32[768]{0:T(1024)S(1)}, f32[768]{0:T(1024)}, u32[]{:S(2)}) copy-start(f32[768]{0:T(1024)} %param.22) | copy-start | bytes 9220
  25.0 11.3 %copy-start.12 = (f32[768]{0:T(1024)S(1)}, f32[768]{0:T(1024)}, u32[]{:S(2)}) copy-start(f32[768]{0:T(1024)} %param.23) | copy-start | bytes 9220
  25.0 11.8 %copy-start.13 = (f32[768]{0:T(1024)S(1)}, f32[768]{0:T(1024)}, u32[]{:S(2)}) copy-start(f32[768]{0:T(1024)} %param.27) | copy-start | bytes 9220
  25.0 23.8 %all-to-all-start.1 = ((bf16[8,128,768]{2,1,0:T(8,128)(2,1)}), bf16[8,128,768]{2,1,0:T(8,128)(2,1)S(1)}, u32[]{:S(2)}, u32[]{:S(2)}) async-start(bf16[8,128,768]{2,1,0:T(8,128)(2,1)} %param.28), calls=%async_computation.1 | async-start | bytes 3145728 | tf_op jit(solution)/shard_map/all_to_all | solution.py:637
  34.9 0.8 copy-start.1
  307.4 5.0 %copy-start = (bf16[9,2,4,768,128]{4,3,2,1,0:T(8,128)(2,1)S(1)}, bf16[9,2,4,768,128]{4,3,2,1,0:T(8,128)(2,1)}, u32[]{:S(2)}) copy-start(bf16[9,2,4,768,128]{4,3,2,1,0:T(8,128)(2,1)} %get-tuple-element.31) | copy-start | bytes 42467332
  326.4 1.9 copy-start.6
  326.4 3.7 %copy-start.4 = (bf16[8,128,768]{2,1,0:T(8,128)(2,1)S(1)}, bf16[8,128,768]{2,1,0:T(8,128)(2,1)}, u32[]{:S(2)}) copy-start(bf16[8,128,768]{2,1,0:T(8,128)(2,1)} %get-tuple-element.29) | copy-start | bytes 4718596
  330.2 2.0 copy-start.5
  330.2 3.1 copy-start.3

commit v3 on v2

--- a/solution.py
+++ b/solution.py
@@ -51,99 +51,6 @@
     return (lane < HD) if half == 0 else (lane >= HD)
 
 
-def fwd_kernel(x_ref, g1_ref, b1_ref, wqkv_ref, qb_ref, wout_ref, ob_ref, qkv_ref, lse_ref, ctx_ref, mid_ref, lacc):
-    length = x_ref.shape[0]
-    x = x_ref[...].astype(F32)
-    xhat, _ = norm_parts(x)
-    a1 = (xhat * g1_ref[...] + b1_ref[...]).astype(BF)
-    for j in range(3):
-        c = slice(j * D, (j + 1) * D)
-        qkv_ref[:, c] = (dot_nn(a1, wqkv_ref[:, c]) + qb_ref[:, c]).astype(BF)
-
-    def pair(p, carry):
-        at = pl.multiple_of(p * LANE, LANE)
-        q = qkv_ref[:, pl.ds(at, LANE)] * BF(0.125)
-        k = qkv_ref[:, pl.ds(pl.multiple_of(D + at, LANE), LANE)]
-        v = qkv_ref[:, pl.ds(pl.multiple_of(2 * D + at, LANE), LANE)]
-        outs = []
-        lse = lacc[...]
-        lane = lax.broadcasted_iota(jnp.int32, lse.shape, 1)
-        for half in range(2):
-            qm = jnp.where(lane_half(q.shape, half), q, BF(0))
-            s = dot_nt(qm, k)
-            m = jnp.max(s, -1, keepdims=True)
-            e = jnp.exp(s - m)
-            t = jnp.sum(e, -1, keepdims=True)
-            pr = (e * (1.0 / t)).astype(BF)
-            outs.append(dot_nn(pr, v))
-            lse = jnp.where(lane == 2 * p + half, m + jnp.log(t), lse)
-        lacc[...] = lse
-        ctx_ref[:, pl.ds(at, LANE)] = jnp.where(lane_half(outs[0].shape, 0), outs[0], outs[1]).astype(BF)
-        return carry
-
-    lacc[...] = jnp.zeros_like(lacc)
-    lax.fori_loop(0, NH // 2, pair, 0)
-    lt = lacc[...].T
-    for h in range(NH):
-        lse_ref[h] = lt[h : h + 1, :]
-    mid_ref[...] = x + (dot_nn(ctx_ref[...], wout_ref[...]) + ob_ref[...])
-
-
-def forward(x, g1, b1, wqkv, qb, wout, ob, length):
-    tokens = x.shape[0]
-    rows = tokens // length
-    whole = lambda a: pl.BlockSpec(a.shape, lambda i: (0,) * a.ndim)
-    return pl.pallas_call(
-        fwd_kernel,
-        grid=(rows,),
-        in_specs=[pl.BlockSpec((length, D), lambda i: (i, 0))] + [whole(a) for a in (g1, b1, wqkv, qb, wout, ob)],
-        out_specs=[
-            pl.BlockSpec((length, 3 * D), lambda i: (i, 0)),
-            pl.BlockSpec((NH, 1, length), lambda i: (i, 0, 0)),
-            pl.BlockSpec((length, D), lambda i: (i, 0)),
-            pl.BlockSpec((length, D), lambda i: (i, 0)),
-        ],
-        out_shape=[
-            jax.ShapeDtypeStruct((tokens, 3 * D), BF),
-            jax.ShapeDtypeStruct((rows * NH, 1, length), F32),
-            jax.ShapeDtypeStruct((tokens, D), BF),
-            jax.ShapeDtypeStruct((tokens, D), F32),
-        ],
-        scratch_shapes=[pltpu.VMEM((length, LANE), F32)],
-        compiler_params=pltpu.CompilerParams(vmem_limit_bytes=58 * MIB),
-        name="attn_forward",
-    )(x, g1, b1, wqkv, qb, wout, ob)
-
-
-def count_kernel(ids_ref, out_ref):
-    hashes, rows, chars = ids_ref.shape
-    high = BUCKETS // LANE
-
-    def one(h, carry):
-        total = jnp.zeros((high, LANE), F32)
-        for r in range(rows):
-            ids = ids_ref[h, r : r + 1, :]
-            row = lax.broadcasted_iota(jnp.int32, (high, chars), 0)
-            hi = jnp.where(row == (ids >> 7), 1.0, 0.0).astype(BF)
-            lo = jnp.where(row == (ids & (LANE - 1)), 1.0, 0.0).astype(BF)
-            total = total + dot_nt(hi, lo)
-        out_ref[h] = total.astype(jnp.int32)
-        return carry
-
-    lax.fori_loop(0, hashes, one, 0)
-
-
-def count(ids):
-    return pl.pallas_call(
-        count_kernel,
-        in_specs=[pl.BlockSpec(memory_space=pltpu.VMEM)],
-        out_specs=pl.BlockSpec(memory_space=pltpu.VMEM),
-        out_shape=jax.ShapeDtypeStruct((ids.shape[0], BUCKETS // LANE, LANE), jnp.int32),
-        compiler_params=pltpu.CompilerParams(vmem_limit_bytes=32 * MIB),
-        name="bucket_tally",
-    )(ids)
-
-
 NB = 4
 NFF = FF // (NB * LANE)
 NPAIR = NFF + 3
@@ -168,7 +75,8 @@
 def orders(shape):
     seq = [("seq", 1 << b) for b in range(shape["seq"].bit_length() - 1)]
     row = [("rows", 1 << b) for b in range(shape["rows"].bit_length() - 1)]
-    return [seq + row, seq[:1] + row[:1] + seq[1:] + row[1:]]
+    first, rest, near, far = seq[:1], seq[1:], row[:1], row[1:]
+    return first + near + far + rest, first + rest + near + far
 
 
 class Halving:
@@ -198,11 +106,14 @@
             self.row_at.append(row_at)
         self.gathers = [i for i in reversed(range(len(order))) if self.split[i] is not None]
 
+    def partner(self, i):
+        return across(self.order[i])
+
     def rows_of(self, at, size):
         return pl.ds(pl.multiple_of(at, self.tile), size)
 
     def send(self, i, mine, land, sems):
-        step, (lead, rows) = self.order[i], self.size[i]
+        lead, rows = self.size[i]
         if i == 0:
             src = mine.at[pl.ds(lead - self.first, lead)]
         else:
@@ -213,7 +124,7 @@
                 ra = ra + (1 - self.own[i]) * rows
             src = land[0].at[pl.ds(la, lead), self.rows_of(ra, rows)]
         return pltpu.make_async_remote_copy(src_ref=src, dst_ref=land[i], send_sem=sems[0].at[i], recv_sem=sems[1].at[i],
-                                            device_id=across(step), device_id_type=MESH)
+                                            device_id=self.partner(i), device_id_type=MESH)
 
     def add(self, i, mine, land):
         lead, rows = self.size[i]
@@ -250,7 +161,7 @@
         here = out.at[self.out_level(i)]
         src = land[0].at[self.at_level(len(self.order) - 1)] if m == 0 else here
         return pltpu.make_async_remote_copy(src_ref=src, dst_ref=here, send_sem=sems[0].at[m], recv_sem=sems[1].at[m],
-                                            device_id=across(self.order[i]), device_id_type=MESH)
+                                            device_id=self.partner(i), device_id_type=MESH)
 
     def reduce_step(self, k, mine, land, sems):
         n = len(self.order)
@@ -282,7 +193,187 @@
     return shapes
 
 
-AG_AT = (8, 13, 18, 22, 23, 24, 25, 27, 28)
+def peers(nseq):
+    me = lax.axis_index("seq")
+    found = []
+    for m in sorted(range(1, nseq), key=lambda m: -(m >> 1)):
+        to = 0
+        for b in range(nseq.bit_length() - 1):
+            bit = (me // (1 << b)) % 2
+            to = to + (bit + ((m >> b) & 1) * (1 - 2 * bit)) * (1 << b)
+        found.append((m, to))
+    return found
+
+
+def front_kernel(shape, mol_h, cot_h, wqkv_h, wout_h, ids_ref, g1_ref, b1_ref, qb_ref, ob_ref,
+                 x_out, dy_out, qkv_out, ctx_out, mid_out, lse_ref, cnt_ref,
+                 xs, qkv_s, ctx_s, mid_s, wqkv_s, wout_s, lacc,
+                 w_sem, m_send, m_recv, m_own, c_send, c_recv, c_own, o_sem):
+    nseq = shape["seq"]
+    rows, length = xs.shape[0], xs.shape[1]
+    local = length // nseq
+    rows_idx, me = spots()
+    near = peers(nseq)
+
+    barrier = pltpu.get_barrier_semaphore()
+    for _, to in near:
+        pl.semaphore_signal(barrier, inc=1, device_id=(rows_idx, to), device_id_type=MESH)
+    fetch = [pltpu.make_async_copy(wqkv_h, wqkv_s, w_sem.at[0]), pltpu.make_async_copy(wout_h, wout_s, w_sem.at[1])]
+    here = pl.ds(pl.multiple_of(me * local, local), local)
+
+    def own(r):
+        return pltpu.make_async_copy(mol_h.at[me * rows + r], xs.at[r, here], m_own.at[r])
+
+    def mol(r, n):
+        m, to = near[n]
+        return pltpu.make_async_remote_copy(src_ref=mol_h.at[to * rows + r], dst_ref=xs.at[r, here], send_sem=m_send.at[r, m],
+                                            recv_sem=m_recv.at[r, m], device_id=(rows_idx, to), device_id_type=MESH)
+
+    def cot(n):
+        m, to = near[n]
+        return pltpu.make_async_remote_copy(src_ref=cot_h.at[pl.ds(to * rows, rows)], dst_ref=dy_out.at[:, here],
+                                            send_sem=c_send.at[m], recv_sem=c_recv.at[m], device_id=(rows_idx, to),
+                                            device_id_type=MESH)
+
+    cot_own = pltpu.make_async_copy(cot_h.at[pl.ds(me * rows, rows)], dy_out.at[:, here], c_own)
+
+    for r in range(rows):
+        own(r).start()
+    fetch[0].start()
+    pl.semaphore_wait(barrier, len(near))
+    for r in range(rows):
+        for n in range(len(near)):
+            mol(r, n).start()
+    fetch[1].start()
+    cot_own.start()
+
+    half = 2 * local
+
+    def project(r, at):
+        src = pl.ds(pl.multiple_of(at, half), half)
+        dst = pl.ds(pl.multiple_of(r * length + at, half), half)
+        xhat, _ = norm_parts(xs[r, src].astype(F32))
+        a1 = (xhat * g1_ref[...] + b1_ref[...]).astype(BF)
+        for c in range(3):
+            cols = slice(c * D, (c + 1) * D)
+            qkv_s[dst, cols] = (dot_nn(a1, wqkv_s[:, cols]) + qb_ref[:, cols]).astype(BF)
+
+    for r in range(rows):
+        own(r).wait()
+        mol(r, len(near) - 1).wait()
+    fetch[0].wait()
+    mine = (me // 2) * half
+
+    def early(r, carry):
+        project(r, mine)
+        return carry
+
+    lax.fori_loop(0, rows, early, 0)
+
+    hashes, id_rows, chars = ids_ref.shape
+    high = BUCKETS // LANE
+
+    def tally(h, carry):
+        total = jnp.zeros((high, LANE), F32)
+        for r in range(id_rows):
+            ids = ids_ref[h, r : r + 1, :]
+            row = lax.broadcasted_iota(jnp.int32, (high, chars), 0)
+            hi = jnp.where(row == (ids >> 7), 1.0, 0.0).astype(BF)
+            lo = jnp.where(row == (ids & (LANE - 1)), 1.0, 0.0).astype(BF)
+            total = total + dot_nt(hi, lo)
+        cnt_ref[h] = total.astype(jnp.int32)
+        return carry
+
+    lax.fori_loop(0, hashes, tally, 0)
+    fetch[1].wait()
+
+    def outs(r):
+        at = pl.ds(r * length, length)
+        return [pltpu.make_async_copy(xs.at[r], x_out.at[r], o_sem.at[r, 0]),
+                pltpu.make_async_copy(qkv_s.at[at], qkv_out.at[at], o_sem.at[r, 1]),
+                pltpu.make_async_copy(ctx_s.at[at], ctx_out.at[at], o_sem.at[r, 2]),
+                pltpu.make_async_copy(mid_s.at[at], mid_out.at[at], o_sem.at[r, 3])]
+
+    for r in range(rows):
+        for n in range(len(near) - 1):
+            mol(r, n).wait()
+        for other in range(1, nseq // 2):
+            project(r, ((me // 2 + other) % (nseq // 2)) * half)
+        ready = outs(r)
+        ready[0].start()
+        ready[1].start()
+        tok = slice(r * length, (r + 1) * length)
+
+        def pair(p, carry):
+            at = pl.multiple_of(p * LANE, LANE)
+            q = qkv_s[tok, pl.ds(at, LANE)] * BF(0.125)
+            k = qkv_s[tok, pl.ds(pl.multiple_of(D + at, LANE), LANE)]
+            v = qkv_s[tok, pl.ds(pl.multiple_of(2 * D + at, LANE), LANE)]
+            ctx = []
+            lse = lacc[...]
+            lane = lax.broadcasted_iota(jnp.int32, lse.shape, 1)
+            for half_of in range(2):
+                qm = jnp.where(lane_half(q.shape, half_of), q, BF(0))
+                s = dot_nt(qm, k)
+                m = jnp.max(s, -1, keepdims=True)
+                e = jnp.exp(s - m)
+                t = jnp.sum(e, -1, keepdims=True)
+                pr = (e * (1.0 / t)).astype(BF)
+                ctx.append(dot_nn(pr, v))
+                lse = jnp.where(lane == 2 * p + half_of, m + jnp.log(t), lse)
+            lacc[...] = lse
+            ctx_s[tok, pl.ds(at, LANE)] = jnp.where(lane_half(ctx[0].shape, 0), ctx[0], ctx[1]).astype(BF)
+            if r == 0:
+
+                @pl.when(p == 3)
+                def _():
+                    for n in range(len(near)):
+                        cot(n).start()
+
+            return carry
+
+        lacc[...] = jnp.zeros_like(lacc)
+        lax.fori_loop(0, NH // 2, pair, 0)
+        ready[2].start()
+        lt = lacc[...].T
+        for h in range(NH):
+            lse_ref[r * NH + h] = lt[h : h + 1, :]
+        mid_s[tok] = xs[r].astype(F32) + (dot_nn(ctx_s[tok], wout_s[...]) + ob_ref[...])
+        ready[3].start()
+    for r in range(rows):
+        for copy in outs(r):
+            copy.wait()
+    cot_own.wait()
+    for n in range(len(near)):
+        cot(n).wait()
+
+
+def front(shape, mol, cot, wqkv, wout, ids, g1, b1, qb, ob):
+    nseq = shape["seq"]
+    rows, length = mol.shape[0] // nseq, mol.shape[1] * nseq
+    tokens = rows * length
+    vm, hb = pl.BlockSpec(memory_space=pltpu.VMEM), pl.BlockSpec(memory_space=pl.ANY)
+    dma = pltpu.SemaphoreType.DMA
+    sds = jax.ShapeDtypeStruct
+    return pl.pallas_call(
+        functools.partial(front_kernel, shape),
+        in_specs=[hb] * 4 + [vm] * 5,
+        out_specs=[hb] * 5 + [vm] * 2,
+        out_shape=[sds((rows, length, D), BF), sds((rows, length, D), BF), sds((tokens, 3 * D), BF), sds((tokens, D), BF),
+                   sds((tokens, D), F32), sds((rows * NH, 1, length), F32), sds((ids.shape[0], BUCKETS // LANE, LANE), jnp.int32)],
+        scratch_shapes=[pltpu.VMEM((rows, length, D), BF), pltpu.VMEM((tokens, 3 * D), BF), pltpu.VMEM((tokens, D), BF),
+                        pltpu.VMEM((tokens, D), F32), pltpu.VMEM((D, 3 * D), BF), pltpu.VMEM((D, D), BF),
+                        pltpu.VMEM((length, LANE), F32), dma((2,)), dma((rows, nseq)), dma((rows, nseq)), dma((rows,)),
+                        dma((nseq,)), dma((nseq,)), dma, dma((rows, 4))],
+        compiler_params=pltpu.CompilerParams(vmem_limit_bytes=60 * MIB, collective_id=1, has_side_effects=True),
+        name="front",
+    )(mol, cot, wqkv, wout, ids, g1, b1, qb, ob)
+
+
+GAP_IN, GAP_OUT, GAP = 3, 3, 2
+IN_AT = tuple(2 * j + 1 for j in range(NFF)) + (2 * NFF + 6, 2 * NFF + 11, 2 * NFF + 16)
+AG_AT = (16, 18, 22, 24, 26, 28, 33, 38, 43)
+DRAIN = 2 * NFF + 17
 
 
 def rear_kernel(shape, length, mid_h, dy_h, x_h, qkv_h, ctx_h, wup_h, wdn_h, wqkv_h, wout_h, lse_ref, cnt_ref,
@@ -326,43 +417,45 @@
         copy.start()
     pl.semaphore_wait(barrier, len(others))
 
-    plans = [Halving(order, NB, D, 16) for order in both]
-    tally = Halving(both[1], cnt_ref.shape[0], cnt_ref.shape[1], 8)
-    in_at = list(range(NFF)) + [NFF + 5, NFF + 10, NFF + 15]
-    out_at = [max(a, b + nd) for a, b in zip(AG_AT, in_at)]
-    last_tick = NFF + 16
+    def plans(j):
+        return [Halving(order, NB, D, 16) for order in both]
+
+    tally = Halving(both[0], cnt_ref.shape[0], cnt_ref.shape[1], 8)
+    most = len(Halving(both[0], NB, D, 16).gathers)
+    out_at = []
+    for a, b in zip(AG_AT, IN_AT):
+        out_at.append(max(a, b + GAP_IN * nd, out_at[-1] + 1 if out_at else 0))
 
     def tick(t):
         for k in reversed(range(nd + 1)):
-            hit = sum(jnp.where(t == in_at[j] + k, 1, 0) for j in range(NPAIR))
-            j = sum(jnp.where(t == in_at[j] + k, j, 0) for j in range(NPAIR))
+            hit = sum(jnp.where(t == IN_AT[j] + GAP_IN * k, 1, 0) for j in range(NPAIR))
+            j = sum(jnp.where(t == IN_AT[j] + GAP_IN * k, j, 0) for j in range(NPAIR))
 
             @pl.when(hit == 1)
             def _():
-                for o, plan in enumerate(plans):
+                for o, plan in enumerate(plans(j)):
                     plan.reduce_step(k, stage_s.at[j % 2, o], [r.at[j, o] for r in land], (rs_send.at[j, o], rs_recv.at[j, o]))
 
-        most = max(len(plan.gathers) for plan in plans)
         for m in reversed(range(most + 1)):
-            hit = sum(jnp.where(t == out_at[j] + m, 1, 0) for j in range(NPAIR))
-            j = sum(jnp.where(t == out_at[j] + m, j, 0) for j in range(NPAIR))
+            hit = sum(jnp.where(t == out_at[j] + GAP_OUT * m, 1, 0) for j in range(NPAIR))
+            j = sum(jnp.where(t == out_at[j] + GAP_OUT * m, j, 0) for j in range(NPAIR))
 
             @pl.when(hit == 1)
             def _():
-                for o, plan in enumerate(plans):
+                for o, plan in enumerate(plans(j)):
                     plan.gather_step(m, [r.at[j, o] for r in land], sum_out.at[j, o], (ag_send.at[j, o], ag_recv.at[j, o]),
                                      keep_sem.at[j, o])
 
     def tick_counts(t):
         for k in range(nd + 1):
 
-            @pl.when(t == k)
+            @pl.when(t == GAP * k)
             def _():
                 tally.reduce_step(k, cnt_ref, cland, (crs_send, crs_recv))
 
         for m in range(len(tally.gathers) + 1):
 
-            @pl.when(t == nd + 1 + m)
+            @pl.when(t == GAP * (nd + 1 + m))
             def _():
                 tally.gather_step(m, cland, cnt_out, (cag_send, cag_recv), ckeep_sem)
 
@@ -417,6 +510,8 @@
         hid = (u * cdf).astype(BF)
         du = (dh * (cdf + u * pdf)).astype(BF)
         gub_s[:, cols] = jnp.sum(du.astype(F32), 0, keepdims=True)
+        tick(2 * i)
+        tick_counts(2 * i)
         acc_s[...] += dot_nn(hid, wdn_s[slot])
         da2_s[...] += dot_nt(du, wup_s[slot])
         gd = dot_nn(dyt_s[...], hid).astype(BF)
@@ -424,8 +519,8 @@
         for b in range(NB):
             stage_s[slot, 0, b] = gd[:, b * LANE : (b + 1) * LANE]
             stage_s[slot, 1, b] = gu[:, b * LANE : (b + 1) * LANE]
-        tick(i)
-        tick_counts(i)
+        tick(2 * i + 1)
+        tick_counts(2 * i + 1)
         return carry
 
     lax.fori_loop(0, NFF, ff, 0)
@@ -454,6 +549,8 @@
     dctx_s, do_s, dx2_s, da1_s, a1t_s = dy_s, a2_s, da2_s, acc_s, a2t_s
     for copy in give_back(0, lo_out):
         copy.start()
+    tick(2 * NFF)
+    tick_counts(2 * NFF)
     fetch(4).wait()
     fetch(2).wait()
     gout = dot_tn(ctx_s[...], do_s[...]).astype(BF)
@@ -470,8 +567,8 @@
     lax.fori_loop(0, pieces, first_norm, 0)
     fetch(3).wait()
     fetch(5).wait()
-    tick(NFF)
-    tick_counts(NFF)
+    tick(2 * NFF + 1)
+    tick_counts(2 * NFF + 1)
 
     def group(g, carry):
         def unit(n, inner_carry):
@@ -502,8 +599,8 @@
             dqkv_s[tok, pl.ds(pl.multiple_of(h * LANE, LANE), LANE)] = (jnp.where(sel, dqs[0], dqs[1]) * 0.125).astype(BF)
             dqkv_s[tok, pl.ds(pl.multiple_of(h * LANE + 2 * LANE, LANE), LANE)] = jnp.where(sel, dks[0], dks[1]).astype(BF)
             dqkv_s[tok, pl.ds(pl.multiple_of(h * LANE + 4 * LANE, LANE), LANE)] = jnp.where(sel, dvs[0], dvs[1]).astype(BF)
-            tick(NFF + 1 + 5 * g + n)
-            tick_counts(NFF + 1 + 5 * g + n)
+            tick(2 * NFF + 2 + 5 * g + n)
+            tick_counts(2 * NFF + 2 + 5 * g + n)
             return inner_carry
 
         lax.fori_loop(0, 4, unit, 0)
@@ -520,8 +617,8 @@
         here = pl.ds(pl.multiple_of(g * two, two), two)
         part_s[6:7, here] = jnp.sum(dqkv_s[:, 0:two].astype(F32), 0, keepdims=True)
         part_s[7:8, here] = jnp.sum(dqkv_s[:, 2 * two : 3 * two].astype(F32), 0, keepdims=True)
-        tick(NFF + 5 + 5 * g)
-        tick_counts(NFF + 5 + 5 * g)
+        tick(2 * NFF + 6 + 5 * g)
+        tick_counts(2 * NFF + 6 + 5 * g)
         return carry
 
     lax.fori_loop(0, 3, group, 0)
@@ -554,7 +651,7 @@
     def drain(t, carry):
         for i in range(nd + 1):
 
-            @pl.when(t == last_tick + i)
+            @pl.when(t == DRAIN + GAP * i)
             def _():
                 if i > 0:
                     swap(i - 1).wait()
@@ -565,8 +662,8 @@
         tick(t)
         return carry
 
-    end = max(max(out_at) + max(len(plan.gathers) for plan in plans), last_tick + nd) + 1
-    lax.fori_loop(last_tick, end, drain, 0)
+    end = max(max(out_at) + GAP_OUT * most, DRAIN + GAP * nd) + 1
+    lax.fori_loop(DRAIN, end, drain, 0)
     vec_out[...] = vacc_s[nd]
     for copy in give_back(1, gm_out):
         copy.wait()
@@ -605,47 +702,95 @@
     )(mid, dy, x, qkv, ctx, wup, wdn, wqkv, wout, lse, cnt, g1, b1, g2, b2, ub, db)
 
 
-def widen_kernel(turned, src_ref, out_ref):
-    for j in range(src_ref.shape[0]):
-        at = slice(j * LANE, (j + 1) * LANE)
-        if turned:
-            out_ref[at, :] = src_ref[j].astype(F32).T
-        else:
-            out_ref[:, at] = src_ref[j].astype(F32)
-
-
-def widen(blocks, number, group, where, turned=False):
-    wide = group * LANE
+def widen_kernel(src_ref, gm_ref, gmol_ref, qkv_out, out_out, up_out, down_out, wide_s, tall_s, sem):
+    j = pl.program_id(0)
+    slot = j % 2
+    fc = NB * LANE
+    two = 2 * LANE
+
+    def first(i, s):
+        at = pl.ds(pl.multiple_of(i * fc, fc), fc)
+        return [pltpu.make_async_copy(tall_s.at[s], down_out.at[at], sem.at[s, 0]),
+                pltpu.make_async_copy(wide_s.at[s, 0], up_out.at[:, at], sem.at[s, 1])]
+
+    def later(i, s):
+        g = i - NFF
+        to = lambda c: pl.ds(pl.multiple_of(c * D + g * two, two), two)
+        return [pltpu.make_async_copy(wide_s.at[s, 0, :, 0:two], qkv_out.at[:, to(0)], sem.at[s, 0]),
+                pltpu.make_async_copy(wide_s.at[s, 0, :, two : 2 * two], qkv_out.at[:, to(1)], sem.at[s, 1]),
+                pltpu.make_async_copy(wide_s.at[s, 1, :, 0:two], qkv_out.at[:, to(2)], sem.at[s, 2]),
+                pltpu.make_async_copy(wide_s.at[s, 1, :, two : 2 * two], out_out.at[:, to(0)], sem.at[s, 3])]
+
+    def finish(i, s):
+        @pl.when(i < NFF)
+        def _():
+            for copy in first(i, s):
+                copy.wait()
+
+        @pl.when(i >= NFF)
+        def _():
+            for copy in later(i, s):
+                copy.wait()
+
+    @pl.when(j >= 2)
+    def _():
+        finish(j - 2, slot)
+
+    gmol_ref[...] = gm_ref[...].astype(F32)
+
+    @pl.when(j < NFF)
+    def _():
+        for b in range(NB):
+            at = slice(b * LANE, (b + 1) * LANE)
+            tall_s[slot, at, :] = src_ref[0, 0, b].astype(F32).T
+            wide_s[slot, 0, :, at] = src_ref[0, 1, b].astype(F32)
+        for copy in first(j, slot):
+            copy.start()
+
+    @pl.when(j >= NFF)
+    def _():
+        for o in range(2):
+            for b in range(NB):
+                wide_s[slot, o, :, b * LANE : (b + 1) * LANE] = src_ref[0, o, b].astype(F32)
+        for copy in later(j, slot):
+            copy.start()
+
+    @pl.when(j == NPAIR - 1)
+    def _():
+        finish(j - 1, 1 - slot)
+        finish(j, slot)
+
+
+def widen(sums, gm):
+    hb = pl.BlockSpec(memory_space=pl.ANY)
+    sds = jax.ShapeDtypeStruct
+    rows = gm.shape[0]
+    some = pl.BlockSpec((1,) + gm.shape[1:], lambda j: (jnp.minimum(j, rows - 1), 0, 0))
     return pl.pallas_call(
-        functools.partial(widen_kernel, turned),
-        grid=(number,),
-        in_specs=[pl.BlockSpec((group, D, LANE), lambda i: (where(i), 0, 0))],
-        out_specs=pl.BlockSpec((wide, D), lambda i: (i, 0)) if turned else pl.BlockSpec((D, wide), lambda i: (0, i)),
-        out_shape=jax.ShapeDtypeStruct((number * wide, D) if turned else (D, number * wide), F32),
-        compiler_params=pltpu.CompilerParams(vmem_limit_bytes=32 * MIB),
+        widen_kernel,
+        grid=(NPAIR,),
+        in_specs=[pl.BlockSpec((1, 2, NB, D, LANE), lambda j: (j, 0, 0, 0, 0)), some],
+        out_specs=[some, hb, hb, hb, hb],
+        out_shape=[sds(gm.shape, F32), sds((D, 3 * D), F32), sds((D, D), F32), sds((D, FF), F32), sds((FF, D), F32)],
+        scratch_shapes=[pltpu.VMEM((2, 2, D, NB * LANE), F32), pltpu.VMEM((2, NB * LANE, D), F32), pltpu.SemaphoreType.DMA((2, 4))],
+        compiler_params=pltpu.CompilerParams(vmem_limit_bytes=60 * MIB),
         name="widen",
-    )(blocks)
+    )(sums, gm)
 
 
 def on_device(shape, molecules, ln1_gain, ln1_bias, w_qkv, qkv_bias, w_out, out_bias, ln2_gain, ln2_bias, w_up, up_bias,
               w_down, down_bias, out_cotangent, bucket_ids):
-    rows_here, local_len, width = molecules.shape
-    length = local_len * shape["seq"]
+    width = molecules.shape[2]
+    length = molecules.shape[1] * shape["seq"]
     row = lambda a: a.reshape(1, -1)
-    tally = count(bucket_ids)
-    x = lax.all_to_all(molecules, "seq", split_axis=0, concat_axis=1, tiled=True).reshape(-1, width)
-    dy = lax.all_to_all(out_cotangent, "seq", split_axis=0, concat_axis=1, tiled=True).reshape(-1, width)
     qb = jnp.concatenate([qkv_bias[0], jnp.zeros((width,), F32), qkv_bias[1]]).reshape(1, -1)
-    qkv, lse, ctx, mid = forward(x, row(ln1_gain), row(ln1_bias), w_qkv, qb, w_out, row(out_bias), length)
+    x, dy, qkv, ctx, mid, lse, tally = front(shape, molecules, out_cotangent, w_qkv, w_out, bucket_ids, row(ln1_gain),
+                                             row(ln1_bias), qb, row(out_bias))
     layer_out, gm, sums, counts, vec = rear(
-        shape, length, mid, dy, x, qkv, ctx, w_up, w_down, w_qkv, w_out, lse, tally, row(ln1_gain), row(ln1_bias),
-        row(ln2_gain), row(ln2_bias), row(up_bias), row(down_bias))
-    blocks = sums.reshape(-1, D, LANE)
-    g_qkv = widen(blocks, 9, 2, lambda i: (NFF + i % 3) * NB + i // 3)
-    g_out = widen(blocks, 3, 2, lambda i: (NFF + i) * NB + 3)
-    g_up = widen(blocks, NFF, NB, lambda i: 2 * i + 1)
-    g_down = widen(blocks, NFF, NB, lambda i: 2 * i, True)
-    return (layer_out, gm.astype(F32), vec[4], vec[5], g_qkv, vec[6:8], g_out, vec[3], vec[1], vec[2],
+        shape, length, mid, dy.reshape(-1, width), x.reshape(-1, width), qkv, ctx, w_up, w_down, w_qkv, w_out, lse, tally,
+        row(ln1_gain), row(ln1_bias), row(ln2_gain), row(ln2_bias), row(up_bias), row(down_bias))
+    g_mol, g_qkv, g_out, g_up, g_down = widen(sums, gm)
+    return (layer_out, g_mol, vec[4], vec[5], g_qkv, vec[6:8], g_out, vec[3], vec[1], vec[2],
             g_up, vec[8:12].reshape(-1), g_down, vec[0], counts.reshape(bucket_ids.shape[0], BUCKETS))
 
 

time: 335 us -> 263 us (0.79)
  Pallas kernels: 277 us -> 245 us
  blocking collectives: 24.3 us -> 0 us
  waiting for transfers between devices: 10.1 us -> 0 us
  starting transfers between devices: 3.71 us -> 0 us
    pallas_call x1, Pallas kernels: 231 us -> 185 us  [rear(): pl.pallas_call(functools.partial(rear_kernel, shape, length), in_specs=[h...]
    all_to_all x1 -> x0, blocking collectives: 24.3 us -> none  [on_device(): lax.all_to_all(molecules, 'seq', split_axis=0, concat_axis=1, tiled=True)]
    pallas_call x6 -> x2, Pallas kernels: 45.6 us -> 60.1 us  [the longest x1 41.6 us: front(): pl.pallas_call(functools.partial(front_kernel, shape), in_specs=[hb] * 4...]
    all_to_all x1 -> x0, waiting for transfers between devices: 10.1 us -> none  [on_device(): lax.all_to_all(out_cotangent, 'seq', split_axis=0, concat_axis=1, tiled=T...]
    unnamed x30 -> x4, local copies, waits for them, and re-layouts: 8.1 us -> 3.29 us
    reshape x6, local copies, waits for them, and re-layouts: 3.48 us -> 7.6 us  [on_device(): row = lambda a: a.reshape(1, -1)]
    all_to_all x1 -> x0, starting transfers between devices: 3.71 us -> none  [on_device(): lax.all_to_all(out_cotangent, 'seq', split_axis=0, concat_axis=1, tiled=T...]
  transfers between devices with their start and end apart: 1 -> 0, of which waited for: 1 -> 0; matrix products, arithmetic and copies ran while one was open for 2% -> 0% of each run, Pallas kernels for 1% -> 0%
where the time goes in v3:
time: 263 us
  Pallas kernels  245 us (93%)
  local copies, waits for them, and re-layouts  16.7 us (6%)
    pallas_call x1, Pallas kernels, rear(): pl.pallas_call(functools.partial(rear_kernel, shape, length), in_specs=[h...  185 us
    pallas_call x1, Pallas kernels, front(): pl.pallas_call(functools.partial(front_kernel, shape), in_specs=[hb] * 4...  41.6 us
    pallas_call x1, Pallas kernels, widen(): pl.pallas_call(widen_kernel, grid=(NPAIR,), in_specs=[pl.BlockSpec((1, 2,...  18.6 us
    reshape x6, local copies, waits for them, and re-layouts, on_device(): row = lambda a: a.reshape(1, -1)  7.6 us

profile of v3, /device:TPU:0, one launch (start us, length us, event | category | flops | bytes accessed | tf_op | source)
XLA Modules:
  0.0 262.7 jit_solution(6952371404054779328)
XLA Ops:
  0.6 1.3 reshape.68.g1_ref
  1.9 1.3 reshape.69.b1_ref
  3.2 1.3 reshape.71.ob_ref
  4.4 1.3 reshape.74.g2_ref
  5.7 1.3 reshape.75.b2_ref
  7.0 1.3 reshape.77.db_ref
  8.2 0.8 slice_reduce_fusion.7
  9.1 0.6 reshape.70.qb_ref
  9.7 41.6 %front.1 = (bf16[2,512,768]{2,1,0:T(8,128)(2,1)}, bf16[2,512,768]{2,1,0:T(8,128)(2,1)}, bf16[1024,2304]{1,0:T(8,128)(2,1)}, bf16[1024,768]{1,0:T(8,128)(2,1)}, f...) custom-call(bf16[8,128,768]{2,1,0:T(8,128)(2,1)} %mol_h.1, bf16[8,128,768]{2,1,0:T(8,128)(2,1)} %cot_h.1, ...), custom_call_target="tpu_custom_call" | custom-call | tf_op jit(solution)/shard_map/front/pallas_call | solution.py:358
  51.2 185.1 %rear.1 = (bf16[8,128,768]{2,1,0:T(8,128)(2,1)}, bf16[8,128,768]{2,1,0:T(8,128)(2,1)}, bf16[9,2,4,768,128]{4,3,2,1,0:T(8,128)(2,1)}, s32[8,128,128]{2,1,0:T(8,128)}, f32[16,768]{1,0:T(8,128)}) custom-call(f32[1024,768]{1,0:T(8,128)} %get-tuple-element.32.mid_h, bf16[1024,768]{1,0:T(8,128)(2,1)} %bitcast.8, bf16[1024,768]{1,0:T(8,128)(2,1)} %bitcast.7, ...), custom_call_target="tpu_custom_call" | custom-call | tf_op jit(solution)/shard_map/rear/pallas_call | solution.py:692
  236.4 1.3 slice.34
  237.7 0.7 slice.38
  238.5 1.7 slice_reduce_fusion
  240.2 0.6 reshape.78
  240.8 2.1 copy.32
  243.0 0.0 copy-start
  243.0 18.6 %widen.1 = (f32[8,128,768]{2,1,0:T(8,128)}, f32[768,2304]{1,0:T(8,128)}, f32[768,768]{1,0:T(8,128)}, f32[768,3072]{1,0:T(8,128)}, f32[3072,768]{1,0:T(8,128)}) custom-call(bf16[9,2,4,768,128]{4,3,2,1,0:T(8,128)(2,1)} %get-tuple-element.40.src_ref, bf16[8,128,768]{2,1,0:T(8,128)(2,1)} %get-tuple-element.41.gm_ref), custom_call_target="tpu_custom_call" | custom-call | tf_op jit(solution)/shard_map/widen/pallas_call | solution.py:769
  261.5 0.0 copy-done
  261.5 1.1 copy.34
  (2 shorter events, 0.0 us)
Async XLA Ops:
  243.0 18.6 %copy-start = (bf16[8,128,768]{2,1,0:T(8,128)(2,1)S(1)}, bf16[8,128,768]{2,1,0:T(8,128)(2,1)}, u32[]{:S(2)}) copy-start(bf16[8,128,768]{2,1,0:T(8,128)(2,1)} %get-tuple-element.72) | copy-start | bytes 4718596

commit v4 on v3

--- a/solution.py
+++ b/solution.py
@@ -76,7 +76,9 @@
     seq = [("seq", 1 << b) for b in range(shape["seq"].bit_length() - 1)]
     row = [("rows", 1 << b) for b in range(shape["rows"].bit_length() - 1)]
     first, rest, near, far = seq[:1], seq[1:], row[:1], row[1:]
-    return first + near + far + rest, first + rest + near + far
+    named = {"W": near + far + rest, "X": rest + near + far, "Y": near + rest + far, "Z": far + near + rest,
+             "V": rest + far + near, "U": far + rest + near}
+    return {name: first + then for name, then in named.items()}
 
 
 class Halving:
@@ -205,7 +207,7 @@
     return found
 
 
-def front_kernel(shape, mol_h, cot_h, wqkv_h, wout_h, ids_ref, g1_ref, b1_ref, qb_ref, ob_ref,
+def front_kernel(shape, mol_h, cot_h, wqkv_h, wout_h, ids_ref, g1_in, b1_in, qb_ref, ob_in,
                  x_out, dy_out, qkv_out, ctx_out, mid_out, lse_ref, cnt_ref,
                  xs, qkv_s, ctx_s, mid_s, wqkv_s, wout_s, lacc,
                  w_sem, m_send, m_recv, m_own, c_send, c_recv, c_own, o_sem):
@@ -253,10 +255,13 @@
         src = pl.ds(pl.multiple_of(at, half), half)
         dst = pl.ds(pl.multiple_of(r * length + at, half), half)
         xhat, _ = norm_parts(xs[r, src].astype(F32))
-        a1 = (xhat * g1_ref[...] + b1_ref[...]).astype(BF)
+        a1 = (xhat * g1 + b1).astype(BF)
         for c in range(3):
             cols = slice(c * D, (c + 1) * D)
-            qkv_s[dst, cols] = (dot_nn(a1, wqkv_s[:, cols]) + qb_ref[:, cols]).astype(BF)
+            part = dot_nn(a1, wqkv_s[:, cols])
+            qkv_s[dst, cols] = (part if c == 1 else part + qb_ref[c // 2 : c // 2 + 1]).astype(BF)
+
+    g1, b1, ob = (ref[...].reshape(1, D) for ref in (g1_in, b1_in, ob_in))
 
     for r in range(rows):
         own(r).wait()
@@ -281,7 +286,7 @@
             hi = jnp.where(row == (ids >> 7), 1.0, 0.0).astype(BF)
             lo = jnp.where(row == (ids & (LANE - 1)), 1.0, 0.0).astype(BF)
             total = total + dot_nt(hi, lo)
-        cnt_ref[h] = total.astype(jnp.int32)
+        cnt_ref[:, pl.ds(h, 1), :] = total.astype(jnp.int32).reshape(high, 1, LANE)
         return carry
 
     lax.fori_loop(0, hashes, tally, 0)
@@ -338,7 +343,7 @@
         lt = lacc[...].T
         for h in range(NH):
             lse_ref[r * NH + h] = lt[h : h + 1, :]
-        mid_s[tok] = xs[r].astype(F32) + (dot_nn(ctx_s[tok], wout_s[...]) + ob_ref[...])
+        mid_s[tok] = xs[r].astype(F32) + (dot_nn(ctx_s[tok], wout_s[...]) + ob)
         ready[3].start()
     for r in range(rows):
         for copy in outs(r):
@@ -360,7 +365,7 @@
         in_specs=[hb] * 4 + [vm] * 5,
         out_specs=[hb] * 5 + [vm] * 2,
         out_shape=[sds((rows, length, D), BF), sds((rows, length, D), BF), sds((tokens, 3 * D), BF), sds((tokens, D), BF),
-                   sds((tokens, D), F32), sds((rows * NH, 1, length), F32), sds((ids.shape[0], BUCKETS // LANE, LANE), jnp.int32)],
+                   sds((tokens, D), F32), sds((rows * NH, 1, length), F32), sds((BUCKETS // LANE, ids.shape[0], LANE), jnp.int32)],
         scratch_shapes=[pltpu.VMEM((rows, length, D), BF), pltpu.VMEM((tokens, 3 * D), BF), pltpu.VMEM((tokens, D), BF),
                         pltpu.VMEM((tokens, D), F32), pltpu.VMEM((D, 3 * D), BF), pltpu.VMEM((D, D), BF),
                         pltpu.VMEM((length, LANE), F32), dma((2,)), dma((rows, nseq)), dma((rows, nseq)), dma((rows,)),
@@ -370,21 +375,77 @@
     )(mol, cot, wqkv, wout, ids, g1, b1, qb, ob)
 
 
-GAP_IN, GAP_OUT, GAP = 3, 3, 2
-IN_AT = tuple(2 * j + 1 for j in range(NFF)) + (2 * NFF + 6, 2 * NFF + 11, 2 * NFF + 16)
-AG_AT = (16, 18, 22, 24, 26, 28, 33, 38, 43)
-DRAIN = 2 * NFF + 17
+SPLIT = 2
+MID = SPLIT * NFF
+DRAIN = MID + 17
+IN_AT = tuple(SPLIT * (j + 1) - 1 for j in range(NFF)) + (MID + 6, MID + 11, MID + 16)
+EARLY_WAYS, LATE_WAYS, COUNT_WAY = ('X', 'W'), ('W', 'Y'), 'Z'
+REDUCE_AT = (
+    ((1, 2, 4, 5, 6, 7), (1, 2, 4, 5, 7, 8)),
+    ((3, 4, 6, 7, 8, 9), (3, 4, 7, 9, 11, 12)),
+    ((5, 6, 8, 9, 11, 12), (5, 6, 9, 11, 13, 17)),
+    ((7, 8, 10, 12, 13, 15), (7, 8, 11, 13, 16, 18)),
+    ((9, 10, 12, 13, 16, 19), (9, 10, 13, 17, 20, 25)),
+    ((11, 12, 15, 19, 22, 24), (11, 12, 15, 18, 21, 26)),
+    ((18, 19, 22, 25, 28, 99), (18, 20, 24, 28, 99, 99)),
+    ((23, 24, 28, 99, 99, 99), (23, 24, 99, 99, 99, 99)),
+    ((28, 99, 99, 99, 99, 99), (28, 99, 99, 99, 99, 99)),
+)
+GATHER_AT = (
+    ((7, 8, 9, 11, 13, 14), (8, 9, 12, 14, 18, 20)),
+    ((9, 10, 12, 16, 19, 20), (12, 13, 17, 20, 26, 28)),
+    ((12, 13, 17, 19, 25, 26), (17, 21, 24, 28, 99, 99)),
+    ((15, 18, 21, 27, 99, 99), (18, 23, 27, 99, 99, 99)),
+    ((27, 28, 99, 99, 99, 99), (27, 99, 99, 99, 99, 99)),
+    ((28, 99, 99, 99, 99, 99), (28, 99, 99, 99, 99, 99)),
+    ((99, 99, 99, 99, 99, 99), (99, 99, 99, 99, 99, 99)),
+    ((99, 99, 99, 99, 99, 99), (99, 99, 99, 99, 99, 99)),
+    ((99, 99, 99, 99, 99, 99), (99, 99, 99, 99, 99, 99)),
+)
+COUNT_AT = (0, 1, 3, 5, 7, 8, 15, 17, 20, 23, 26, 27)
+BACK_AT = (17, 24, 13, 18)
+LATE = (
+    (3, 0, 0, 0), (1, 3, 1, 3), (1, 3, 0, 4), (0, 7, 1, 2), (0, 8, 0, 1), (1, 4, 1, 1), (0, 6, 0, 5), (0, 6, 1, 4), (0, 8, 1, 1),
+    (3, 0, 0, 1), (1, 5, 1, 1), (1, 3, 0, 5), (0, 7, 0, 3), (1, 4, 0, 2), (1, 2, 1, 4), (1, 5, 0, 1), (1, 2, 1, 5), (1, 4, 1, 2),
+    (0, 6, 1, 5), (1, 3, 1, 4), (1, 6, 0, 0), (1, 6, 1, 0), (1, 5, 1, 2), (1, 3, 1, 5), (1, 5, 0, 2), (0, 7, 0, 4), (0, 8, 0, 2),
+    (1, 4, 1, 3), (1, 6, 1, 1), (0, 8, 1, 2), (1, 5, 1, 3), (1, 4, 0, 3), (0, 8, 0, 3), (0, 7, 1, 3), (1, 6, 1, 2), (3, 0, 0, 2),
+    (1, 5, 0, 3), (1, 6, 0, 1), (0, 7, 0, 5), (1, 7, 0, 0), (0, 7, 1, 4), (0, 8, 0, 4), (0, 8, 1, 3), (1, 4, 1, 4), (1, 6, 0, 2),
+    (0, 7, 1, 5), (1, 7, 1, 0), (0, 8, 1, 4), (1, 4, 1, 5), (1, 4, 0, 4), (1, 6, 0, 3), (1, 5, 1, 4), (1, 4, 0, 5), (1, 7, 1, 1),
+    (1, 6, 1, 3), (3, 0, 0, 3), (1, 5, 1, 5), (0, 8, 1, 5), (1, 8, 1, 0), (1, 7, 1, 2), (3, 0, 0, 4), (1, 5, 0, 4), (1, 8, 1, 1),
+    (1, 6, 0, 4), (1, 7, 0, 1), (0, 8, 0, 5), (1, 8, 0, 0), (1, 5, 0, 5), (1, 6, 0, 5), (1, 7, 1, 3), (3, 0, 0, 5), (1, 8, 1, 2),
+    (1, 8, 0, 1), (1, 6, 1, 4), (1, 7, 0, 2), (1, 6, 1, 5), (1, 8, 1, 3), (1, 8, 0, 2), (1, 7, 1, 4), (1, 7, 0, 3), (1, 7, 1, 5),
+    (1, 8, 0, 3), (1, 8, 1, 4), (1, 8, 1, 5), (1, 7, 0, 4), (1, 7, 0, 5), (1, 8, 0, 4), (1, 8, 0, 5),
+)
+
+
+def timetable(nd, gathers, tally_gathers):
+    if nd == len(REDUCE_AT[0][0]) - 1:
+        ticks = {}
+        for j in range(NPAIR):
+            for o in range(2):
+                ticks |= {(0, j, o, k): t for k, t in enumerate(REDUCE_AT[j][o])}
+                ticks |= {(1, j, o, m): t for m, t in enumerate(GATHER_AT[j][o])}
+        ticks |= {(2, 0, 0, k): t for k, t in enumerate(COUNT_AT)}
+        return {key: t for key, t in ticks.items() if t < DRAIN}, BACK_AT, list(LATE)
+    ticks = {}
+    for j, t in enumerate(IN_AT):
+        for o in range(2):
+            ticks |= {(0, j, o, k): t + 3 * k for k in range(nd + 1)}
+            ticks |= {(1, j, o, m): max(t + 3 * nd, 20 + 2 * j) + 3 * m for m in range(gathers + 1)}
+    ticks |= {(2, 0, 0, k): 2 * k for k in range(nd + 2 + tally_gathers)}
+    late = sorted((t, key) for key, t in ticks.items() if t >= DRAIN)
+    return {key: t for key, t in ticks.items() if t < DRAIN}, (MID + 1,) * 4, [(3, 0, 0, k) for k in range(nd + 1)] + [key for _, key in late]
 
 
 def rear_kernel(shape, length, mid_h, dy_h, x_h, qkv_h, ctx_h, wup_h, wdn_h, wqkv_h, wout_h, lse_ref, cnt_ref,
-                g1_ref, b1_ref, g2_ref, b2_ref, ub_ref, db_ref,
+                g1_in, b1_in, g2_in, b2_in, ub_in, db_in,
                 lo_out, gm_out, sum_out, cnt_out, vec_out,
                 mid_s, dy_s, a2_s, a2t_s, dyt_s, acc_s, da2_s, wup_s, wdn_s, qkv_s, ctx_s, x_s, wqkv_s, wout_s,
-                dqkv_s, gout_s, lo_s, vec_s, gub_s, part_s, fetch_sem, stage_s, vland_s, vacc_s,
+                dqkv_s, gout_s, lo_s, vec_s, gub_s, part_s, fetch_sem, stage_s, vland_s, vacc_s, five_s, ub_s,
                 rs_send, rs_recv, ag_send, ag_recv, keep_sem, crs_send, crs_recv, cag_send, cag_recv, ckeep_sem,
                 v_send, v_recv, t_send, t_recv, t_own, *lands):
-    both = orders(shape)
-    nd = len(both[0])
+    ways = orders(shape)
+    nd = len(ways["X"])
     nseq = shape["seq"]
     land = lands[:nd]
     cland = lands[nd:]
@@ -395,11 +456,8 @@
     fc = NB * LANE
 
     barrier = pltpu.get_barrier_semaphore()
-    others = [across(step) for step in both[0]]
-    for m in range(3, nseq):
-        if m & (m - 1):
-            others.append((rows_idx, sum(((me // (1 << b)) % 2 + ((m >> b) & 1) * (1 - 2 * ((me // (1 << b)) % 2))) * (1 << b)
-                                         for b in range(nseq.bit_length() - 1))))
+    others = [across(step) for step in ways["X"]]
+    others += [(rows_idx, to) for m, to in peers(nseq) if m & (m - 1)]
     for other in others:
         pl.semaphore_signal(barrier, inc=1, device_id=other, device_id_type=MESH)
 
@@ -411,65 +469,86 @@
         return (pltpu.make_async_copy(wup_h.at[:, pl.ds(pl.multiple_of(i * fc, fc), fc)], wup_s.at[slot], fetch_sem.at[8 + slot]),
                 pltpu.make_async_copy(wdn_h.at[pl.ds(pl.multiple_of(i * fc, fc), fc)], wdn_s.at[slot], fetch_sem.at[10 + slot]))
 
+    for n, ref in enumerate((g1_in, b1_in, g2_in, b2_in, db_in)):
+        five_s[n : n + 1] = ref[...].reshape(1, D)
+    ub_s[...] = ub_in[...].reshape(1, FF)
+    g1_ref, b1_ref, g2_ref, b2_ref, db_ref = (five_s.at[n : n + 1] for n in range(5))
+    ub_ref = ub_s
     fetch(0).start()
     fetch(1).start()
     for copy in weights(0, 0):
         copy.start()
     pl.semaphore_wait(barrier, len(others))
 
-    def plans(j):
-        return [Halving(order, NB, D, 16) for order in both]
-
-    tally = Halving(both[0], cnt_ref.shape[0], cnt_ref.shape[1], 8)
-    most = len(Halving(both[0], NB, D, 16).gathers)
-    out_at = []
-    for a, b in zip(AG_AT, IN_AT):
-        out_at.append(max(a, b + GAP_IN * nd, out_at[-1] + 1 if out_at else 0))
-
-    def tick(t):
-        for k in reversed(range(nd + 1)):
-            hit = sum(jnp.where(t == IN_AT[j] + GAP_IN * k, 1, 0) for j in range(NPAIR))
-            j = sum(jnp.where(t == IN_AT[j] + GAP_IN * k, j, 0) for j in range(NPAIR))
-
-            @pl.when(hit == 1)
-            def _():
-                for o, plan in enumerate(plans(j)):
-                    plan.reduce_step(k, stage_s.at[j % 2, o], [r.at[j, o] for r in land], (rs_send.at[j, o], rs_recv.at[j, o]))
-
-        for m in reversed(range(most + 1)):
-            hit = sum(jnp.where(t == out_at[j] + GAP_OUT * m, 1, 0) for j in range(NPAIR))
-            j = sum(jnp.where(t == out_at[j] + GAP_OUT * m, j, 0) for j in range(NPAIR))
-
-            @pl.when(hit == 1)
-            def _():
-                for o, plan in enumerate(plans(j)):
-                    plan.gather_step(m, [r.at[j, o] for r in land], sum_out.at[j, o], (ag_send.at[j, o], ag_recv.at[j, o]),
-                                     keep_sem.at[j, o])
-
-    def tick_counts(t):
-        for k in range(nd + 1):
-
-            @pl.when(t == GAP * k)
-            def _():
-                tally.reduce_step(k, cnt_ref, cland, (crs_send, crs_recv))
-
-        for m in range(len(tally.gathers) + 1):
-
-            @pl.when(t == GAP * (nd + 1 + m))
-            def _():
-                tally.gather_step(m, cland, cnt_out, (cag_send, cag_recv), ckeep_sem)
-
-    def give_back(which, out):
-        copies = []
-        for m in range(1, nseq):
-            bits = [(me // (1 << b)) % 2 for b in range(nseq.bit_length() - 1)]
-            to = sum((bit + ((m >> b) & 1) * (1 - 2 * bit)) * (1 << b) for b, bit in enumerate(bits))
-            copies.append(pltpu.make_async_remote_copy(
-                src_ref=lo_s.at[:, pl.ds(pl.multiple_of(to * local, local), local)], dst_ref=out.at[pl.ds(me * rows, rows)],
-                send_sem=t_send.at[which, m], recv_sem=t_recv.at[which, m], device_id=(rows_idx, to), device_id_type=MESH))
-        copies.append(pltpu.make_async_copy(lo_s.at[:, pl.ds(pl.multiple_of(me * local, local), local)],
-                                            out.at[pl.ds(me * rows, rows)], t_own.at[which]))
-        return copies
+    near = peers(nseq)
+
+    def give_back(which, out, r, n):
+        m, to = near[n]
+        return pltpu.make_async_remote_copy(
+            src_ref=lo_s.at[r, pl.ds(pl.multiple_of(to * local, local), local)], dst_ref=out.at[me * rows + r],
+            send_sem=t_send.at[which, r, m], recv_sem=t_recv.at[which, r, m], device_id=(rows_idx, to), device_id_type=MESH)
+
+    def give_self(which, out):
+        return pltpu.make_async_copy(lo_s.at[:, pl.ds(pl.multiple_of(me * local, local), local)],
+                                     out.at[pl.ds(me * rows, rows)], t_own.at[which])
+
+    def give_wait(which, out):
+        give_self(which, out).wait()
+        for r in range(rows):
+            for n in range(len(near)):
+                give_back(which, out, r, n).wait()
+
+    back = [(r, n) for r in range(rows) for n in range(len(near) - 1)]
+
+    tally = Halving(ways[COUNT_WAY], cnt_ref.shape[0], cnt_ref.shape[1], 8)
+    gathers = len(Halving(ways["X"], NB, D, 16).gathers)
+    ticks, back_at, late = timetable(nd, gathers, len(tally.gathers))
+
+    def act(kind, j, o, k, which):
+        plan = Halving(ways[which], NB, D, 16)
+        here = [r.at[j, o] for r in land]
+        if kind == 0:
+            plan.reduce_step(k, stage_s.at[j % 2, o], here, (rs_send.at[j, o], rs_recv.at[j, o]))
+        else:
+            plan.gather_step(k, here, sum_out.at[j, o], (ag_send.at[j, o], ag_recv.at[j, o]), keep_sem.at[j, o])
+
+    def act_counts(k):
+        if k <= nd:
+            tally.reduce_step(k, cnt_ref, cland, (crs_send, crs_recv))
+        else:
+            tally.gather_step(k - nd - 1, cland, cnt_out, (cag_send, cag_recv), ckeep_sem)
+
+    def tick(t, low, high):
+        for kind, most in ((0, nd), (1, gathers)):
+            for k in reversed(range(most + 1)):
+                for o in range(2):
+                    for named, pairs in ((EARLY_WAYS[o], range(NFF)), (LATE_WAYS[o], range(NFF, NPAIR))):
+                        found = [(ticks.get((kind, j, o, k), -1), j) for j in pairs]
+                        found = [(at, j) for at, j in found if low <= at <= high]
+                        assert len({at for at, _ in found}) == len(found)
+                        if not found:
+                            continue
+                        hit = sum(jnp.where(t == at, 1, 0) for at, _ in found)
+                        j = sum(jnp.where(t == at, j, 0) for at, j in found)
+
+                        @pl.when(hit == 1)
+                        def _():
+                            act(kind, j, o, k, named)
+
+        for k in range(nd + 2 + len(tally.gathers)):
+            at = ticks.get((2, 0, 0, k), -1)
+            if low <= at <= high:
+
+                @pl.when(t == at)
+                def _():
+                    act_counts(k)
+
+        for n, at in enumerate(back_at):
+            if low <= at <= high:
+
+                @pl.when(t == at)
+                def _():
+                    give_back(0, lo_out, *back[n]).start()
 
     step = 256
     pieces = tokens // step
@@ -510,8 +589,7 @@
         hid = (u * cdf).astype(BF)
         du = (dh * (cdf + u * pdf)).astype(BF)
         gub_s[:, cols] = jnp.sum(du.astype(F32), 0, keepdims=True)
-        tick(2 * i)
-        tick_counts(2 * i)
+        tick(SPLIT * i, 0, MID - 1)
         acc_s[...] += dot_nn(hid, wdn_s[slot])
         da2_s[...] += dot_nt(du, wup_s[slot])
         gd = dot_nn(dyt_s[...], hid).astype(BF)
@@ -519,8 +597,7 @@
         for b in range(NB):
             stage_s[slot, 0, b] = gd[:, b * LANE : (b + 1) * LANE]
             stage_s[slot, 1, b] = gu[:, b * LANE : (b + 1) * LANE]
-        tick(2 * i + 1)
-        tick_counts(2 * i + 1)
+        tick(SPLIT * i + SPLIT - 1, 0, MID - 1)
         return carry
 
     lax.fori_loop(0, NFF, ff, 0)
@@ -547,10 +624,10 @@
 
     lax.fori_loop(0, pieces, turn_piece, 0)
     dctx_s, do_s, dx2_s, da1_s, a1t_s = dy_s, a2_s, da2_s, acc_s, a2t_s
-    for copy in give_back(0, lo_out):
-        copy.start()
-    tick(2 * NFF)
-    tick_counts(2 * NFF)
+    give_self(0, lo_out).start()
+    for r in range(rows):
+        give_back(0, lo_out, r, len(near) - 1).start()
+    tick(MID, MID, MID)
     fetch(4).wait()
     fetch(2).wait()
     gout = dot_tn(ctx_s[...], do_s[...]).astype(BF)
@@ -567,8 +644,7 @@
     lax.fori_loop(0, pieces, first_norm, 0)
     fetch(3).wait()
     fetch(5).wait()
-    tick(2 * NFF + 1)
-    tick_counts(2 * NFF + 1)
+    tick(MID + 1, MID + 1, MID + 1)
 
     def group(g, carry):
         def unit(n, inner_carry):
@@ -599,8 +675,7 @@
             dqkv_s[tok, pl.ds(pl.multiple_of(h * LANE, LANE), LANE)] = (jnp.where(sel, dqs[0], dqs[1]) * 0.125).astype(BF)
             dqkv_s[tok, pl.ds(pl.multiple_of(h * LANE + 2 * LANE, LANE), LANE)] = jnp.where(sel, dks[0], dks[1]).astype(BF)
             dqkv_s[tok, pl.ds(pl.multiple_of(h * LANE + 4 * LANE, LANE), LANE)] = jnp.where(sel, dvs[0], dvs[1]).astype(BF)
-            tick(2 * NFF + 2 + 5 * g + n)
-            tick_counts(2 * NFF + 2 + 5 * g + n)
+            tick(MID + 2 + 5 * g + n, MID + 2, DRAIN - 1)
             return inner_carry
 
         lax.fori_loop(0, 4, unit, 0)
@@ -617,14 +692,12 @@
         here = pl.ds(pl.multiple_of(g * two, two), two)
         part_s[6:7, here] = jnp.sum(dqkv_s[:, 0:two].astype(F32), 0, keepdims=True)
         part_s[7:8, here] = jnp.sum(dqkv_s[:, 2 * two : 3 * two].astype(F32), 0, keepdims=True)
-        tick(2 * NFF + 6 + 5 * g)
-        tick_counts(2 * NFF + 6 + 5 * g)
+        tick(MID + 6 + 5 * g, MID + 2, DRAIN - 1)
         return carry
 
     lax.fori_loop(0, 3, group, 0)
 
-    for copy in give_back(0, lo_out):
-        copy.wait()
+    give_wait(0, lo_out)
 
     def last_piece(n, carry):
         at = pl.ds(pl.multiple_of(n * step, step), step)
@@ -637,8 +710,10 @@
         return carry
 
     lax.fori_loop(0, pieces, last_piece, 0)
-    for copy in give_back(1, gm_out):
-        copy.start()
+    give_self(1, gm_out).start()
+    for r in range(rows):
+        for n in range(len(near)):
+            give_back(1, gm_out, r, n).start()
     vacc_s[0, 0:8] = part_s[...]
     for b in range(FF // (2 * LANE)):
         vacc_s[0, 8 + b // 3 : 9 + b // 3, (b % 3) * 2 * LANE : (b % 3 + 1) * 2 * LANE] = gub_s[:, b * 2 * LANE : (b + 1) * 2 * LANE]
@@ -646,34 +721,28 @@
 
     def swap(i):
         return pltpu.make_async_remote_copy(src_ref=vacc_s.at[i], dst_ref=vland_s.at[i], send_sem=v_send.at[i], recv_sem=v_recv.at[i],
-                                            device_id=across(both[0][i]), device_id_type=MESH)
-
-    def drain(t, carry):
-        for i in range(nd + 1):
-
-            @pl.when(t == DRAIN + GAP * i)
-            def _():
-                if i > 0:
-                    swap(i - 1).wait()
-                    vacc_s[i] = vacc_s[i - 1] + vland_s[i - 1]
-                if i < nd:
-                    swap(i).start()
-
-        tick(t)
-        return carry
-
-    end = max(max(out_at) + GAP_OUT * most, DRAIN + GAP * nd) + 1
-    lax.fori_loop(DRAIN, end, drain, 0)
+                                            device_id=across(ways["X"][i]), device_id_type=MESH)
+
+    for kind, j, o, k in late:
+        if kind < 2:
+            act(kind, j, o, k, (EARLY_WAYS if j < NFF else LATE_WAYS)[o])
+        elif kind == 2:
+            act_counts(k)
+        else:
+            if k > 0:
+                swap(k - 1).wait()
+                vacc_s[k] = vacc_s[k - 1] + vland_s[k - 1]
+            if k < nd:
+                swap(k).start()
     vec_out[...] = vacc_s[nd]
-    for copy in give_back(1, gm_out):
-        copy.wait()
+    give_wait(1, gm_out)
 
 
 def rear(shape, length, mid, dy, x, qkv, ctx, wup, wdn, wqkv, wout, lse, cnt, g1, b1, g2, b2, ub, db):
     tokens = mid.shape[0]
     nseq = shape["seq"]
     rows = tokens // length
-    nd = len(orders(shape)[0])
+    nd = len(orders(shape)["X"])
     vm, hb = pl.BlockSpec(memory_space=pltpu.VMEM), pl.BlockSpec(memory_space=pl.ANY)
     dma = pltpu.SemaphoreType.DMA
     V = pltpu.VMEM
@@ -682,9 +751,9 @@
         V((tokens, D), F32), V((tokens, D), BF), V((tokens, D), BF), V((D, tokens), BF), V((D, tokens), BF), V((tokens, D), F32),
         V((tokens, D), F32), V((2, D, fc), BF), V((2, fc, D), BF), V((tokens, 3 * D), BF), V((tokens, D), BF), V((tokens, D), BF),
         V((D, 3 * D), BF), V((D, D), BF), V((tokens, D), BF), V((D // LANE, D, LANE), BF), V((rows, length, D), BF), V((8, D), F32),
-        V((1, FF), F32), V((8, D), F32), dma((12,)), V((2, 2, NB, D, LANE), BF), V((nd, 16, D), F32), V((nd + 1, 16, D), F32),
+        V((1, FF), F32), V((8, D), F32), dma((12,)), V((2, 2, NB, D, LANE), BF), V((nd, 16, D), F32), V((nd + 1, 16, D), F32), V((8, D), F32), V((1, FF), F32),
         dma((NPAIR, 2, nd)), dma((NPAIR, 2, nd)), dma((NPAIR, 2, nd)), dma((NPAIR, 2, nd)), dma((NPAIR, 2)),
-        dma((nd,)), dma((nd,)), dma((nd,)), dma((nd,)), dma, dma((nd,)), dma((nd,)), dma((2, nseq)), dma((2, nseq)), dma((2,)),
+        dma((nd,)), dma((nd,)), dma((nd,)), dma((nd,)), dma, dma((nd,)), dma((nd,)), dma((2, rows, nseq)), dma((2, rows, nseq)), dma((2,)),
     ]
     scratch += land_shapes((NPAIR, 2), NB, D, 16, nd, BF)
     scratch += land_shapes((), cnt.shape[0], cnt.shape[1], 8, nd, jnp.int32)
@@ -702,7 +771,8 @@
     )(mid, dy, x, qkv, ctx, wup, wdn, wqkv, wout, lse, cnt, g1, b1, g2, b2, ub, db)
 
 
-def widen_kernel(src_ref, gm_ref, gmol_ref, qkv_out, out_out, up_out, down_out, wide_s, tall_s, sem):
+def widen_kernel(src_ref, gm_ref, lo_ref, vec_ref, cnt_ref, gmol_ref, lout_ref, counts_ref, g1_ref, b1_ref, qb_ref, ob_ref, g2_ref,
+                 b2_ref, ub_ref, db_ref, qkv_out, out_out, up_out, down_out, wide_s, tall_s, sem):
     j = pl.program_id(0)
     slot = j % 2
     fc = NB * LANE
@@ -737,6 +807,16 @@
         finish(j - 2, slot)
 
     gmol_ref[...] = gm_ref[...].astype(F32)
+    lout_ref[...] = lo_ref[...]
+
+    @pl.when(j == 0)
+    def _():
+        for n, ref in ((0, db_ref), (1, g2_ref), (2, b2_ref), (3, ob_ref), (4, g1_ref), (5, b1_ref)):
+            ref[...] = vec_ref[n : n + 1].reshape(D)
+        qb_ref[...] = vec_ref[6:8]
+        ub_ref[...] = jnp.concatenate([vec_ref[n : n + 1] for n in range(8, 12)], 1).reshape(FF)
+        for n in range(cnt_ref.shape[0]):
+            counts_ref[:, n * LANE : (n + 1) * LANE] = cnt_ref[n]
 
     @pl.when(j < NFF)
     def _():
@@ -761,37 +841,38 @@
         finish(j, slot)
 
 
-def widen(sums, gm):
+def widen(sums, gm, lo, vec, cnt):
     hb = pl.BlockSpec(memory_space=pl.ANY)
+    vm = pl.BlockSpec(memory_space=pltpu.VMEM)
     sds = jax.ShapeDtypeStruct
+    one = sds((D,), F32)
     rows = gm.shape[0]
     some = pl.BlockSpec((1,) + gm.shape[1:], lambda j: (jnp.minimum(j, rows - 1), 0, 0))
     return pl.pallas_call(
         widen_kernel,
         grid=(NPAIR,),
-        in_specs=[pl.BlockSpec((1, 2, NB, D, LANE), lambda j: (j, 0, 0, 0, 0)), some],
-        out_specs=[some, hb, hb, hb, hb],
-        out_shape=[sds(gm.shape, F32), sds((D, 3 * D), F32), sds((D, D), F32), sds((D, FF), F32), sds((FF, D), F32)],
+        in_specs=[pl.BlockSpec((1, 2, NB, D, LANE), lambda j: (j, 0, 0, 0, 0)), some, some, vm, vm],
+        out_specs=[some, some] + [vm] * 9 + [hb] * 4,
+        out_shape=[sds(gm.shape, F32), sds(lo.shape, BF), sds((cnt.shape[1], BUCKETS), jnp.int32), one, one, sds((2, D), F32), one, one,
+                   one, sds((FF,), F32), one, sds((D, 3 * D), F32), sds((D, D), F32), sds((D, FF), F32), sds((FF, D), F32)],
         scratch_shapes=[pltpu.VMEM((2, 2, D, NB * LANE), F32), pltpu.VMEM((2, NB * LANE, D), F32), pltpu.SemaphoreType.DMA((2, 4))],
         compiler_params=pltpu.CompilerParams(vmem_limit_bytes=60 * MIB),
         name="widen",
-    )(sums, gm)
+    )(sums, gm, lo, vec, cnt)
 
 
 def on_device(shape, molecules, ln1_gain, ln1_bias, w_qkv, qkv_bias, w_out, out_bias, ln2_gain, ln2_bias, w_up, up_bias,
               w_down, down_bias, out_cotangent, bucket_ids):
     width = molecules.shape[2]
     length = molecules.shape[1] * shape["seq"]
-    row = lambda a: a.reshape(1, -1)
-    qb = jnp.concatenate([qkv_bias[0], jnp.zeros((width,), F32), qkv_bias[1]]).reshape(1, -1)
-    x, dy, qkv, ctx, mid, lse, tally = front(shape, molecules, out_cotangent, w_qkv, w_out, bucket_ids, row(ln1_gain),
-                                             row(ln1_bias), qb, row(out_bias))
+    x, dy, qkv, ctx, mid, lse, tally = front(shape, molecules, out_cotangent, w_qkv, w_out, bucket_ids, ln1_gain, ln1_bias,
+                                             qkv_bias, out_bias)
     layer_out, gm, sums, counts, vec = rear(
         shape, length, mid, dy.reshape(-1, width), x.reshape(-1, width), qkv, ctx, w_up, w_down, w_qkv, w_out, lse, tally,
-        row(ln1_gain), row(ln1_bias), row(ln2_gain), row(ln2_bias), row(up_bias), row(down_bias))
-    g_mol, g_qkv, g_out, g_up, g_down = widen(sums, gm)
-    return (layer_out, g_mol, vec[4], vec[5], g_qkv, vec[6:8], g_out, vec[3], vec[1], vec[2],
-            g_up, vec[8:12].reshape(-1), g_down, vec[0], counts.reshape(bucket_ids.shape[0], BUCKETS))
+        ln1_gain, ln1_bias, ln2_gain, ln2_bias, up_bias, down_bias)
+    (g_mol, layer_out, counts, g_g1, g_b1, g_qb, g_ob, g_g2, g_b2, g_ub, g_db, g_qkv, g_out, g_up,
+     g_down) = widen(sums, gm, layer_out, vec, counts)
+    return (layer_out, g_mol, g_g1, g_b1, g_qkv, g_qb, g_out, g_ob, g_g2, g_b2, g_up, g_ub, g_down, g_db, counts)
 
 
 def solution(mesh):

time: 263 us -> 232 us (0.88)
  local copies, waits for them, and re-layouts: 16.7 us -> 0 us
  Pallas kernels: 245 us -> 231 us
    pallas_call x1, Pallas kernels: 185 us -> 170 us  [rear(): pl.pallas_call(functools.partial(rear_kernel, shape, length), in_specs=[h...]
    reshape x8 -> x0, local copies, waits for them, and re-layouts: 8.81 us -> none  [the longest x6 7.6 us: on_device(): row = lambda a: a.reshape(1, -1)]
    slice x4 -> x0, local copies, waits for them, and re-layouts: 4.61 us -> none  [the longest x1 1.74 us: on_device(): vec[0]]
    unnamed x4 -> x0, local copies, waits for them, and re-layouts: 3.29 us -> none
where the time goes in v4:
time: 232 us
  Pallas kernels  231 us (100%)
    pallas_call x1, Pallas kernels, rear(): pl.pallas_call(functools.partial(rear_kernel, shape, length), in_specs=[h...  170 us
    pallas_call x1, Pallas kernels, front(): pl.pallas_call(functools.partial(front_kernel, shape), in_specs=[hb] * 4...  41.5 us
    pallas_call x1, Pallas kernels, widen(): pl.pallas_call(widen_kernel, grid=(NPAIR,), in_specs=[pl.BlockSpec((1, 2,...  19.7 us

profile of v4, /device:TPU:0, one launch (start us, length us, event | category | flops | bytes accessed | tf_op | source)
XLA Modules:
  0.0 231.9 jit_solution(16817900741185777536)
XLA Ops:
  0.6 41.5 %front.1 = (bf16[2,512,768]{2,1,0:T(8,128)(2,1)}, bf16[2,512,768]{2,1,0:T(8,128)(2,1)}, bf16[1024,2304]{1,0:T(8,128)(2,1)}, bf16[1024,768]{1,0:T(8,128)(2,1)}, f...) custom-call(bf16[8,128,768]{2,1,0:T(8,128)(2,1)} %mol_h.1, bf16[8,128,768]{2,1,0:T(8,128)(2,1)} %cot_h.1, ...), custom_call_target="tpu_custom_call" | custom-call | tf_op jit(solution)/shard_map/front/pallas_call | solution.py:363
  42.2 169.8 %rear.1 = (bf16[8,128,768]{2,1,0:T(8,128)(2,1)}, bf16[8,128,768]{2,1,0:T(8,128)(2,1)}, bf16[9,2,4,768,128]{4,3,2,1,0:T(8,128)(2,1)}, s32[128,8,128]{2,1,0:T(8,128)}, f32[16,768]{1,0:T(8,128)}) custom-call(f32[1024,768]{1,0:T(8,128)} %get-tuple-element.42.mid_h, bf16[1024,768]{1,0:T(8,128)(2,1)} %bitcast.3, bf16[1024,768]{1,0:T(8,128)(2,1)} %bitcast.2, ...), custom_call_target="tpu_custom_call" | custom-call | tf_op jit(solution)/shard_map/rear/pallas_call | solution.py:761
  212.0 19.7 %widen.1 = (f32[8,128,768]{2,1,0:T(8,128)}, bf16[8,128,768]{2,1,0:T(8,128)(2,1)}, s32[8,16384]{1,0:T(8,128)}, f32[768]{0:T(1024)}, f32[768]{0:T(1024)}, /*index=...) custom-call(bf16[9,2,4,768,128]{4,3,2,1,0:T(8,128)(2,1)} %get-tuple-, ...), custom_call_target="tpu_custom_call" | custom-call | tf_op jit(solution)/shard_map/widen/pallas_call | solution.py:851

commit v5 on v4

v5 whole, which is shorter than its diff:
```python
import functools
import jax
import jax.numpy as jnp
from jax import lax
from jax.experimental import pallas as pl
from jax.experimental.pallas import tpu as pltpu
from jax.sharding import PartitionSpec as P

MESH = pl.DeviceIdType.MESH
BF = jnp.bfloat16
F32 = jnp.float32
EPS = 1e-5
D = 768
HD = 64
NH = 12
FF = 3072
BUCKETS = 16384
LANE = 128
MIB = 1 << 20


def dot_nn(a, b):
    return lax.dot_general(a, b, (((1,), (0,)), ((), ())), preferred_element_type=F32)


def dot_nt(a, b):
    return lax.dot_general(a, b, (((1,), (1,)), ((), ())), preferred_element_type=F32)


def dot_tn(a, b):
    return lax.dot_general(a, b, (((0,), (0,)), ((), ())), preferred_element_type=F32)


def norm_parts(x):
    mean = jnp.mean(x, -1, keepdims=True)
    cen = x - mean
    var = jnp.mean(cen * cen, -1, keepdims=True)
    rstd = lax.rsqrt(var + EPS)
    return cen * rstd, rstd


def norm_back(xhat, rstd, gain, dy):
    dxh = dy * gain
    m1 = jnp.mean(dxh, -1, keepdims=True)
    m2 = jnp.mean(dxh * xhat, -1, keepdims=True)
    return rstd * (dxh - m1 - xhat * m2)


def lane_half(shape, half):
    lane = lax.broadcasted_iota(jnp.int32, shape, 1)
    return (lane < HD) if half == 0 else (lane >= HD)


NB = 4
NFF = FF // (NB * LANE)
NPAIR = NFF + 3


def spots():
    return lax.axis_index("rows"), lax.axis_index("seq")


def bit_of(step):
    axis, mask = step
    return (lax.axis_index(axis) // mask) % 2


def across(step):
    axis, mask = step
    rows, seq = spots()
    move = mask - 2 * mask * bit_of(step)
    return (rows + move, seq) if axis == "rows" else (rows, seq + move)


def orders(shape):
    seq = [("seq", 1 << b) for b in range(shape["seq"].bit_length() - 1)]
    row = [("rows", 1 << b) for b in range(shape["rows"].bit_length() - 1)]
    first, rest, near, far = seq[:1], seq[1:], row[:1], row[1:]
    named = {"W": near + far + rest, "X": rest + near + far, "Y": near + rest + far, "Z": far + near + rest,
             "V": rest + far + near, "U": far + rest + near}
    return {name: first + then for name, then in named.items()}


class Halving:
    def __init__(self, order, lead, rows, tile):
        self.order, self.tile = order, tile
        self.size, self.split, self.lead_at, self.row_at, self.own = [], [], [], [], []
        lead_at, row_at = 0, 0
        for i, step in enumerate(order):
            bit = bit_of(step)
            if lead > 1:
                lead //= 2
                how = 0
                if i == 0:
                    self.first = bit * lead
                else:
                    lead_at = lead_at + bit * lead
            elif rows % (2 * tile) == 0:
                rows //= 2
                how = 1
                row_at = row_at + bit * rows
            else:
                how = None
            self.own.append(bit)
            self.split.append(how)
            self.size.append((lead, rows))
            self.lead_at.append(lead_at)
            self.row_at.append(row_at)
        self.gathers = [i for i in reversed(range(len(order))) if self.split[i] is not None]

    def partner(self, i):
        return across(self.order[i])

    def rows_of(self, at, size):
        return pl.ds(pl.multiple_of(at, self.tile), size)

    def send(self, i, mine, land, sems):
        lead, rows = self.size[i]
        if i == 0:
            src = mine.at[pl.ds(lead - self.first, lead)]
        else:
            la, ra = self.lead_at[i - 1], self.row_at[i - 1]
            if self.split[i] == 0:
                la = la + (1 - self.own[i]) * lead
            elif self.split[i] == 1:
                ra = ra + (1 - self.own[i]) * rows
            src = land[0].at[pl.ds(la, lead), self.rows_of(ra, rows)]
        return pltpu.make_async_remote_copy(src_ref=src, dst_ref=land[i], send_sem=sems[0].at[i], recv_sem=sems[1].at[i],
                                            device_id=self.partner(i), device_id_type=MESH)

    def add(self, i, mine, land):
        lead, rows = self.size[i]
        part = rows if rows <= LANE else 96
        wide = F32 if land[0].dtype == BF else land[0].dtype

        def some(t, carry):
            at = t * part
            if i == 0:
                here = (slice(None), self.rows_of(at, part))
                left, right = land[0][here], mine[pl.ds(self.first, lead), self.rows_of(at, part)]
            else:
                here = (pl.ds(self.lead_at[i], lead), self.rows_of(self.row_at[i] + at, part))
                left, right = land[0][here], land[i][:, self.rows_of(at, part)]
            land[0][here] = (left.astype(wide) + right.astype(wide)).astype(land[0].dtype)
            return carry

        lax.fori_loop(0, rows // part, some, 0)

    def at_level(self, i):
        lead, rows = self.size[i]
        return pl.ds(self.lead_at[i], lead), self.rows_of(self.row_at[i], rows)

    def out_level(self, i):
        lead, rows = self.size[i]
        return pl.ds(self.first + self.lead_at[i], lead), self.rows_of(self.row_at[i], rows)

    def keep(self, land, out, sem):
        last = len(self.order) - 1
        return pltpu.make_async_copy(land[0].at[self.at_level(last)], out.at[self.out_level(last)], sem)

    def gather(self, m, land, out, sems):
        i = self.gathers[m]
        here = out.at[self.out_level(i)]
        src = land[0].at[self.at_level(len(self.order) - 1)] if m == 0 else here
        return pltpu.make_async_remote_copy(src_ref=src, dst_ref=here, send_sem=sems[0].at[m], recv_sem=sems[1].at[m],
                                            device_id=self.partner(i), device_id_type=MESH)

    def reduce_step(self, k, mine, land, sems):
        n = len(self.order)
        if k > 0:
            self.send(k - 1, mine, land, sems).wait()
            self.add(k - 1, mine, land)
        if k < n:
            self.send(k, mine, land, sems).start()

    def gather_step(self, m, land, out, sems, sem):
        if m == 0:
            self.keep(land, out, sem).start()
        else:
            if m == 1:
                self.keep(land, out, sem).wait()
            self.gather(m - 1, land, out, sems).wait()
        if m < len(self.gathers):
            self.gather(m, land, out, sems).start()


def land_shapes(count, lead, rows, tile, steps, dtype):
    shapes = []
    for _ in range(steps):
        if lead > 1:
            lead //= 2
        elif rows % (2 * tile) == 0:
            rows //= 2
        shapes.append(pltpu.VMEM(count + (lead, rows, LANE), dtype))
    return shapes


def peers(nseq):
    me = lax.axis_index("seq")
    found = []
    for m in sorted(range(1, nseq), key=lambda m: -(m >> 1)):
        to = 0
        for b in range(nseq.bit_length() - 1):
            bit = (me // (1 << b)) % 2
            to = to + (bit + ((m >> b) & 1) * (1 - 2 * bit)) * (1 << b)
        found.append((m, to))
    return found


SPLIT = 2
TOGETHER = 2
MID = SPLIT * NFF
DRAIN = MID + 17
IN_AT = tuple(SPLIT * (j + 1) - 1 for j in range(NFF)) + (MID + 6, MID + 11, MID + 16)
COUNT_WAY = 'Y'
WAYS = (
    ('Y', 'W'), ('W', 'Y'), ('W', 'W'), ('X', 'Y'), ('Y', 'X'), ('X', 'W'), ('X', 'W'), ('X', 'W'), ('W', 'Z'),
)
REDUCE_AT = (
    ((1, 2, 4, 5, 6, 7), (1, 2, 5, 7, 9, 11)),
    ((3, 4, 7, 9, 11, 13), (3, 4, 8, 9, 11, 12)),
    ((5, 6, 9, 11, 13, 18), (5, 6, 10, 12, 14, 18)),
    ((7, 8, 11, 13, 14, 16), (7, 8, 11, 13, 14, 16)),
    ((9, 10, 12, 14, 16, 19), (9, 10, 12, 14, 18, 21)),
    ((11, 12, 16, 19, 21, 24), (11, 12, 16, 20, 24, 26)),
    ((18, 19, 24, 26, 28, 99), (18, 19, 23, 28, 99, 99)),
    ((23, 24, 28, 99, 99, 99), (23, 24, 28, 99, 99, 99)),
    ((28, 99, 99, 99, 99, 99), (28, 99, 99, 99, 99, 99)),
)
GATHER_AT = (
    ((7, 8, 9, 11, 14, 16), (11, 12, 14, 18, 21, 23)),
    ((13, 18, 21, 24, 99, 99), (12, 13, 16, 19, 24, 26)),
    ((18, 21, 26, 28, 99, 99), (18, 21, 26, 99, 99, 99)),
    ((16, 19, 22, 26, 99, 99), (16, 19, 23, 26, 99, 99)),
    ((99, 99, 99, 99, 99, 99), (99, 99, 99, 99, 99, 99)),
    ((24, 28, 99, 99, 99, 99), (26, 99, 99, 99, 99, 99)),
    ((99, 99, 99, 99, 99, 99), (99, 99, 99, 99, 99, 99)),
    ((99, 99, 99, 99, 99, 99), (99, 99, 99, 99, 99, 99)),
    ((99, 99, 99, 99, 99, 99), (99, 99, 99, 99, 99, 99)),
)
COUNT_AT = (0, 1, 3, 4, 5, 6, 21, 26, 99, 99, 99, 99)
BACK_AT = (13, 18, 19, 25)
LATE = (
    (3, 0, 0, 0), (1, 5, 1, 1), (1, 2, 1, 3), (1, 1, 0, 4), (2, 0, 0, 8), (0, 8, 0, 1), (0, 6, 0, 5), (0, 8, 1, 1), (3, 0, 0, 1),
    (1, 1, 0, 5), (0, 6, 1, 4), (1, 3, 0, 4), (1, 3, 1, 4), (0, 7, 1, 3), (1, 3, 0, 5), (1, 5, 0, 2), (1, 3, 1, 5), (0, 7, 0, 3),
    (1, 5, 1, 2), (1, 2, 0, 4), (0, 8, 1, 2), (1, 6, 0, 0), (1, 2, 0, 5), (0, 7, 0, 4), (0, 7, 1, 4), (1, 2, 1, 4), (1, 5, 1, 3),
    (1, 2, 1, 5), (0, 8, 0, 2), (0, 8, 1, 3), (1, 6, 0, 1), (1, 5, 0, 3), (1, 4, 0, 0), (1, 4, 1, 0), (0, 7, 0, 5), (2, 0, 0, 9),
    (3, 0, 0, 2), (0, 8, 0, 3), (0, 6, 1, 5), (1, 6, 1, 0), (0, 7, 1, 5), (1, 6, 0, 2), (1, 4, 0, 1), (1, 5, 1, 4), (1, 4, 1, 1),
    (0, 8, 1, 4), (1, 5, 1, 5), (1, 7, 0, 0), (1, 7, 1, 0), (1, 5, 0, 4), (0, 8, 0, 4), (1, 4, 0, 2), (1, 6, 1, 1), (0, 8, 1, 5),
    (1, 8, 1, 0), (2, 0, 0, 10), (1, 4, 1, 2), (1, 7, 1, 1), (1, 5, 0, 5), (3, 0, 0, 3), (1, 7, 0, 1), (0, 8, 0, 5), (1, 8, 0, 0),
    (2, 0, 0, 11), (1, 6, 0, 3), (1, 6, 1, 2), (1, 4, 0, 3), (1, 8, 1, 1), (1, 8, 0, 1), (1, 4, 1, 3), (3, 0, 0, 4), (1, 7, 1, 2),
    (1, 7, 0, 2), (1, 6, 1, 3), (1, 6, 0, 4), (1, 4, 0, 4), (1, 8, 1, 2), (1, 8, 0, 2), (1, 6, 0, 5), (1, 4, 0, 5), (1, 7, 0, 3),
    (3, 0, 0, 5), (1, 4, 1, 4), (1, 7, 1, 3), (1, 4, 1, 5), (1, 6, 1, 4), (1, 8, 0, 3), (1, 8, 1, 3), (1, 7, 0, 4), (1, 6, 1, 5),
    (1, 7, 0, 5), (1, 7, 1, 4), (1, 7, 1, 5), (1, 8, 1, 4), (1, 8, 0, 4), (1, 8, 1, 5), (1, 8, 0, 5),
)


def timetable(nd, gathers, tally_gathers):
    if nd == len(REDUCE_AT[0][0]) - 1:
        ticks = {}
        for j in range(NPAIR):
            for o in range(2):
                ticks |= {(0, j, o, k): t for k, t in enumerate(REDUCE_AT[j][o])}
                ticks |= {(1, j, o, m): t for m, t in enumerate(GATHER_AT[j][o])}
        ticks |= {(2, 0, 0, k): t for k, t in enumerate(COUNT_AT)}
        return {key: t for key, t in ticks.items() if t < DRAIN}, BACK_AT, list(LATE)
    ticks = {}
    for j, t in enumerate(IN_AT):
        for o in range(2):
            ticks |= {(0, j, o, k): t + 3 * k for k in range(nd + 1)}
            ticks |= {(1, j, o, m): max(t + 3 * nd, 20 + 2 * j) + 3 * m for m in range(gathers + 1)}
    ticks |= {(2, 0, 0, k): 2 * k for k in range(nd + 2 + tally_gathers)}
    late = sorted((t, key) for key, t in ticks.items() if t >= DRAIN)
    return {key: t for key, t in ticks.items() if t < DRAIN}, (MID + 1,) * 4, [(3, 0, 0, k) for k in range(nd + 1)] + [key for _, key in late]


def layer_kernel(shape, mol_h, cot_h, wup_h, wdn_h, wqkv_h, wout_h, ids_ref,
                 g1_in, b1_in, qb_ref, ob_in, g2_in, b2_in, ub_in, db_in,
                 lo_out, gm_out, sum_out, cnt_out, vec_out,
                 mid_s, dy_s, a2_s, a2t_s, dyt_s, acc_s, da2_s, wup_s, wdn_s, qkv_s, ctx_s, x_s, wqkv_s, wout_s,
                 dqkv_s, lo_s, gub_s, part_s, fetch_sem, stage_s, vland_s, vacc_s, six_s, ub_s, lacc, lse_s, cnt_s,
                 rs_send, rs_recv, ag_send, ag_recv, keep_sem, crs_send, crs_recv, cag_send, cag_recv, ckeep_sem,
                 v_send, v_recv, t_send, t_recv, t_own, m_send, m_recv, m_own, c_send, c_recv, c_own, *lands):
    ways = orders(shape)
    nd = len(ways["X"])
    nseq = shape["seq"]
    land = lands[:nd]
    cland = lands[nd:]
    rows_idx, me = spots()
    rows, length = x_s.shape[0], x_s.shape[1]
    tokens = rows * length
    local = length // nseq
    near = peers(nseq)
    fc = NB * LANE

    barrier = pltpu.get_barrier_semaphore()
    others = [across(step) for step in ways["X"]]
    others += [(rows_idx, to) for m, to in near if m & (m - 1)]
    for other in others:
        pl.semaphore_signal(barrier, inc=1, device_id=other, device_id_type=MESH)

    here = pl.ds(pl.multiple_of(me * local, local), local)

    def weights(i, slot):
        return (pltpu.make_async_copy(wup_h.at[:, pl.ds(pl.multiple_of(i * fc, fc), fc)], wup_s.at[slot], fetch_sem.at[slot]),
                pltpu.make_async_copy(wdn_h.at[pl.ds(pl.multiple_of(i * fc, fc), fc)], wdn_s.at[slot], fetch_sem.at[2 + slot]))

    fetch = [pltpu.make_async_copy(wqkv_h, wqkv_s, fetch_sem.at[4]), pltpu.make_async_copy(wout_h, wout_s, fetch_sem.at[5])]

    def own(r):
        return pltpu.make_async_copy(mol_h.at[me * rows + r], x_s.at[r, here], m_own.at[r])

    def mol(r, n):
        m, to = near[n]
        return pltpu.make_async_remote_copy(src_ref=mol_h.at[to * rows + r], dst_ref=x_s.at[r, here], send_sem=m_send.at[r, m],
                                            recv_sem=m_recv.at[r, m], device_id=(rows_idx, to), device_id_type=MESH)

    def cot(n):
        m, to = near[n]
        return pltpu.make_async_remote_copy(src_ref=cot_h.at[pl.ds(to * rows, rows)], dst_ref=dy_s.at[:, here],
                                            send_sem=c_send.at[m], recv_sem=c_recv.at[m], device_id=(rows_idx, to),
                                            device_id_type=MESH)

    cot_own = pltpu.make_async_copy(cot_h.at[pl.ds(me * rows, rows)], dy_s.at[:, here], c_own)
    for r in range(rows):
        own(r).start()
    fetch[0].start()
    for n, ref in enumerate((g1_in, b1_in, g2_in, b2_in, db_in, ob_in)):
        six_s[n : n + 1] = ref[...].reshape(1, D)
    ub_s[...] = ub_in[...].reshape(1, FF)
    g1_ref, b1_ref, g2_ref, b2_ref, db_ref, ob_ref = (six_s.at[n : n + 1] for n in range(6))
    ub_ref = ub_s
    pl.semaphore_wait(barrier, len(others))
    for r in range(rows):
        for n in range(len(near)):
            mol(r, n).start()
    fetch[1].start()
    cot_own.start()
    for copy in weights(0, 0):
        copy.start()


    def give_back(which, out, r, n):
        m, to = near[n]
        return pltpu.make_async_remote_copy(
            src_ref=lo_s.at[r, pl.ds(pl.multiple_of(to * local, local), local)], dst_ref=out.at[me * rows + r],
            send_sem=t_send.at[which, r, m], recv_sem=t_recv.at[which, r, m], device_id=(rows_idx, to), device_id_type=MESH)

    def give_self(which, out):
        return pltpu.make_async_copy(lo_s.at[:, pl.ds(pl.multiple_of(me * local, local), local)],
                                     out.at[pl.ds(me * rows, rows)], t_own.at[which])

    def give_wait(which, out):
        give_self(which, out).wait()
        for r in range(rows):
            for n in range(len(near)):
                give_back(which, out, r, n).wait()

    back = [(r, n) for r in range(rows) for n in range(len(near) - 1)]

    tally = Halving(ways[COUNT_WAY], cnt_s.shape[0], cnt_s.shape[1], 8)
    gathers = len(Halving(ways["X"], NB, D, 16).gathers)
    ticks, back_at, late = timetable(nd, gathers, len(tally.gathers))

    def act(kind, j, o, k, which):
        plan = Halving(ways[which], NB, D, 16)
        here = [r.at[j, o] for r in land]
        if kind == 0:
            plan.reduce_step(k, stage_s.at[j % 2, o], here, (rs_send.at[j, o], rs_recv.at[j, o]))
        else:
            plan.gather_step(k, here, sum_out.at[j, o], (ag_send.at[j, o], ag_recv.at[j, o]), keep_sem.at[j, o])

    def act_counts(k):
        if k <= nd:
            tally.reduce_step(k, cnt_s, cland, (crs_send, crs_recv))
        else:
            tally.gather_step(k - nd - 1, cland, cnt_out, (cag_send, cag_recv), ckeep_sem)

    def tick(t, low, high):
        for kind, most in ((0, nd), (1, gathers)):
            for k in reversed(range(most + 1)):
                for o in range(2):
                    for named in sorted(set(way[o] for way in WAYS)):
                        found = [(ticks.get((kind, j, o, k), -1), j) for j in range(NPAIR) if WAYS[j][o] == named]
                        found = [(at, j) for at, j in found if low <= at <= high]
                        assert len({at for at, _ in found}) == len(found)
                        if not found:
                            continue
                        hit = sum(jnp.where(t == at, 1, 0) for at, _ in found)
                        j = sum(jnp.where(t == at, j, 0) for at, j in found)

                        @pl.when(hit == 1)
                        def _():
                            act(kind, j, o, k, named)

        for k in range(nd + 2 + len(tally.gathers)):
            at = ticks.get((2, 0, 0, k), -1)
            if low <= at <= high:

                @pl.when(t == at)
                def _():
                    act_counts(k)

        for n, at in enumerate(back_at):
            if low <= at <= high:

                @pl.when(t == at)
                def _():
                    give_back(0, lo_out, *back[n]).start()

    half = 2 * local

    def project(r, at):
        src = pl.ds(pl.multiple_of(at, half), half)
        dst = pl.ds(pl.multiple_of(r * length + at, half), half)
        xhat, _ = norm_parts(x_s[r, src].astype(F32))
        a1 = (xhat * g1_ref[...] + b1_ref[...]).astype(BF)
        for c in range(3):
            cols = slice(c * D, (c + 1) * D)
            part = dot_nn(a1, wqkv_s[:, cols])
            qkv_s[dst, cols] = (part if c == 1 else part + qb_ref[c // 2 : c // 2 + 1]).astype(BF)

    for r in range(rows):
        own(r).wait()
        mol(r, len(near) - 1).wait()
    fetch[0].wait()
    mine = (me // 2) * half

    def early(r, carry):
        project(r, mine)
        return carry

    lax.fori_loop(0, rows, early, 0)

    hashes, id_rows, chars = ids_ref.shape
    high = BUCKETS // LANE

    def bucket(h, carry):
        total = jnp.zeros((high, LANE), F32)
        for r in range(id_rows):
            ids = ids_ref[h, r : r + 1, :]
            row = lax.broadcasted_iota(jnp.int32, (high, chars), 0)
            hi = jnp.where(row == (ids >> 7), 1.0, 0.0).astype(BF)
            lo = jnp.where(row == (ids & (LANE - 1)), 1.0, 0.0).astype(BF)
            total = total + dot_nt(hi, lo)
        cnt_s[:, pl.ds(h, 1), :] = total.astype(jnp.int32).reshape(high, 1, LANE)
        return carry

    lax.fori_loop(0, hashes, bucket, 0)
    fetch[1].wait()
    early_counts = [k for k, t in enumerate(COUNT_AT) if t < 0] if nd == len(COUNT_AT) // 2 - 1 else []

    for r in range(rows):
        for n in range(len(near) - 1):
            mol(r, n).wait()
        for other in range(1, nseq // 2):
            project(r, ((me // 2 + other) % (nseq // 2)) * half)
        tok = slice(r * length, (r + 1) * length)

        def pair(p):
            at = pl.multiple_of(p * LANE, LANE)
            q = qkv_s[tok, pl.ds(at, LANE)] * BF(0.125)
            k = qkv_s[tok, pl.ds(pl.multiple_of(D + at, LANE), LANE)]
            v = qkv_s[tok, pl.ds(pl.multiple_of(2 * D + at, LANE), LANE)]
            ctx = []
            lse = lacc[...]
            lane = lax.broadcasted_iota(jnp.int32, lse.shape, 1)
            for half_of in range(2):
                qm = jnp.where(lane_half(q.shape, half_of), q, BF(0))
                s = dot_nt(qm, k)
                m = jnp.max(s, -1, keepdims=True)
                e = jnp.exp(s - m)
                t = jnp.sum(e, -1, keepdims=True)
                pr = (e * (1.0 / t)).astype(BF)
                ctx.append(dot_nn(pr, v))
                lse = jnp.where(lane == 2 * p + half_of, m + jnp.log(t), lse)
            lacc[...] = lse
            ctx_s[tok, pl.ds(at, LANE)] = jnp.where(lane_half(ctx[0].shape, 0), ctx[0], ctx[1]).astype(BF)

        lacc[...] = jnp.zeros_like(lacc)
        def some(i, carry):
            for n in range(TOGETHER):
                pair(TOGETHER * i + n)
            return carry

        ends = (0, 4 // TOGETHER, NH // (2 * TOGETHER))
        for part in range(2):
            lax.fori_loop(ends[part], ends[part + 1], some, 0)
            if r == 0 and part == 0:
                for n in range(len(near)):
                    cot(n).start()
            if 2 * r + part in early_counts:
                act_counts(2 * r + part)
        lt = lacc[...].T
        for h in range(NH):
            lse_s[r * NH + h] = lt[h : h + 1, :]
        mid_s[tok] = x_s[r].astype(F32) + (dot_nn(ctx_s[tok], wout_s[...]) + ob_ref[...])

    step = 256
    pieces = tokens // step

    def piece(n):
        at = pl.ds(pl.multiple_of(n * step, step), step)
        return at, (n * step // length, pl.ds(pl.multiple_of((n * step) % length, step), step))

    cot_own.wait()
    for n in range(len(near)):
        cot(n).wait()

    def open_piece(n, carry):
        at, row_at = piece(n)
        mid = mid_s[at]
        xhat, _ = norm_parts(mid)
        a2 = (xhat * g2_ref[...] + b2_ref[...]).astype(BF)
        a2_s[at] = a2
        a2t_s[:, at] = a2.T
        dyt_s[:, at] = dy_s[row_at].T
        acc_s[at] = mid + db_ref[...]
        da2_s[at] = jnp.zeros((step, D), F32)
        return carry

    lax.fori_loop(0, pieces, open_piece, 0)

    def ff(i, carry):
        slot = i % 2

        @pl.when(i + 1 < NFF)
        def _():
            for copy in weights(i + 1, 1 - slot):
                copy.start()

        for copy in weights(i, slot):
            copy.wait()
        cols = pl.ds(pl.multiple_of(i * fc, fc), fc)
        u = dot_nn(a2_s[...], wup_s[slot]) + ub_ref[:, cols]
        dh = dot_nt(dy_s[...].reshape(tokens, D), wdn_s[slot])
        cdf = 0.5 + 0.5 * lax.erf(u * (2.0 ** -0.5))
        pdf = jnp.exp(u * u * -0.5) * 0.3989422804014327
        hid = (u * cdf).astype(BF)
        du = (dh * (cdf + u * pdf)).astype(BF)
        gub_s[:, cols] = jnp.sum(du.astype(F32), 0, keepdims=True)
        tick(SPLIT * i, 0, MID - 1)
        acc_s[...] += dot_nn(hid, wdn_s[slot])
        da2_s[...] += dot_nt(du, wup_s[slot])
        gd = dot_nn(dyt_s[...], hid).astype(BF)
        gu = dot_nn(a2t_s[...], du).astype(BF)
        for b in range(NB):
            stage_s[slot, 0, b] = gd[:, b * LANE : (b + 1) * LANE]
            stage_s[slot, 1, b] = gu[:, b * LANE : (b + 1) * LANE]
        tick(SPLIT * i + SPLIT - 1, 0, MID - 1)
        return carry

    lax.fori_loop(0, NFF, ff, 0)

    part_s[...] = jnp.zeros_like(part_s)

    def turn_piece(n, carry):
        at, row_at = piece(n)
        lo_s[row_at] = acc_s[at].astype(BF)
        dy = dy_s[row_at].astype(F32)
        xhat, rstd = norm_parts(mid_s[at])
        da2 = da2_s[at]
        dx2 = dy + norm_back(xhat, rstd, g2_ref[...], da2)
        da2_s[at] = dx2
        do = dx2.astype(BF)
        a2_s[at] = do
        part_s[0:1] += jnp.sum(dy, 0, keepdims=True)
        part_s[1:2] += jnp.sum(da2 * xhat, 0, keepdims=True)
        part_s[2:3] += jnp.sum(da2, 0, keepdims=True)
        part_s[3:4] += jnp.sum(do.astype(F32), 0, keepdims=True)
        dy_s[row_at] = dot_nt(do, wout_s[...]).astype(BF)
        return carry

    lax.fori_loop(0, pieces, turn_piece, 0)
    dctx_s, do_s, dx2_s, da1_s, a1t_s = dy_s, a2_s, da2_s, acc_s, a2t_s
    give_self(0, lo_out).start()
    for r in range(rows):
        give_back(0, lo_out, r, len(near) - 1).start()
    tick(MID, MID, MID)
    gout_s = dyt_s
    gout_s[:, 0:D] = dot_tn(ctx_s[...], do_s[...]).astype(BF)

    def first_norm(n, carry):
        at, row_at = piece(n)
        xhat, _ = norm_parts(x_s[row_at].astype(F32))
        a1t_s[:, at] = (xhat * g1_ref[...] + b1_ref[...]).astype(BF).T
        da1_s[at] = jnp.zeros((step, D), F32)
        return carry

    lax.fori_loop(0, pieces, first_norm, 0)
    tick(MID + 1, MID + 1, MID + 1)

    def group(g, carry):
        def unit(r, h):
            p = 2 * g + h
            tok = pl.ds(pl.multiple_of(r * length, length), length)
            cq = pl.ds(pl.multiple_of(p * LANE, LANE), LANE)
            q = qkv_s[tok, cq] * BF(0.125)
            k = qkv_s[tok, pl.ds(pl.multiple_of(p * LANE + D, LANE), LANE)]
            v = qkv_s[tok, pl.ds(pl.multiple_of(p * LANE + 2 * D, LANE), LANE)]
            dc = dctx_s[r, :, cq]
            dqs, dks, dvs = [], [], []
            for half in range(2):
                keep = lane_half(k.shape, half)
                km = jnp.where(keep, k, BF(0))
                vm = jnp.where(keep, v, BF(0))
                lse = lse_s[r * NH + 2 * p + half]
                st = dot_nt(km, q)
                pt = jnp.exp(st - lse)
                dpt = dot_nt(vm, dc)
                inner = jnp.sum(pt * dpt, 0, keepdims=True)
                dst = (pt * (dpt - inner)).astype(BF)
                dvs.append(dot_nn(pt.astype(BF), dc))
                dks.append(dot_nn(dst, q))
                dqs.append(dot_tn(dst, k))
            sel = lane_half(dqs[0].shape, 0)
            dqkv_s[tok, pl.ds(pl.multiple_of(h * LANE, LANE), LANE)] = (jnp.where(sel, dqs[0], dqs[1]) * 0.125).astype(BF)
            dqkv_s[tok, pl.ds(pl.multiple_of(h * LANE + 2 * LANE, LANE), LANE)] = jnp.where(sel, dks[0], dks[1]).astype(BF)
            dqkv_s[tok, pl.ds(pl.multiple_of(h * LANE + 4 * LANE, LANE), LANE)] = jnp.where(sel, dvs[0], dvs[1]).astype(BF)

        def both_halves(n, inner_carry):
            unit(n, 0)
            unit(n, 1)
            tick(MID + 2 + 5 * g + 2 * n, MID + 2, DRAIN - 1)
            tick(MID + 3 + 5 * g + 2 * n, MID + 2, DRAIN - 1)
            return inner_carry

        lax.fori_loop(0, rows, both_halves, 0)
        slot = (NFF + g) % 2
        grads = dot_nn(a1t_s[...], dqkv_s[...]).astype(BF)
        for b in range(6):
            stage_s[slot, b // NB, b % NB] = grads[:, b * LANE : (b + 1) * LANE]
        for b in range(2):
            stage_s[slot, 1, 2 + b] = gout_s[:, pl.ds(pl.multiple_of((2 * g + b) * LANE, LANE), LANE)]
        two = 2 * LANE
        for c in range(3):
            at = pl.ds(pl.multiple_of(c * D + g * two, two), two)
            da1_s[...] += dot_nt(dqkv_s[:, c * two : (c + 1) * two], wqkv_s[:, at])
        here = pl.ds(pl.multiple_of(g * two, two), two)
        part_s[6:7, here] = jnp.sum(dqkv_s[:, 0:two].astype(F32), 0, keepdims=True)
        part_s[7:8, here] = jnp.sum(dqkv_s[:, 2 * two : 3 * two].astype(F32), 0, keepdims=True)
        tick(MID + 6 + 5 * g, MID + 2, DRAIN - 1)
        return carry

    lax.fori_loop(0, 3, group, 0)

    give_wait(0, lo_out)

    def last_piece(n, carry):
        at, row_at = piece(n)
        xhat, rstd = norm_parts(x_s[row_at].astype(F32))
        da1 = da1_s[at]
        part_s[4:5] += jnp.sum(da1 * xhat, 0, keepdims=True)
        part_s[5:6] += jnp.sum(da1, 0, keepdims=True)
        gm = dx2_s[at] + norm_back(xhat, rstd, g1_ref[...], da1)
        lo_s[row_at] = gm.astype(BF)
        return carry

    lax.fori_loop(0, pieces, last_piece, 0)
    give_self(1, gm_out).start()
    for r in range(rows):
        for n in range(len(near)):
            give_back(1, gm_out, r, n).start()
    vacc_s[0, 0:8] = part_s[...]
    for b in range(FF // (2 * LANE)):
        vacc_s[0, 8 + b // 3 : 9 + b // 3, (b % 3) * 2 * LANE : (b % 3 + 1) * 2 * LANE] = gub_s[:, b * 2 * LANE : (b + 1) * 2 * LANE]
    vacc_s[0, 12:16] = jnp.zeros((4, D), F32)

    def swap(i):
        return pltpu.make_async_remote_copy(src_ref=vacc_s.at[i], dst_ref=vland_s.at[i], send_sem=v_send.at[i], recv_sem=v_recv.at[i],
                                            device_id=across(ways["X"][i]), device_id_type=MESH)

    for kind, j, o, k in late:
        if kind < 2:
            act(kind, j, o, k, WAYS[j][o])
        elif kind == 2:
            act_counts(k)
        else:
            if k > 0:
                swap(k - 1).wait()
                vacc_s[k] = vacc_s[k - 1] + vland_s[k - 1]
            if k < nd:
                swap(k).start()
    vec_out[...] = vacc_s[nd]
    give_wait(1, gm_out)


def layer(shape, mol, cot, wup, wdn, wqkv, wout, ids, g1, b1, qb, ob, g2, b2, ub, db):
    nseq = shape["seq"]
    local = mol.shape[1]
    rows, length = mol.shape[0] // nseq, local * nseq
    tokens = rows * length
    nd = len(orders(shape)["X"])
    vm, hb = pl.BlockSpec(memory_space=pltpu.VMEM), pl.BlockSpec(memory_space=pl.ANY)
    dma = pltpu.SemaphoreType.DMA
    V = pltpu.VMEM
    sds = jax.ShapeDtypeStruct
    fc = NB * LANE
    cnt = (BUCKETS // LANE, ids.shape[0], LANE)
    scratch = [
        V((tokens, D), F32), V((rows, length, D), BF), V((tokens, D), BF), V((D, tokens), BF), V((D, tokens), BF), V((tokens, D), F32),
        V((tokens, D), F32), V((2, D, fc), BF), V((2, fc, D), BF), V((tokens, 3 * D), BF), V((tokens, D), BF), V((rows, length, D), BF),
        V((D, 3 * D), BF), V((D, D), BF), V((tokens, D), BF), V((rows, length, D), BF),
        V((1, FF), F32), V((8, D), F32), dma((6,)), V((2, 2, NB, D, LANE), BF), V((nd, 16, D), F32), V((nd + 1, 16, D), F32),
        V((8, D), F32), V((1, FF), F32), V((length, LANE), F32), V((rows * NH, 1, length), F32), V(cnt, jnp.int32),
        dma((NPAIR, 2, nd)), dma((NPAIR, 2, nd)), dma((NPAIR, 2, nd)), dma((NPAIR, 2, nd)), dma((NPAIR, 2)),
        dma((nd,)), dma((nd,)), dma((nd,)), dma((nd,)), dma, dma((nd,)), dma((nd,)), dma((2, rows, nseq)), dma((2, rows, nseq)), dma((2,)),
        dma((rows, nseq)), dma((rows, nseq)), dma((rows,)), dma((nseq,)), dma((nseq,)), dma,
    ]
    scratch += land_shapes((NPAIR, 2), NB, D, 16, nd, BF)
    scratch += land_shapes((), cnt[0], cnt[1], 8, nd, jnp.int32)
    return pl.pallas_call(
        functools.partial(layer_kernel, shape),
        in_specs=[hb] * 6 + [vm] * 9,
        out_specs=[hb, hb, hb, hb, vm],
        out_shape=[sds((rows * nseq, local, D), BF), sds((rows * nseq, local, D), BF), sds((NPAIR, 2, NB, D, LANE), BF),
                   sds(cnt, jnp.int32), sds((16, D), F32)],
        scratch_shapes=scratch,
        compiler_params=pltpu.CompilerParams(vmem_limit_bytes=63 * MIB, collective_id=0, has_side_effects=True),
        name="layer",
    )(mol, cot, wup, wdn, wqkv, wout, ids, g1, b1, qb, ob, g2, b2, ub, db)


def widen_kernel(src_ref, gm_ref, lo_ref, vec_ref, cnt_ref, gmol_ref, lout_ref, counts_ref, g1_ref, b1_ref, qb_ref, ob_ref, g2_ref,
                 b2_ref, ub_ref, db_ref, qkv_out, out_out, up_out, down_out, wide_s, tall_s, sem):
    j = pl.program_id(0)
    slot = j % 2
    fc = NB * LANE
    two = 2 * LANE

    def first(i, s):
        at = pl.ds(pl.multiple_of(i * fc, fc), fc)
        return [pltpu.make_async_copy(tall_s.at[s], down_out.at[at], sem.at[s, 0]),
                pltpu.make_async_copy(wide_s.at[s, 0], up_out.at[:, at], sem.at[s, 1])]

    def later(i, s):
        g = i - NFF
        to = lambda c: pl.ds(pl.multiple_of(c * D + g * two, two), two)
        return [pltpu.make_async_copy(wide_s.at[s, 0, :, 0:two], qkv_out.at[:, to(0)], sem.at[s, 0]),
                pltpu.make_async_copy(wide_s.at[s, 0, :, two : 2 * two], qkv_out.at[:, to(1)], sem.at[s, 1]),
                pltpu.make_async_copy(wide_s.at[s, 1, :, 0:two], qkv_out.at[:, to(2)], sem.at[s, 2]),
                pltpu.make_async_copy(wide_s.at[s, 1, :, two : 2 * two], out_out.at[:, to(0)], sem.at[s, 3])]

    def finish(i, s):
        @pl.when(i < NFF)
        def _():
            for copy in first(i, s):
                copy.wait()

        @pl.when(i >= NFF)
        def _():
            for copy in later(i, s):
                copy.wait()

    @pl.when(j >= 2)
    def _():
        finish(j - 2, slot)

    gmol_ref[...] = gm_ref[...].astype(F32)
    lout_ref[...] = lo_ref[...]

    @pl.when(j == 0)
    def _():
        for n, ref in ((0, db_ref), (1, g2_ref), (2, b2_ref), (3, ob_ref), (4, g1_ref), (5, b1_ref)):
            ref[...] = vec_ref[n : n + 1].reshape(D)
        qb_ref[...] = vec_ref[6:8]
        ub_ref[...] = jnp.concatenate([vec_ref[n : n + 1] for n in range(8, 12)], 1).reshape(FF)
        for n in range(cnt_ref.shape[0]):
            counts_ref[:, n * LANE : (n + 1) * LANE] = cnt_ref[n]

    @pl.when(j < NFF)
    def _():
        for b in range(NB):
            at = slice(b * LANE, (b + 1) * LANE)
            tall_s[slot, at, :] = src_ref[0, 0, b].astype(F32).T
            wide_s[slot, 0, :, at] = src_ref[0, 1, b].astype(F32)
        for copy in first(j, slot):
            copy.start()

    @pl.when(j >= NFF)
    def _():
        for o in range(2):
            for b in range(NB):
                wide_s[slot, o, :, b * LANE : (b + 1) * LANE] = src_ref[0, o, b].astype(F32)
        for copy in later(j, slot):
            copy.start()

    @pl.when(j == NPAIR - 1)
    def _():
        finish(j - 1, 1 - slot)
        finish(j, slot)


def widen(sums, gm, lo, vec, cnt):
    hb = pl.BlockSpec(memory_space=pl.ANY)
    vm = pl.BlockSpec(memory_space=pltpu.VMEM)
    sds = jax.ShapeDtypeStruct
    one = sds((D,), F32)
    rows = gm.shape[0]
    some = pl.BlockSpec((1,) + gm.shape[1:], lambda j: (jnp.minimum(j, rows - 1), 0, 0))
    return pl.pallas_call(
        widen_kernel,
        grid=(NPAIR,),
        in_specs=[pl.BlockSpec((1, 2, NB, D, LANE), lambda j: (j, 0, 0, 0, 0)), some, some, vm, vm],
        out_specs=[some, some] + [vm] * 9 + [hb] * 4,
        out_shape=[sds(gm.shape, F32), sds(lo.shape, BF), sds((cnt.shape[1], BUCKETS), jnp.int32), one, one, sds((2, D), F32), one, one,
                   one, sds((FF,), F32), one, sds((D, 3 * D), F32), sds((D, D), F32), sds((D, FF), F32), sds((FF, D), F32)],
        scratch_shapes=[pltpu.VMEM((2, 2, D, NB * LANE), F32), pltpu.VMEM((2, NB * LANE, D), F32), pltpu.SemaphoreType.DMA((2, 4))],
        compiler_params=pltpu.CompilerParams(vmem_limit_bytes=60 * MIB),
        name="widen",
    )(sums, gm, lo, vec, cnt)


def on_device(shape, molecules, ln1_gain, ln1_bias, w_qkv, qkv_bias, w_out, out_bias, ln2_gain, ln2_bias, w_up, up_bias,
              w_down, down_bias, out_cotangent, bucket_ids):
    layer_out, gm, sums, counts, vec = layer(shape, molecules, out_cotangent, w_up, w_down, w_qkv, w_out, bucket_ids, ln1_gain, ln1_bias,
                                             qkv_bias, out_bias, ln2_gain, ln2_bias, up_bias, down_bias)
    (g_mol, layer_out, counts, g_g1, g_b1, g_qb, g_ob, g_g2, g_b2, g_ub, g_db, g_qkv, g_out, g_up,
     g_down) = widen(sums, gm, layer_out, vec, counts)
    return (layer_out, g_mol, g_g1, g_b1, g_qkv, g_qb, g_out, g_ob, g_g2, g_b2, g_up, g_ub, g_down, g_db, counts)


def solution(mesh):
    tok = P("rows", "seq", None)
    return jax.shard_map(
        functools.partial(on_device, dict(mesh.shape)),
        mesh=mesh,
        in_specs=(tok,) + (P(),) * 12 + (tok, P(None, "rows", "seq")),
        out_specs=(tok, tok) + (P(),) * 13,
        check_vma=False,
    )
```

time: 232 us -> 220 us (0.948)
  Pallas kernels: 231 us -> 218 us
    pallas_call x2 -> x1, Pallas kernels: 211 us -> 199 us  [layer(): pl.pallas_call(functools.partial(layer_kernel, shape), in_specs=[hb] * 6...]
where the time goes in v5:
time: 220 us; the launch traced here: 219 us
  Pallas kernels  218 us (99%)
    pallas_call x1, Pallas kernels, layer(): pl.pallas_call(functools.partial(layer_kernel, shape), in_specs=[hb] * 6...  199 us
    pallas_call x1, Pallas kernels, widen(): pl.pallas_call(widen_kernel, grid=(NPAIR,), in_specs=[pl.BlockSpec((1, 2,...  19.7 us

profile of v5, /device:TPU:0, one launch (start us, length us, event | category | flops | bytes accessed | tf_op | source)
XLA Modules:
  0.0 219.3 jit_solution(14324792992828695090)
XLA Ops:
  0.7 198.8 %layer.1 = (bf16[8,128,768]{2,1,0:T(8,128)(2,1)}, bf16[8,128,768]{2,1,0:T(8,128)(2,1)}, bf16[9,2,4,768,128]{4,3,2,1,0:T(8,128)(2,1)}, s32[128,8,128]{2,1,0:T(8,128)}, f32[16,768]{1,0:T(8,128)}) custom-call(bf16[8,128,768]{2,1,0:T(8,128)(2,1)} %mol_h.1, bf16[8,128,768]{2,1,0:T(8,128)(2,1)} %cot_h.1, bf16[768,3072]{1,0:T(8,128)(2,1)} %wup_h.1, ...), custom_call_target="tpu_custom_call" | custom-call | tf_op jit(solution)/shard_map/layer/pallas_call | solution.py:712
  199.4 19.7 %widen.1 = (f32[8,128,768]{2,1,0:T(8,128)}, bf16[8,128,768]{2,1,0:T(8,128)(2,1)}, s32[8,16384]{1,0:T(8,128)}, f32[768]{0:T(1024)}, f32[768]{0:T(1024)}, /*index=...) custom-call(bf16[9,2,4,768,128]{4,3,2,1,0:T(8,128)(2,1)} %get-tuple-, ...), custom_call_target="tpu_custom_call" | custom-call | tf_op jit(solution)/shard_map/widen/pallas_call | solution.py:801

commit v6 on v5

--- a/solution.py
+++ b/solution.py
@@ -212,46 +212,46 @@
 MID = SPLIT * NFF
 DRAIN = MID + 17
 IN_AT = tuple(SPLIT * (j + 1) - 1 for j in range(NFF)) + (MID + 6, MID + 11, MID + 16)
-COUNT_WAY = 'Y'
+COUNT_WAY = 'U'
 WAYS = (
-    ('Y', 'W'), ('W', 'Y'), ('W', 'W'), ('X', 'Y'), ('Y', 'X'), ('X', 'W'), ('X', 'W'), ('X', 'W'), ('W', 'Z'),
+    ('Y', 'Y'), ('Y', 'X'), ('Z', 'W'), ('W', 'Y'), ('X', 'Y'), ('W', 'Y'), ('W', 'W'), ('Y', 'V'), ('Z', 'X'),
 )
 REDUCE_AT = (
-    ((1, 2, 4, 5, 6, 7), (1, 2, 5, 7, 9, 11)),
-    ((3, 4, 7, 9, 11, 13), (3, 4, 8, 9, 11, 12)),
-    ((5, 6, 9, 11, 13, 18), (5, 6, 10, 12, 14, 18)),
-    ((7, 8, 11, 13, 14, 16), (7, 8, 11, 13, 14, 16)),
-    ((9, 10, 12, 14, 16, 19), (9, 10, 12, 14, 18, 21)),
-    ((11, 12, 16, 19, 21, 24), (11, 12, 16, 20, 24, 26)),
-    ((18, 19, 24, 26, 28, 99), (18, 19, 23, 28, 99, 99)),
-    ((23, 24, 28, 99, 99, 99), (23, 24, 28, 99, 99, 99)),
+    ((1, 2, 4, 6, 7, 9), (1, 2, 6, 8, 9, 11)),
+    ((3, 4, 7, 9, 11, 13), (3, 4, 7, 9, 11, 13)),
+    ((5, 6, 8, 10, 12, 13), (5, 6, 8, 10, 12, 13)),
+    ((7, 8, 10, 12, 14, 18), (7, 8, 11, 13, 15, 18)),
+    ((9, 10, 12, 13, 16, 18), (9, 10, 13, 17, 19, 21)),
+    ((11, 12, 15, 18, 21, 26), (11, 12, 17, 21, 25, 28)),
+    ((18, 19, 24, 28, 99, 99), (18, 19, 26, 99, 99, 99)),
+    ((23, 24, 99, 99, 99, 99), (23, 24, 99, 99, 99, 99)),
     ((28, 99, 99, 99, 99, 99), (28, 99, 99, 99, 99, 99)),
 )
 GATHER_AT = (
-    ((7, 8, 9, 11, 14, 16), (11, 12, 14, 18, 21, 23)),
-    ((13, 18, 21, 24, 99, 99), (12, 13, 16, 19, 24, 26)),
-    ((18, 21, 26, 28, 99, 99), (18, 21, 26, 99, 99, 99)),
-    ((16, 19, 22, 26, 99, 99), (16, 19, 23, 26, 99, 99)),
-    ((99, 99, 99, 99, 99, 99), (99, 99, 99, 99, 99, 99)),
-    ((24, 28, 99, 99, 99, 99), (26, 99, 99, 99, 99, 99)),
+    ((9, 10, 12, 14, 19, 21), (11, 12, 14, 18, 21, 23)),
+    ((13, 14, 16, 19, 28, 99), (13, 14, 16, 19, 24, 26)),
+    ((13, 16, 19, 23, 28, 99), (13, 16, 19, 23, 28, 99)),
+    ((18, 21, 26, 99, 99, 99), (18, 19, 24, 99, 99, 99)),
+    ((18, 19, 24, 99, 99, 99), (21, 24, 28, 99, 99, 99)),
+    ((26, 99, 99, 99, 99, 99), (28, 99, 99, 99, 99, 99)),
     ((99, 99, 99, 99, 99, 99), (99, 99, 99, 99, 99, 99)),
     ((99, 99, 99, 99, 99, 99), (99, 99, 99, 99, 99, 99)),
     ((99, 99, 99, 99, 99, 99), (99, 99, 99, 99, 99, 99)),
 )
-COUNT_AT = (0, 1, 3, 4, 5, 6, 21, 26, 99, 99, 99, 99)
-BACK_AT = (13, 18, 19, 25)
+COUNT_AT = (-1, -1, -1, -1, 0, 1, 1, 2, 3, 5, 7, 8)
+BACK_AT = (21, 13, 17, 22)
 LATE = (
-    (3, 0, 0, 0), (1, 5, 1, 1), (1, 2, 1, 3), (1, 1, 0, 4), (2, 0, 0, 8), (0, 8, 0, 1), (0, 6, 0, 5), (0, 8, 1, 1), (3, 0, 0, 1),
-    (1, 1, 0, 5), (0, 6, 1, 4), (1, 3, 0, 4), (1, 3, 1, 4), (0, 7, 1, 3), (1, 3, 0, 5), (1, 5, 0, 2), (1, 3, 1, 5), (0, 7, 0, 3),
-    (1, 5, 1, 2), (1, 2, 0, 4), (0, 8, 1, 2), (1, 6, 0, 0), (1, 2, 0, 5), (0, 7, 0, 4), (0, 7, 1, 4), (1, 2, 1, 4), (1, 5, 1, 3),
-    (1, 2, 1, 5), (0, 8, 0, 2), (0, 8, 1, 3), (1, 6, 0, 1), (1, 5, 0, 3), (1, 4, 0, 0), (1, 4, 1, 0), (0, 7, 0, 5), (2, 0, 0, 9),
-    (3, 0, 0, 2), (0, 8, 0, 3), (0, 6, 1, 5), (1, 6, 1, 0), (0, 7, 1, 5), (1, 6, 0, 2), (1, 4, 0, 1), (1, 5, 1, 4), (1, 4, 1, 1),
-    (0, 8, 1, 4), (1, 5, 1, 5), (1, 7, 0, 0), (1, 7, 1, 0), (1, 5, 0, 4), (0, 8, 0, 4), (1, 4, 0, 2), (1, 6, 1, 1), (0, 8, 1, 5),
-    (1, 8, 1, 0), (2, 0, 0, 10), (1, 4, 1, 2), (1, 7, 1, 1), (1, 5, 0, 5), (3, 0, 0, 3), (1, 7, 0, 1), (0, 8, 0, 5), (1, 8, 0, 0),
-    (2, 0, 0, 11), (1, 6, 0, 3), (1, 6, 1, 2), (1, 4, 0, 3), (1, 8, 1, 1), (1, 8, 0, 1), (1, 4, 1, 3), (3, 0, 0, 4), (1, 7, 1, 2),
-    (1, 7, 0, 2), (1, 6, 1, 3), (1, 6, 0, 4), (1, 4, 0, 4), (1, 8, 1, 2), (1, 8, 0, 2), (1, 6, 0, 5), (1, 4, 0, 5), (1, 7, 0, 3),
-    (3, 0, 0, 5), (1, 4, 1, 4), (1, 7, 1, 3), (1, 4, 1, 5), (1, 6, 1, 4), (1, 8, 0, 3), (1, 8, 1, 3), (1, 7, 0, 4), (1, 6, 1, 5),
-    (1, 7, 0, 5), (1, 7, 1, 4), (1, 7, 1, 5), (1, 8, 1, 4), (1, 8, 0, 4), (1, 8, 1, 5), (1, 8, 0, 5),
+    (3, 0, 0, 0), (0, 7, 1, 2), (0, 6, 1, 3), (0, 8, 0, 1), (0, 8, 1, 1), (1, 3, 1, 3), (1, 3, 0, 3), (4, 0, 0, 0), (1, 5, 0, 1),
+    (1, 1, 0, 5), (1, 5, 1, 1), (1, 2, 0, 5), (0, 7, 0, 2), (1, 2, 1, 5), (3, 0, 0, 1), (1, 4, 1, 3), (4, 0, 0, 1), (0, 6, 0, 4),
+    (1, 4, 0, 3), (0, 7, 1, 3), (0, 6, 1, 4), (0, 8, 1, 2), (1, 3, 1, 4), (1, 3, 1, 5), (0, 8, 0, 2), (1, 5, 1, 2), (1, 5, 0, 2),
+    (1, 3, 0, 4), (0, 7, 0, 3), (1, 3, 0, 5), (0, 7, 1, 4), (3, 0, 0, 2), (1, 4, 1, 4), (1, 4, 1, 5), (0, 8, 0, 3), (1, 5, 0, 3),
+    (0, 8, 1, 3), (0, 7, 1, 5), (0, 6, 0, 5), (1, 6, 0, 0), (1, 7, 1, 0), (0, 7, 0, 4), (3, 0, 0, 3), (0, 8, 0, 4), (0, 8, 1, 4),
+    (0, 7, 0, 5), (1, 7, 0, 0), (3, 0, 0, 4), (1, 4, 0, 4), (4, 0, 0, 2), (0, 6, 1, 5), (1, 6, 1, 0), (0, 8, 1, 5), (1, 8, 1, 0),
+    (1, 4, 0, 5), (1, 7, 0, 1), (1, 5, 0, 4), (1, 7, 1, 1), (1, 5, 1, 3), (1, 6, 0, 1), (0, 8, 0, 5), (1, 8, 0, 0), (1, 5, 0, 5),
+    (3, 0, 0, 5), (1, 8, 1, 1), (1, 7, 0, 2), (1, 7, 1, 2), (4, 0, 0, 3), (1, 6, 1, 1), (1, 5, 1, 4), (1, 8, 0, 1), (1, 6, 0, 2),
+    (1, 8, 1, 2), (1, 5, 1, 5), (1, 7, 0, 3), (1, 8, 0, 2), (1, 7, 1, 3), (1, 8, 1, 3), (1, 6, 1, 2), (1, 6, 0, 3), (1, 7, 0, 4),
+    (1, 6, 1, 3), (1, 8, 0, 3), (1, 7, 1, 4), (1, 7, 0, 5), (1, 7, 1, 5), (1, 6, 0, 4), (1, 8, 1, 4), (1, 6, 0, 5), (1, 8, 0, 4),
+    (1, 8, 1, 5), (1, 6, 1, 4), (1, 8, 0, 5), (1, 6, 1, 5),
 )
 
 
@@ -271,7 +271,7 @@
             ticks |= {(1, j, o, m): max(t + 3 * nd, 20 + 2 * j) + 3 * m for m in range(gathers + 1)}
     ticks |= {(2, 0, 0, k): 2 * k for k in range(nd + 2 + tally_gathers)}
     late = sorted((t, key) for key, t in ticks.items() if t >= DRAIN)
-    return {key: t for key, t in ticks.items() if t < DRAIN}, (MID + 1,) * 4, [(3, 0, 0, k) for k in range(nd + 1)] + [key for _, key in late]
+    return {key: t for key, t in ticks.items() if t < DRAIN}, (MID + 1,) * 4, [(4, 0, 0, k) for k in range(4)] + [(3, 0, 0, k) for k in range(nd + 1)] + [key for _, key in late]
 
 
 def layer_kernel(shape, mol_h, cot_h, wup_h, wdn_h, wqkv_h, wout_h, ids_ref,
@@ -334,6 +334,8 @@
     for r in range(rows):
         for n in range(len(near)):
             mol(r, n).start()
+    for n in range(len(near)):
+        cot(n).start()
     fetch[1].start()
     cot_own.start()
     for copy in weights(0, 0):
@@ -376,13 +378,13 @@
         else:
             tally.gather_step(k - nd - 1, cland, cnt_out, (cag_send, cag_recv), ckeep_sem)
 
-    def tick(t, low, high):
+    def tick(t, met):
         for kind, most in ((0, nd), (1, gathers)):
             for k in reversed(range(most + 1)):
                 for o in range(2):
                     for named in sorted(set(way[o] for way in WAYS)):
                         found = [(ticks.get((kind, j, o, k), -1), j) for j in range(NPAIR) if WAYS[j][o] == named]
-                        found = [(at, j) for at, j in found if low <= at <= high]
+                        found = [(at, j) for at, j in found if at in met]
                         assert len({at for at, _ in found}) == len(found)
                         if not found:
                             continue
@@ -395,14 +397,14 @@
 
         for k in range(nd + 2 + len(tally.gathers)):
             at = ticks.get((2, 0, 0, k), -1)
-            if low <= at <= high:
+            if at in met:
 
                 @pl.when(t == at)
                 def _():
                     act_counts(k)
 
         for n, at in enumerate(back_at):
-            if low <= at <= high:
+            if at in met:
 
                 @pl.when(t == at)
                 def _():
@@ -486,9 +488,6 @@
         ends = (0, 4 // TOGETHER, NH // (2 * TOGETHER))
         for part in range(2):
             lax.fori_loop(ends[part], ends[part + 1], some, 0)
-            if r == 0 and part == 0:
-                for n in range(len(near)):
-                    cot(n).start()
             if 2 * r + part in early_counts:
                 act_counts(2 * r + part)
         lt = lacc[...].T
@@ -503,23 +502,28 @@
         at = pl.ds(pl.multiple_of(n * step, step), step)
         return at, (n * step // length, pl.ds(pl.multiple_of((n * step) % length, step), step))
 
-    cot_own.wait()
-    for n in range(len(near)):
-        cot(n).wait()
-
     def open_piece(n, carry):
-        at, row_at = piece(n)
+        at, _ = piece(n)
         mid = mid_s[at]
         xhat, _ = norm_parts(mid)
         a2 = (xhat * g2_ref[...] + b2_ref[...]).astype(BF)
         a2_s[at] = a2
         a2t_s[:, at] = a2.T
-        dyt_s[:, at] = dy_s[row_at].T
         acc_s[at] = mid + db_ref[...]
         da2_s[at] = jnp.zeros((step, D), F32)
         return carry
 
     lax.fori_loop(0, pieces, open_piece, 0)
+    cot_own.wait()
+    for n in range(len(near)):
+        cot(n).wait()
+
+    def turn_cotangent(n, carry):
+        at, row_at = piece(n)
+        dyt_s[:, at] = dy_s[row_at].T
+        return carry
+
+    lax.fori_loop(0, pieces, turn_cotangent, 0)
 
     def ff(i, carry):
         slot = i % 2
@@ -539,7 +543,7 @@
         hid = (u * cdf).astype(BF)
         du = (dh * (cdf + u * pdf)).astype(BF)
         gub_s[:, cols] = jnp.sum(du.astype(F32), 0, keepdims=True)
-        tick(SPLIT * i, 0, MID - 1)
+        tick(SPLIT * i, range(0, MID, SPLIT))
         acc_s[...] += dot_nn(hid, wdn_s[slot])
         da2_s[...] += dot_nt(du, wup_s[slot])
         gd = dot_nn(dyt_s[...], hid).astype(BF)
@@ -547,7 +551,7 @@
         for b in range(NB):
             stage_s[slot, 0, b] = gd[:, b * LANE : (b + 1) * LANE]
             stage_s[slot, 1, b] = gu[:, b * LANE : (b + 1) * LANE]
-        tick(SPLIT * i + SPLIT - 1, 0, MID - 1)
+        tick(SPLIT * i + SPLIT - 1, range(SPLIT - 1, MID, SPLIT))
         return carry
 
     lax.fori_loop(0, NFF, ff, 0)
@@ -576,7 +580,7 @@
     give_self(0, lo_out).start()
     for r in range(rows):
         give_back(0, lo_out, r, len(near) - 1).start()
-    tick(MID, MID, MID)
+    tick(MID, (MID,))
     gout_s = dyt_s
     gout_s[:, 0:D] = dot_tn(ctx_s[...], do_s[...]).astype(BF)
 
@@ -588,7 +592,7 @@
         return carry
 
     lax.fori_loop(0, pieces, first_norm, 0)
-    tick(MID + 1, MID + 1, MID + 1)
+    tick(MID + 1, (MID + 1,))
 
     def group(g, carry):
         def unit(r, h):
@@ -621,8 +625,9 @@
         def both_halves(n, inner_carry):
             unit(n, 0)
             unit(n, 1)
-            tick(MID + 2 + 5 * g + 2 * n, MID + 2, DRAIN - 1)
-            tick(MID + 3 + 5 * g + 2 * n, MID + 2, DRAIN - 1)
+            for late_tick in range(2):
+                first = MID + 2 + late_tick
+                tick(first + 5 * g + 2 * n, [first + 5 * a + 2 * b for a in range(3) for b in range(2)])
             return inner_carry
 
         lax.fori_loop(0, rows, both_halves, 0)
@@ -639,7 +644,7 @@
         here = pl.ds(pl.multiple_of(g * two, two), two)
         part_s[6:7, here] = jnp.sum(dqkv_s[:, 0:two].astype(F32), 0, keepdims=True)
         part_s[7:8, here] = jnp.sum(dqkv_s[:, 2 * two : 3 * two].astype(F32), 0, keepdims=True)
-        tick(MID + 6 + 5 * g, MID + 2, DRAIN - 1)
+        tick(MID + 6 + 5 * g, range(MID + 6, DRAIN, 5))
         return carry
 
     lax.fori_loop(0, 3, group, 0)
@@ -659,8 +664,7 @@
     lax.fori_loop(0, pieces, last_piece, 0)
     give_self(1, gm_out).start()
     for r in range(rows):
-        for n in range(len(near)):
-            give_back(1, gm_out, r, n).start()
+        give_back(1, gm_out, r, len(near) - 1).start()
     vacc_s[0, 0:8] = part_s[...]
     for b in range(FF // (2 * LANE)):
         vacc_s[0, 8 + b // 3 : 9 + b // 3, (b % 3) * 2 * LANE : (b % 3 + 1) * 2 * LANE] = gub_s[:, b * 2 * LANE : (b + 1) * 2 * LANE]
@@ -675,6 +679,8 @@
             act(kind, j, o, k, WAYS[j][o])
         elif kind == 2:
             act_counts(k)
+        elif kind == 4:
+            give_back(1, gm_out, *back[k]).start()
         else:
             if k > 0:
                 swap(k - 1).wait()

time: 220 us -> 210 us (0.955)
  Pallas kernels: 218 us -> 209 us
    pallas_call x1, Pallas kernels: 199 us -> 189 us  [layer(): pl.pallas_call(functools.partial(layer_kernel, shape), in_specs=[hb] * 6...]
where the time goes in v6:
time: 210 us
  Pallas kernels  209 us (100%)
    pallas_call x1, Pallas kernels, layer(): pl.pallas_call(functools.partial(layer_kernel, shape), in_specs=[hb] * 6...  189 us
    pallas_call x1, Pallas kernels, widen(): pl.pallas_call(widen_kernel, grid=(NPAIR,), in_specs=[pl.BlockSpec((1, 2,...  19.7 us

profile of v6, /device:TPU:0, one launch (start us, length us, event | category | flops | bytes accessed | tf_op | source)
XLA Modules:
  0.0 209.8 jit_solution(10413102214497843429)
XLA Ops:
  0.7 189.2 %layer.1 = (bf16[8,128,768]{2,1,0:T(8,128)(2,1)}, bf16[8,128,768]{2,1,0:T(8,128)(2,1)}, bf16[9,2,4,768,128]{4,3,2,1,0:T(8,128)(2,1)}, s32[128,8,128]{2,1,0:T(8,128)}, f32[16,768]{1,0:T(8,128)}) custom-call(bf16[8,128,768]{2,1,0:T(8,128)(2,1)} %mol_h.1, bf16[8,128,768]{2,1,0:T(8,128)(2,1)} %cot_h.1, bf16[768,3072]{1,0:T(8,128)(2,1)} %wup_h.1, ...), custom_call_target="tpu_custom_call" | custom-call | tf_op jit(solution)/shard_map/layer/pallas_call | solution.py:718
  189.9 19.7 %widen.1 = (f32[8,128,768]{2,1,0:T(8,128)}, bf16[8,128,768]{2,1,0:T(8,128)(2,1)}, s32[8,16384]{1,0:T(8,128)}, f32[768]{0:T(1024)}, f32[768]{0:T(1024)}, /*index=...) custom-call(bf16[9,2,4,768,128]{4,3,2,1,0:T(8,128)(2,1)} %get-tuple-, ...), custom_call_target="tpu_custom_call" | custom-call | tf_op jit(solution)/shard_map/widen/pallas_call | solution.py:807
